TPU v7x, 256 devices: a whole 4x4x8 slice. The times are simulated.
256 devices in a mesh: op: 64 (over y, z, core), wf: 4 (over x).
Axes of the slice: x: 4, y: 4, z: 8, core: 2. Of those that a mesh axis runs over, the one named last changes fastest.
Arguments:
- guess: float32 [16, 128, 128], P('wf'), may hold values from -6 to 6
- left_ops: bfloat16 [1024, 16, 128, 128], P('op', 'wf'), may hold values from -1 to 1
- right_ops: bfloat16 [1024, 16, 128, 128], P('op', 'wf'), may hold values from -1 to 1
- op_shift: int32 [1024], P('op'), may hold values from -2 to 2
- op_mask: int32 [1024, 16], P('op', 'wf'), may hold values 0 or 1
- left_dims: int32 [16], replicated, may hold values from 1 to 128, 1984 in all
- right_dims: int32 [16], replicated, may hold values from 1 to 128, 1984 in all
Outputs:
- ritz_vector: float32 [16, 128, 128], P('wf')
- energies: float32 [2], replicated
Inputs may be any that keep to these rules, and one draw needn't show every extreme that they name: `left_dims`: left sector dimensions sum to 1984 and the largest is exactly 128. `right_dims`: right sector dimensions sum to 1984 and the largest is exactly 128.
All inputs are finite; a program needn't handle non-finite values. No bound on the sum of `op_mask` on one device may be relied on, other than what follows from the above.
Results may differ from a plain program's by a relative error of at most 0.004.
Values may be sent and summed in bfloat16 or wider, within the bound.
No kernel may reach another device: no remote copies, remote signals or barrier semaphores. Data moves between devices by JAX's collectives and lax.ppermute only.
A program may use at most 64 MiB of HBM per device.

v0:
```python
import jax
import jax.numpy as jnp
from jax import lax
from jax.sharding import PartitionSpec as P

ITERS = 2


EPS = 1e-06
HIGH = lax.Precision.HIGHEST


def padded(block, sides, width):
    for axis, dim in sides:
        count = lax.axis_size(axis)
        forward = [(i, i + 1) for i in range(count - 1)]
        backward = [(target, source) for source, target in forward]
        low = lax.ppermute(
            lax.slice_in_dim(block, block.shape[dim] - width, None, axis=dim), axis, forward
        )
        high = lax.ppermute(lax.slice_in_dim(block, 0, width, axis=dim), axis, backward)
        block = jnp.concatenate([low, block, high], axis=dim)
    return block


def shards(guess, left_ops, right_ops, op_shift, op_mask, left_dims, right_dims):
    local_count = guess.shape[0]
    block_size = guess.shape[1]
    sectors = local_count * lax.axis_size("wf")
    first_sector = lax.axis_index("wf") * local_count
    own_sectors = first_sector + jnp.arange(local_count, dtype=jnp.int32)
    states = jnp.arange(block_size, dtype=jnp.int32)
    left_here = jnp.take(left_dims, own_sectors)
    right_here = jnp.take(right_dims, sectors - 1 - own_sectors)
    left_live = states[None, :] < left_here[:, None]
    right_live = states[None, :] < right_here[:, None]
    live_mask = (left_live[:, :, None] & right_live[:, None, :]).astype(jnp.float32)
    entries = float(guess.size * lax.axis_size("wf"))
    all_sectors = jnp.arange(sectors, dtype=jnp.int32)
    targets = own_sectors[None, :] + op_shift[:, None]
    fold_table = (targets[:, :, None] == all_sectors[None, None, :]).astype(jnp.float32)
    own_table = (own_sectors[:, None] == all_sectors[None, :]).astype(jnp.float32)
    source_index = jnp.arange(local_count, dtype=jnp.int32)[None, :] + 2 + op_shift[:, None]
    weight_live = op_mask.astype(jnp.float32)[:, :, None, None]

    def apply_hamiltonian(vector):
        vec_half = vector.astype(jnp.bfloat16)
        extended = padded(vec_half, (("wf", 0),), 2)
        source = jnp.take(extended, source_index, axis=0)
        middle = jnp.einsum(
            "ksab,sbc->ksac", left_ops, vec_half, preferred_element_type=jnp.float32
        ).astype(jnp.bfloat16)
        forward = (
            jnp.einsum("ksac,ksdc->ksad", middle, right_ops, preferred_element_type=jnp.float32)
            * weight_live
        )
        back_middle = jnp.einsum(
            "ksba,ksbc->ksac", left_ops, source, preferred_element_type=jnp.float32
        ).astype(jnp.bfloat16)
        adjoint = (
            jnp.einsum(
                "ksac,kscd->ksad", back_middle, right_ops, preferred_element_type=jnp.float32
            )
            * weight_live
        )
        adjoint_sum = jnp.sum(adjoint, axis=0)
        partial_value = jnp.einsum("kst,ksab->tab", fold_table, forward, precision=HIGH)
        partial_value = partial_value + jnp.einsum(
            "st,sab->tab", own_table, adjoint_sum, precision=HIGH
        )
        summed = lax.psum(partial_value, ("op", "wf"))
        own_blocks = lax.dynamic_slice_in_dim(summed, first_sector, local_count, 0)
        return own_blocks * live_mask

    def local_dot(first_vec, second_vec):
        return jnp.sum(first_vec * second_vec) / entries

    start_vec = guess * live_mask
    start_sum = lax.psum(local_dot(start_vec, start_vec), "wf")
    vector = start_vec / jnp.sqrt(start_sum + EPS)
    image = apply_hamiltonian(vector)
    lowest_list = []
    for turn_index in range(ITERS):
        ritz_value = lax.psum(local_dot(vector, image), "wf")
        residual = image - ritz_value * vector
        res_norm = lax.psum(local_dot(residual, residual), "wf")
        direction = residual / jnp.sqrt(res_norm + EPS)
        turned = apply_hamiltonian(direction)
        curvature = lax.psum(local_dot(direction, turned), "wf")
        lowest = 0.5 * (ritz_value + curvature) - jnp.sqrt(
            0.25 * (ritz_value - curvature) * (ritz_value - curvature) + res_norm
        )
        keep_old = curvature - lowest
        take_new = -jnp.sqrt(res_norm)
        scaler = jnp.sqrt(keep_old * keep_old + take_new * take_new)
        vector = (keep_old * vector + take_new * direction) / scaler
        image = (keep_old * image + take_new * turned) / scaler
        lowest_list.append(lowest)
    return (vector, jnp.stack(lowest_list))


def solution(mesh):
    in_specs = (
        P("wf", None, None),
        P("op", "wf", None, None),
        P("op", "wf", None, None),
        P("op"),
        P("op", "wf"),
        P(),
        P(),
    )
    out_specs = (P("wf", None, None), P())
    return jax.shard_map(shards, mesh=mesh, in_specs=in_specs, out_specs=out_specs, check_vma=False)
```

profile of v0, /device:TPU:1, one launch (start us, length us, event | category | flops | bytes accessed | tf_op | source)
XLA Modules:
  0.0 969.6 jit_solution(2783808681081322334)
XLA Ops:
  12.6 9.8 %psum.70 = f32[]{:T(128)} all-reduce(f32[]{:T(128)S(6)} %div.55), channel_id=1, replica_groups=mesh['op'=64,'wf'=4] {'wf'}, use_global_device_ids=true, to_apply=%region_1.3 | all-reduce | flops 1 | bytes 8 | tf_op jit(solution)/shard_map/psum | solution.py:79
  25.7 4.0 collective-permute-start
  34.2 5.5 fusion.36
  42.2 3.9 copy.57
  46.1 3.6 multiply_reduce_fusion.2
  49.8 3.0 convolution_add_fusion.2
  52.9 257.9 %all-reduce.4.cloned.1.call-done = f32[16,128,128]{2,0,1:T(8,128)} async-done(((f32[16,128,128]{2,0,1:T(8,128)}), f32[16,128,128]{2,0,1:T(8,128)}) %all-reduce.4.cloned.1.call-update) | async-done | bytes 1048592 | tf_op jit(solution)/shard_map/psum | solution.py:71
  313.4 8.8 psum.72
  325.4 6.7 psum.73
  340.0 4.0 collective-permute-start.2
  344.0 5.5 fusion.39
  352.0 3.9 copy.67
  355.9 3.6 multiply_reduce_fusion.1
  359.6 3.0 convolution_add_fusion.1
  363.4 257.5 %all-reduce.6.cloned.1.call-done = f32[16,128,128]{2,0,1:T(8,128)} async-done(((f32[16,128,128]{2,0,1:T(8,128)}), f32[16,128,128]{2,0,1:T(8,128)}) %all-reduce.6.cloned.1.call-update) | async-done | bytes 1048592 | tf_op jit(solution)/shard_map/psum | solution.py:71
  623.6 8.9 psum.75
  639.4 6.5 psum.76
  648.0 8.2 psum.77
  663.6 4.0 collective-permute-start.4
  667.6 4.5 fusion.42
  674.5 3.9 copy.77
  678.4 4.4 multiply_reduce_fusion
  686.2 258.9 %all-reduce.8.cloned.1.call-done = f32[16,128,128]{2,0,1:T(8,128)} async-done(((f32[16,128,128]{2,0,1:T(8,128)}), f32[16,128,128]{2,0,1:T(8,128)}) %all-reduce.8.cloned.1.call-update) | async-done | bytes 1048592 | tf_op jit(solution)/shard_map/psum | solution.py:71
  947.9 8.9 psum.79
  (75 shorter events, 50.2 us)
Async XLA Ops:
  7.2 25.4 %copy-start = (bf16[16,4,128,128]{3,2,1,0:T(8,128)(2,1)S(1)}, bf16[16,4,128,128]{3,2,1,0:T(8,128)(2,1)}, u32[]{:S(2)}) copy-start(bf16[16,4,128,128]{3,2,1,0:T(8,128)(2,1)} %param.13) | copy-start | bytes 6291460
  7.2 22.5 %copy-start.3 = (s32[16,4]{0,1:T(4,128)S(1)}, s32[16,4]{0,1:T(4,128)}, u32[]{:S(2)}) copy-start(s32[16,4]{0,1:T(4,128)} %param.15) | copy-start | bytes 772
  7.2 22.6 %copy-start.4 = (s32[16]{0:T(128)S(1)}, s32[16]{0:T(128)}, u32[]{:S(2)}) copy-start(s32[16]{0:T(128)} %param.14) | copy-start | bytes 196
  7.2 303.6 %all-reduce.4.cloned.1.call-start = ((), (), s32[]{:S(2)}) async-start(), calls=%async_computation | async-start | bytes 2097152 | tf_op jit(solution)/shard_map/psum | solution.py:71
  24.4 15.3 %collective-permute-start.1 = (bf16[2,128,128]{2,0,1:T(2,128)(2,1)S(1)}, bf16[2,128,128]{2,0,1:T(2,128)(2,1)S(1)}, u32[]{:S(2)}, u32[]{:S(2)}) collective-permute-start(bf16[2,128,128]{2,0,1:T(2,128)(2,1)S(1)} %get-tuple-element.26), channel_id=1, source_target_pairs={{1,0},{2,1},{3,2},{5,4},{6,5},{7,6},{9,8},{10,9},{11,10},{13,12},{... | collective-permute-start | bytes 196616 | tf_op jit(solution)/shard_map/ppermute | solution.py:21
  25.7 14.0 %collective-permute-start = (bf16[2,128,128]{2,0,1:T(2,128)(2,1)S(1)}, bf16[2,128,128]{2,0,1:T(2,128)(2,1)S(1)}, u32[]{:S(2)}, u32[]{:S(2)}) collective-permute-start(bf16[2,128,128]{2,0,1:T(2,128)(2,1)S(1)} %get-tuple-element.25), channel_id=1, source_target_pairs={{0,1},{1,2},{2,3},{4,5},{5,6},{6,7},{8,9},{9,10},{10,11},{12,13},{... | collective-permute-start | bytes 196616 | tf_op jit(solution)/shard_map/ppermute | solution.py:18
  52.9 568.1 %all-reduce.6.cloned.1.call-start = ((), (), s32[]{:S(2)}) async-start(), calls=%async_computation.1 | async-start | bytes 2097152 | tf_op jit(solution)/shard_map/psum | solution.py:71
  338.7 10.8 %collective-permute-start.3 = (bf16[2,128,128]{2,0,1:T(2,128)(2,1)S(1)}, bf16[2,128,128]{2,0,1:T(2,128)(2,1)S(1)}, u32[]{:S(2)}, u32[]{:S(2)}) collective-permute-start(bf16[2,128,128]{2,0,1:T(2,128)(2,1)S(1)} %get-tuple-element.24), channel_id=1, source_target_pairs={{1,0},{2,1},{3,2},{5,4},{6,5},{7,6},{9,8},{10,9},{11,10},{13,12},{... | collective-permute-start | bytes 196616 | tf_op jit(solution)/shard_map/ppermute | solution.py:21
  340.0 9.5 collective-permute-start.2
  362.6 582.5 %all-reduce.8.cloned.1.call-start = ((), (), s32[]{:S(2)}) async-start(), calls=%async_computation.2 | async-start | bytes 2097152 | tf_op jit(solution)/shard_map/psum | solution.py:71
  638.8 21.9 %copy-start.1 = (f32[4,128,128]{2,0,1:T(4,128)}, f32[4,128,128]{2,0,1:T(4,128)S(1)}, u32[]{:S(2)}) copy-start(f32[4,128,128]{2,0,1:T(4,128)S(1)} %get-tuple-element.15) | copy-start | bytes 786436
  662.3 9.8 %collective-permute-start.5 = (bf16[2,128,128]{2,0,1:T(2,128)(2,1)S(1)}, bf16[2,128,128]{2,0,1:T(2,128)(2,1)S(1)}, u32[]{:S(2)}, u32[]{:S(2)}) collective-permute-start(bf16[2,128,128]{2,0,1:T(2,128)(2,1)S(1)} %get-tuple-element.22), channel_id=1, source_target_pairs={{1,0},{2,1},{3,2},{5,4},{6,5},{7,6},{9,8},{10,9},{11,10},{13,12},{... | collective-permute-start | bytes 196616 | tf_op jit(solution)/shard_map/ppermute | solution.py:21
  663.6 8.5 collective-permute-start.4
  682.8 278.0 %copy-start.2 = (f32[4,128,128]{2,0,1:T(4,128)S(1)}, f32[4,128,128]{2,0,1:T(4,128)}, u32[]{:S(2)}) copy-start(f32[4,128,128]{2,0,1:T(4,128)} %copy-done.1) | copy-start | bytes 786436
Sparse Core Ops, SparseCore 0:
  53.0 257.8 all-reduce.3
  362.8 258.1 all-reduce.5
  685.7 259.3 all-reduce.7
where the time goes:
time: 973 us; the launch traced here: 970 us
  waiting for transfers between devices  774 us (80%)
  blocking collectives  57.9 us (6%)
  matrix products  47.9 us (5%)
  between operations  30.2 us (3%)
  local copies, waits for them, and re-layouts  22.4 us (2%)
  other arithmetic  20.8 us (2%)
  starting transfers between devices  16 us (2%)
    psum x3, waiting for transfers between devices, apply_hamiltonian(): summed = lax.psum(partial_value, ('op', 'wf'))  774 us
  transfers between devices with their start and end apart: 9, of which 3 were waited for; matrix products, arithmetic and copies ran while one was open for 2% of the time, Pallas kernels for 0%

commit v1 on v0

v1 whole, which is shorter than its diff:
```python
import jax
import jax.numpy as jnp
from jax import lax
from jax.experimental import pallas as pl
from jax.experimental.pallas import tpu as pltpu
from jax.sharding import Mesh, PartitionSpec as P

EPS = 1e-06
SECTORS = 16
BLOCK = 128
PAIRS = 16
OWN = 4
WINDOW = 8
PLANE = 32
CHUNK = 32
EXTRA = 8
ENTRIES = float(SECTORS * BLOCK * BLOCK)
PLANE_AXES = ("y", "z")
CROSS_AXES = ("c", "wf")
OP_AXES = ("y", "z", "c")

f32 = jnp.float32
bf16 = jnp.bfloat16


def dot(first, second, first_dim=1, second_dim=0):
    return lax.dot_general(
        first, second, (((first_dim,), (second_dim,)), ((), ())), preferred_element_type=f32
    )


def total(values):
    return jnp.sum(values, axis=(0, 1), keepdims=True)


def ratio(top, bottom):
    return jnp.where(bottom > 0, top / jnp.where(bottom > 0, bottom, 1.0), 0.0)


def sector_at(wf, position):
    base = OWN * wf - 2
    return base + ((position - base) & 7)


def live(left_dims, right_dims, sector, first_row, rows):
    held = jnp.clip(sector, 0, SECTORS - 1)
    inside = (sector >= 0) & (sector < SECTORS)
    height = jnp.where(inside, left_dims[held], 0)
    width = right_dims[SECTORS - 1 - held]
    row = lax.broadcasted_iota(jnp.int32, (rows, BLOCK), 0) + first_row
    column = lax.broadcasted_iota(jnp.int32, (rows, BLOCK), 1)
    return (row < height) & (column < width)


def pack(values):
    lane = lax.broadcasted_iota(jnp.int32, (EXTRA, BLOCK), 1)
    packed = jnp.zeros((EXTRA, BLOCK), f32)
    for place, value in enumerate(values):
        packed = jnp.where(lane == place, value, packed)
    return packed


def lanes(rows, count):
    return [rows[:, place : place + 1] for place in range(count)]


def norm_kernel(ids, left_dims, right_dims, guess, out):
    wf, chunk = ids[0], ids[1]
    sums = jnp.zeros((1, 1), f32)
    for i in range(OWN):
        mask = live(left_dims, right_dims, OWN * wf + i, 0, BLOCK)
        block = jnp.where(mask, guess[i], 0.0)
        sums = sums + total(block * block)
    out[0:EXTRA] = jnp.broadcast_to(sums, (EXTRA, BLOCK))
    block, first_row = (chunk // 4) & 3, pl.multiple_of((chunk & 3) * CHUNK, CHUNK)
    mask = live(left_dims, right_dims, OWN * wf + block, first_row, CHUNK)
    out[EXTRA:] = jnp.where(mask, guess[block, pl.ds(first_row, CHUNK)], 0.0)


def half_step(ids, shift, mask, left, right, vec_half, back, sector, index):
    for k in range(PAIRS):
        position = (sector + shift[k]) & 7
        weight = mask[k * OWN + index].astype(f32)
        value = dot(left[k, 0].T, vec_half[position])
        back[:, k * BLOCK : (k + 1) * BLOCK] = (value * weight).astype(bf16)
    return dot(back[...], right[:, 0].reshape(PAIRS * BLOCK, BLOCK))


def full_step(ids, shift, mask, left, right, vec_half, back, out):
    index = pl.program_id(0)
    sector = OWN * ids[0] + index
    middle = dot(left[:, 0].reshape(PAIRS * BLOCK, BLOCK), vec_half[sector & 7])
    for k in range(PAIRS):
        position = (sector + shift[k]) & 7
        weight = mask[k * OWN + index].astype(f32)
        term = (middle[k * BLOCK : (k + 1) * BLOCK] * weight).astype(bf16)
        out[position] += dot(term, right[k, 0], 1, 1)
    out[sector & 7] += half_step(ids, shift, mask, left, right, vec_half, back, sector, index)


def first_kernel(
    ids, left_dims, right_dims, shift, mask, guess, side_one, side_three, own, one, two, three,
    left, right, out, vector, pieces, vec_half, back,
):
    wf, chunk = ids[0], ids[1]

    @pl.when(pl.program_id(0) == 0)
    def _():
        sums = (own[0:1, 0:1] + one[0:1, 0:1]) + (two[0:1, 0:1] + three[0:1, 0:1])
        scale = 1.0 / jnp.sqrt(sums / ENTRIES + EPS)

        def put(position, block):
            alive = live(left_dims, right_dims, sector_at(wf, position), 0, BLOCK)
            value = jnp.where(alive, block, 0.0) * scale
            vector[position] = value
            vec_half[position] = value.astype(bf16)

        odd = wf & 1
        for i in range(OWN):
            put(4 * odd + i, guess[i])
        for i in range(2):
            put(4 - 2 * odd + i, side_one[i])
            put(6 - 6 * odd + i, side_three[i])
        held = [own[EXTRA:], one[EXTRA:], two[EXTRA:], three[EXTRA:]]
        for place in range(2):
            source = (chunk // 16 + 2 * place) ^ wf
            value = held[0]
            for other in range(1, 4):
                value = jnp.where(source == other, held[other], value)
            pieces[place] = value * scale
        out[...] = jnp.zeros_like(out)

    full_step(ids, shift, mask, left, right, vec_half, back, out)


def spread_kernel(parts, out):
    summed = jnp.sum(parts[...], axis=0)
    for target in range(out.shape[0]):
        out[target] = summed


def combined(ids, left_dims, right_dims, parts):
    chunk = ids[1]
    position, first_row = chunk // 4, (chunk & 3) * CHUNK
    values = []
    for place in range(2):
        sector = position + 8 * place
        value = jnp.zeros((CHUNK, BLOCK), f32)
        for wf in range(4):
            here = sector_at(wf, position) == sector
            value = value + jnp.where(here, parts[wf] + parts[4 + wf], 0.0)
        values.append(jnp.where(live(left_dims, right_dims, sector, first_row, CHUNK), value, 0.0))
    return values


def send(ids, values, sums, out):
    position = ids[1] // 4
    sector = sector_at(ids[0], position)
    chosen = jnp.where(sector == position, values[0], 0.0)
    chosen = jnp.where(sector == position + 8, values[1], chosen)
    packed = pack(sums)
    for target in range(PLANE):
        out[target, 0:CHUNK] = chosen
        out[target, CHUNK:] = packed


def image_kernel(ids, left_dims, right_dims, parts, pieces, out, image_pieces):
    image = combined(ids, left_dims, right_dims, parts)
    vec = [pieces[0], pieces[1]]

    def inner(first, second):
        return total(first[0] * second[0] + first[1] * second[1])

    vec_vec, vec_image = inner(vec, vec), inner(vec, image)
    part = ratio(vec_image, vec_vec)
    rest = [image[i] - part * vec[i] for i in range(2)]
    for i in range(2):
        image_pieces[i] = image[i]
    send(ids, image, [vec_image, vec_vec, part, inner(rest, rest)], out)


def second_kernel(
    ids, shift, mask, gathered, vector, left, right, out, direction, image, scalars, vec_half, back
):
    @pl.when(pl.program_id(0) == 0)
    def _():
        vec_image, vec_vec, part, rest = lanes(gathered[:, CHUNK, :], 4)
        ritz = total(vec_image) / ENTRIES
        apart = ritz - part
        norm = total(rest + apart * apart * vec_vec) / ENTRIES
        scale = 1.0 / jnp.sqrt(norm + EPS)
        scalars[...] = pack([ritz, norm])
        for position in range(WINDOW):
            held = gathered[4 * position : 4 * position + 4, 0:CHUNK, :].reshape(BLOCK, BLOCK)
            value = (held - ritz * vector[position]) * scale
            image[position] = held
            direction[position] = value
            vec_half[position] = value.astype(bf16)
        out[...] = jnp.zeros_like(out)

    full_step(ids, shift, mask, left, right, vec_half, back, out)


def turned_kernel(ids, left_dims, right_dims, parts, pieces, image_pieces, scalars, out):
    turned = combined(ids, left_dims, right_dims, parts)
    ritz, norm = scalars[0:1, 0:1], scalars[0:1, 1:2]
    scale = 1.0 / jnp.sqrt(norm + EPS)
    vec = [pieces[i] for i in range(2)]
    image = [image_pieces[i] for i in range(2)]
    turn = [(image[i] - ritz * vec[i]) * scale for i in range(2)]

    def inner(first, second):
        return total(first[0] * second[0] + first[1] * second[1])

    vec_vec, vec_turned = inner(vec, vec), inner(vec, turned)
    along = ratio(inner(vec, turn), vec_vec)
    new = [turn[i] - along * vec[i] for i in range(2)]
    on_vec = ratio(vec_turned, vec_vec)
    rest = [turned[i] - on_vec * vec[i] for i in range(2)]
    new_new = inner(new, new)
    on_new = ratio(inner(new, rest), new_new)
    rest = [rest[i] - on_new * new[i] for i in range(2)]
    sums = [
        vec_turned, inner(turn, image), inner(turn, turned),
        vec_vec, along, on_vec, new_new, on_new, inner(rest, rest),
    ]
    send(ids, turned, sums, out)


def mixing(ritz, curvature, norm):
    gap = ritz - curvature
    lowest = 0.5 * (ritz + curvature) - jnp.sqrt(0.25 * gap * gap + norm)
    keep = curvature - lowest
    take = -jnp.sqrt(norm)
    scale = jnp.sqrt(keep * keep + take * take)
    return lowest, keep / scale, take / scale


def third_kernel(
    ids, shift, mask, gathered, vector, direction, image, scalars, left, right,
    out, new_vector, new_direction, new_scalars, vec_half, own, back, sums,
):
    index = pl.program_id(0)
    wf = ids[0]

    @pl.when(index == 0)
    def _():
        (
            vec_turned, turn_image, turn_turned, vec_vec, along, on_vec, new_new, on_new, rest,
        ) = lanes(gathered[:, CHUNK, :], 9)
        ritz, norm = scalars[0:1, 0:1], scalars[0:1, 1:2]
        curvature = total(turn_turned) / ENTRIES
        lowest, keep, take = mixing(ritz, curvature, norm)
        mixed = (total(vec_turned) + total(turn_image)) / ENTRIES
        next_ritz = keep * keep * ritz + keep * take * mixed + take * take * curvature
        first = keep * (ritz - next_ritz)
        second = keep * jnp.sqrt(norm + EPS) - take * next_ritz
        on_first = first + second * along + take * on_vec
        on_second = second + take * on_new
        squares = on_first * on_first * vec_vec + on_second * on_second * new_new
        next_norm = total(squares + take * take * rest) / ENTRIES
        scale = 1.0 / jnp.sqrt(next_norm + EPS)
        new_scalars[...] = pack([next_ritz, next_norm, lowest])
        for position in range(WINDOW):
            turned = gathered[4 * position : 4 * position + 4, 0:CHUNK, :].reshape(BLOCK, BLOCK)
            mixed_vec = keep * vector[position] + take * direction[position]
            mixed_image = keep * image[position] + take * turned
            value = (mixed_image - next_ritz * mixed_vec) * scale
            vec_half[position] = value.astype(bf16)
            own[position] = value
            new_vector_here = mixed_vec

            @pl.when((position // 4) == (wf & 1))
            def _():
                new_vector[position % 4] = new_vector_here
                new_direction[position % 4] = value

        sums[...] = jnp.zeros_like(sums)

    sector = OWN * wf + index
    image_half = half_step(ids, shift, mask, left, right, vec_half, back, sector, index)
    sums[...] += image_half * own[sector & 7]

    @pl.when(index == OWN - 1)
    def _():
        value = jnp.broadcast_to(2.0 * total(sums[...]), (EXTRA, BLOCK))
        for target in range(out.shape[0]):
            out[target] = value


def last_kernel(parts, vector, direction, scalars, out, energies):
    curvature = total(jnp.sum(parts[...], axis=0)[0:1, 0:1]) / ENTRIES
    ritz, norm, first_lowest = lanes(scalars[0:1], 3)
    lowest, keep, take = mixing(ritz, curvature, norm)
    for i in range(OWN):
        out[i] = keep * vector[i] + take * direction[i]
    energies[...] = pack([first_lowest, lowest])


SCALAR = pl.BlockSpec(memory_space=pltpu.SMEM)


def whole(*shape):
    return pl.BlockSpec(shape, lambda *_: (0,) * len(shape))


def struct(*shape):
    return jax.ShapeDtypeStruct(shape, f32)


def small(kernel, name, outs, scalars, *arrays):
    return pl.pallas_call(
        kernel,
        name=name,
        in_specs=[SCALAR] * len(scalars) + [pl.BlockSpec(memory_space=pltpu.VMEM)] * len(arrays),
        out_specs=[pl.BlockSpec(memory_space=pltpu.VMEM)] * len(outs),
        out_shape=outs,
    )(*scalars, *arrays)


def step(kernel, name, outs, scratch, scalars, arrays, operators):
    operator_spec = pl.BlockSpec((PAIRS, 1, BLOCK, BLOCK), lambda i: (0, i, 0, 0))
    return pl.pallas_call(
        kernel,
        name=name,
        grid=(OWN,),
        in_specs=[SCALAR] * len(scalars)
        + [whole(*array.shape) for array in arrays]
        + [operator_spec] * 2,
        out_specs=[whole(*out.shape) for out in outs],
        out_shape=outs,
        scratch_shapes=[pltpu.VMEM((WINDOW, BLOCK, BLOCK), bf16)]
        + scratch[:1]
        + [pltpu.VMEM((BLOCK, PAIRS * BLOCK), bf16)]
        + scratch[1:],
        compiler_params=pltpu.CompilerParams(
            dimension_semantics=("arbitrary",), vmem_limit_bytes=32 << 20
        ),
    )(*scalars, *arrays, *operators)


def exchange(value, axes):
    return lax.all_to_all(value, axes, 0, 0, tiled=True)


def shards(guess, left_ops, right_ops, op_shift, op_mask, left_dims, right_dims):
    wf = lax.axis_index("wf")
    chunk = lax.axis_index("y") * lax.axis_size("z") + lax.axis_index("z")
    ids = jnp.stack([wf, chunk]).astype(jnp.int32)
    mask = op_mask.reshape(-1)
    operators = (left_ops, right_ops)
    dims = (left_dims, right_dims)
    blocks = struct(WINDOW, BLOCK, BLOCK)

    def partner(distance):
        return [(i, i ^ distance) for i in range(4)]

    odd = wf & 1
    side_one = lax.dynamic_slice_in_dim(guess, 2 - 2 * odd, 2, 0)
    side_three = lax.dynamic_slice_in_dim(guess, 2 * odd, 2, 0)
    side_one = lax.ppermute(side_one, "wf", partner(1))
    side_three = lax.ppermute(side_three, "wf", partner(3))
    (own,) = small(norm_kernel, "norm", [struct(EXTRA + CHUNK, BLOCK)], (ids, *dims), guess)
    others = [lax.ppermute(own, "wf", partner(distance)) for distance in (1, 2, 3)]

    def reduced(partial):
        parts = exchange(partial.reshape(PLANE, CHUNK, BLOCK), PLANE_AXES)
        (tiled,) = small(spread_kernel, "spread", [struct(8, CHUNK, BLOCK)], (), parts)
        return exchange(tiled, CROSS_AXES)

    partial, vector, pieces = step(
        first_kernel, "first", [blocks, blocks, struct(2, CHUNK, BLOCK)], [],
        (ids, *dims, op_shift, mask),
        (guess, side_one, side_three, own, *others), operators,
    )
    packet = struct(PLANE, CHUNK + EXTRA, BLOCK)
    packets, image_pieces = small(
        image_kernel, "image", [packet, struct(2, CHUNK, BLOCK)], (ids, *dims),
        reduced(partial), pieces,
    )
    gathered = exchange(packets, PLANE_AXES)
    partial, direction, image, scalars = step(
        second_kernel, "second", [blocks, blocks, blocks, struct(EXTRA, BLOCK)], [],
        (ids, op_shift, mask), (gathered, vector), operators,
    )
    (packets,) = small(
        turned_kernel, "turned", [packet], (ids, *dims),
        reduced(partial), pieces, image_pieces, scalars,
    )
    gathered = exchange(packets, PLANE_AXES)
    own_blocks = struct(OWN, BLOCK, BLOCK)
    sums, vector, direction, scalars = step(
        third_kernel, "third",
        [struct(8, EXTRA, BLOCK), own_blocks, own_blocks, struct(EXTRA, BLOCK)],
        [pltpu.VMEM((WINDOW, BLOCK, BLOCK), f32), pltpu.VMEM((BLOCK, BLOCK), f32)],
        (ids, op_shift, mask), (gathered, vector, direction, image, scalars), operators,
    )
    sums = exchange(sums, CROSS_AXES)
    (sums,) = small(spread_kernel, "sums", [struct(PLANE, EXTRA, BLOCK)], (), sums)
    sums = exchange(sums, PLANE_AXES)
    result, energies = small(
        last_kernel, "last", [own_blocks, struct(EXTRA, BLOCK)], (),
        sums, vector, direction, scalars,
    )
    return result, energies[0, 0:2]


def solution(mesh):
    split = Mesh(mesh.devices.reshape(4, 8, 2, 4), (*OP_AXES, "wf"))
    in_specs = (
        P("wf", None, None),
        P(OP_AXES, "wf", None, None),
        P(OP_AXES, "wf", None, None),
        P(OP_AXES),
        P(OP_AXES, "wf"),
        P(),
        P(),
    )
    out_specs = (P("wf", None, None), P())
    return jax.shard_map(
        shards, mesh=split, in_specs=in_specs, out_specs=out_specs, check_vma=False
    )
```

time: 973 us -> 202 us (0.21)
  waiting for transfers between devices: 774 us -> 1.99 us
  blocking collectives: 57.9 us -> 144 us
  matrix products: 47.9 us -> 0 us
  between operations: 30.2 us -> 0.74 us
  Pallas kernels: 0 us -> 28.4 us
  other arithmetic: 20.8 us -> 0.59 us
    psum x3 -> x0, waiting for transfers between devices: 774 us -> none  [apply_hamiltonian(): summed = lax.psum(partial_value, ('op', 'wf'))]
    all_to_all x0 -> x8, blocking collectives: none -> 144 us  [exchange(): return lax.all_to_all(value, axes, 0, 0, tiled=True)]
    psum x7 -> x0, blocking collectives: 57.9 us -> none  [the longest x2 17.8 us: shards(): curvature = lax.psum(local_dot(direction, turned), 'wf')]
    dot_general x15 -> x0, matrix products: 47.9 us -> none  [the longest x3 15.5 us: apply_hamiltonian(): jnp.einsum('kst,ksab->tab', fold_table, forward, precision=HIGH)]
    pallas_call x0 -> x10, Pallas kernels: none -> 28.4 us  [the longest x3 15.3 us: step(): pl.pallas_call(kernel, name=name, grid=(OWN,), in_specs=[SCALAR] * len(sc...]
    gather x8 -> x0, local copies, waits for them, and re-layouts: 20.9 us -> none  [the longest x6 18.2 us: apply_hamiltonian(): source = jnp.take(extended, source_index, axis=0)]
    unnamed x11 -> x45, local copies, waits for them, and re-layouts: 0.75 us -> 15.8 us
    reduce_sum x7 -> x0, other arithmetic: 13.7 us -> none  [local_dot(): return jnp.sum(first_vec * second_vec) / entries]
  transfers between devices with their start and end apart: 9 -> 5, of which waited for: 3 -> 2; matrix products, arithmetic and copies ran while one was open for 2% -> 1% of each run, Pallas kernels for 0% -> 1%
where the time goes in v1:
time: 202 us; the launch traced here: 201 us
  blocking collectives  144 us (71%)
  Pallas kernels  28.4 us (14%)
  local copies, waits for them, and re-layouts  18.1 us (9%)
  starting transfers between devices  6.65 us (3%)
    all_to_all x8, blocking collectives, exchange(): return lax.all_to_all(value, axes, 0, 0, tiled=True)  144 us
    unnamed x45, local copies, waits for them, and re-layouts  15.8 us
    pallas_call x3, Pallas kernels, step(): pl.pallas_call(kernel, name=name, grid=(OWN,), in_specs=[SCALAR] * len(sc...  15.3 us
    pallas_call x7, Pallas kernels, small(): pl.pallas_call(kernel, name=name, in_specs=[SCALAR] * len(scalars) + [pl....  13.1 us
  transfers between devices with their start and end apart: 5, of which 2 were waited for; matrix products, arithmetic and copies ran while one was open for 1% of the time, Pallas kernels for 1%

profile of v1, /device:TPU:1, one launch (start us, length us, event | category | flops | bytes accessed | tf_op | source)
XLA Modules:
  0.0 200.7 jit_solution(5410174123657223279)
XLA Ops:
  1.6 3.4 %collective-permute-start.1 = (f32[2,128,128]{2,1,0:T(8,128)S(1)}, f32[2,128,128]{2,1,0:T(8,128)S(1)}, u32[]{:S(2)}, u32[]{:S(2)}) collective-permute-start(f32[2,128,128]{2,1,0:T(8,128)S(1)} %get-tuple-element.32), channel_id=1, source_target_pairs={{0,3},{1,2},{2,1},{3,0},{4,7},{5,6},{6,5},{7,4},{8,11},{9,10},{10,... | collective-permute-start | bytes 393224 | tf_op jit(solution)/shard_map/ppermute | solution.py:362
  5.6 1.7 norm.1.own
  8.2 2.5 %collective-permute-start.3 = (f32[40,128]{1,0:T(8,128)}, f32[40,128]{1,0:T(8,128)S(1)}, u32[]{:S(2)}, u32[]{:S(2)}) collective-permute-start(f32[40,128]{1,0:T(8,128)} %norm.1.own), channel_id=1, source_target_pairs={{0,2},{1,3},{2,0},{3,1},{4,6},{5,7},{6,4},{7,5},{8,10},{9,11},{10,... | collective-permute-start | bytes 61448 | tf_op jit(solution)/shard_map/ppermute | solution.py:364
  13.5 1.6 copy-done
  15.1 1.6 copy-done.2
  20.9 5.6 %first.1 = (f32[8,128,128]{2,1,0:T(8,128)S(1)}, f32[8,128,128]{2,1,0:T(8,128)S(1)}, f32[2,32,128]{2,1,0:T(8,128)S(1)}) custom-call(s32[2]{0:T(128)S(1)} %copy-done.12, s32[16]{0:T(128)S(1)} %copy-done.17, s32[16]{0:T(128)S(1)} %copy-done.18, s32[16]{0:T(128)S(1)} %copy-done.19, s32[64]{0:T(128)S(1)} %reshape.13.mask, f32[4,128,128]{2,1,0:T(8,128)S(1)} %copy-done.5, ...), custom_call_target="tpu_custom_call" | custom-call | tf_op jit(solution)/shard_map/first/pallas_call | solution.py:323
  27.1 23.7 %all_to_all.40.parts = f32[32,32,128]{2,1,0:T(8,128)} all-to-all(f32[32,32,128]{2,1,0:T(8,128)S(1)} %bitcast.6), channel_id=1, replica_groups=mesh['y'=4,'z'=8,'c'=2,'wf'=4] {'y','z'}, dimensions={0} | all-to-all | bytes 1048576 | tf_op jit(solution)/shard_map/all_to_all | solution.py:343
  50.8 1.7 spread.2
  52.6 14.5 %all_to_all.41.parts = f32[8,32,128]{2,1,0:T(8,128)} all-to-all(f32[8,32,128]{2,1,0:T(8,128)} %spread.2), channel_id=1, replica_groups=mesh['y'=4,'z'=8,'c'=2,'wf'=4] {'c','wf'}, dimensions={0} | all-to-all | bytes 262144 | tf_op jit(solution)/shard_map/all_to_all | solution.py:343
  67.1 2.1 %image.1 = (f32[32,40,128]{2,1,0:T(8,128)}, f32[2,32,128]{2,1,0:T(8,128)}) custom-call(s32[2]{0:T(128)} %pad_add_fusion.ids, s32[16]{0:T(128)} %left_dims.7, s32[16]{0:T(128)} %right_dims.7, f32[8,32,128]{2,1,0:T(8,128)} %all_to_all.41.parts, f32[2,32,128]{2,1,0:T(8,128)} %copy-done.10), custom_call_target="tpu_custom_call" | custom-call | tf_op jit(solution)/shard_map/image/pallas_call | solution.py:312
  69.2 22.4 %all_to_all.42.gathered = f32[32,40,128]{2,1,0:T(8,128)S(1)} all-to-all(f32[32,40,128]{2,1,0:T(8,128)} %get-tuple-element.19), channel_id=1, replica_groups=mesh['y'=4,'z'=8,'c'=2,'wf'=4] {'y','z'}, dimensions={0} | all-to-all | bytes 1310720 | tf_op jit(solution)/shard_map/all_to_all | solution.py:343
  91.6 1.6 copy-done.3
  93.2 5.8 %second.1 = (f32[8,128,128]{2,1,0:T(8,128)S(1)}, f32[8,128,128]{2,1,0:T(8,128)S(1)}, f32[8,128,128]{2,1,0:T(8,128)S(1)}, f32[8,128]{1,0:T(8,128)S(1)}) custom-call(s32[2]{0:T(128)S(1)} %copy-done.13, s32[16]{0:T(128)S(1)} %copy-done.20, s32[64]{0:T(128)S(1)} %reshape.13.mask, f32[32,40,128]{2,1,0:T(8,128)S(1)} %all_to_all.42.gathered, ...), custom_call_target="tpu_custom_call" | custom-call | tf_op jit(solution)/shard_map/second/pallas_call | solution.py:323
  100.4 22.2 %all_to_all.43.parts = f32[32,32,128]{2,1,0:T(8,128)} all-to-all(f32[32,32,128]{2,1,0:T(8,128)S(1)} %bitcast.7), channel_id=1, replica_groups=mesh['y'=4,'z'=8,'c'=2,'wf'=4] {'y','z'}, dimensions={0} | all-to-all | bytes 1048576 | tf_op jit(solution)/shard_map/all_to_all | solution.py:343
  122.6 1.7 spread.3
  124.4 13.3 %all_to_all.44.parts = f32[8,32,128]{2,1,0:T(8,128)} all-to-all(f32[8,32,128]{2,1,0:T(8,128)} %spread.3), channel_id=1, replica_groups=mesh['y'=4,'z'=8,'c'=2,'wf'=4] {'c','wf'}, dimensions={0} | all-to-all | bytes 262144 | tf_op jit(solution)/shard_map/all_to_all | solution.py:343
  137.7 2.3 %turned.1 = f32[32,40,128]{2,1,0:T(8,128)} custom-call(s32[2]{0:T(128)} %pad_add_fusion.ids, s32[16]{0:T(128)} %left_dims.7, s32[16]{0:T(128)} %right_dims.7, f32[8,32,128]{2,1,0:T(8,128)} %all_to_all.44.parts, f32[2,32,128]{2,1,0:T(8,128)} %copy-done.10, f32[2,32,128]{2,1,0:T(8,128)} %get-tuple-element.22.image_pieces, f32[8,128]{1,0:T(8,128)} %copy-done.15), custom_call_target="tpu_custom_call" | custom-call | tf_op jit(solution)/shard_map/turned/pallas_call | solution.py:312
  139.9 21.8 %all_to_all.45.gathered = f32[32,40,128]{2,1,0:T(8,128)S(1)} all-to-all(f32[32,40,128]{2,1,0:T(8,128)} %turned.1), channel_id=1, replica_groups=mesh['y'=4,'z'=8,'c'=2,'wf'=4] {'y','z'}, dimensions={0} | all-to-all | bytes 1310720 | tf_op jit(solution)/shard_map/all_to_all | solution.py:343
  161.7 1.6 copy-done.4
  164.4 3.9 %third.1 = (f32[8,8,128]{2,1,0:T(8,128)S(1)}, f32[4,128,128]{2,1,0:T(8,128)S(1)}, f32[4,128,128]{2,1,0:T(8,128)S(1)}, f32[8,128]{1,0:T(8,128)S(1)}) custom-call(s32[2]{0:T(128)S(1)} %copy-done.14, s32[16]{0:T(128)S(1)} %copy-done.20, s32[64]{0:T(128)S(1)} %reshape.13.mask, f32[32,40,128]{2,1,0:T(8,128)S(1)} %all_to_all.45.gathered, ...), custom_call_target="tpu_custom_call" | custom-call | tf_op jit(solution)/shard_map/third/pallas_call | solution.py:323
  169.7 12.1 %all_to_all.46.parts = f32[8,8,128]{2,1,0:T(8,128)} all-to-all(f32[8,8,128]{2,1,0:T(8,128)S(1)} %get-tuple-element.26), channel_id=1, replica_groups=mesh['y'=4,'z'=8,'c'=2,'wf'=4] {'c','wf'}, dimensions={0} | all-to-all | bytes 65536 | tf_op jit(solution)/shard_map/all_to_all | solution.py:343
  181.8 1.4 sums.1
  183.2 14.2 %all_to_all.47.parts = f32[32,8,128]{2,1,0:T(8,128)} all-to-all(f32[32,8,128]{2,1,0:T(8,128)} %sums.1), channel_id=1, replica_groups=mesh['y'=4,'z'=8,'c'=2,'wf'=4] {'y','z'}, dimensions={0} | all-to-all | bytes 262144 | tf_op jit(solution)/shard_map/all_to_all | solution.py:343
  197.4 2.1 %last.1 = (f32[4,128,128]{2,1,0:T(8,128)}, f32[8,128]{1,0:T(8,128)}) custom-call(f32[32,8,128]{2,1,0:T(8,128)} %all_to_all.47.parts, f32[4,128,128]{2,1,0:T(8,128)} %copy-done.8, f32[4,128,128]{2,1,0:T(8,128)} %copy-done.9, f32[8,128]{1,0:T(8,128)} %copy-done.21), custom_call_target="tpu_custom_call" | custom-call | tf_op jit(solution)/shard_map/last/pallas_call | solution.py:312
  (53 shorter events, 15.1 us)
Async XLA Ops:
  1.6 11.8 %collective-permute-start.1 = (f32[2,128,128]{2,1,0:T(8,128)S(1)}, f32[2,128,128]{2,1,0:T(8,128)S(1)}, u32[]{:S(2)}, u32[]{:S(2)}) collective-permute-start(f32[2,128,128]{2,1,0:T(8,128)S(1)} %get-tuple-element.32), channel_id=1, source_target_pairs={{0,3},{1,2},{2,1},{3,0},{4,7},{5,6},{6,5},{7,4},{8,11},{9,10},{10,... | collective-permute-start | bytes 393224 | tf_op jit(solution)/shard_map/ppermute | solution.py:362
  5.0 8.4 %collective-permute-start = (f32[2,128,128]{2,1,0:T(8,128)S(1)}, f32[2,128,128]{2,1,0:T(8,128)S(1)}, u32[]{:S(2)}, u32[]{:S(2)}) collective-permute-start(f32[2,128,128]{2,1,0:T(8,128)S(1)} %get-tuple-element.33), channel_id=1, source_target_pairs={{0,1},{1,0},{2,3},{3,2},{4,5},{5,4},{6,7},{7,6},{8,9},{9,8},{10,11... | collective-permute-start | bytes 393224 | tf_op jit(solution)/shard_map/ppermute | solution.py:361
  7.4 4.1 %collective-permute-start.4 = (f32[40,128]{1,0:T(8,128)}, f32[40,128]{1,0:T(8,128)S(1)}, u32[]{:S(2)}, u32[]{:S(2)}) collective-permute-start(f32[40,128]{1,0:T(8,128)} %norm.1.own), channel_id=1, source_target_pairs={{0,3},{1,2},{2,1},{3,0},{4,7},{5,6},{6,5},{7,4},{8,11},{9,10},{10,... | collective-permute-start | bytes 61448 | tf_op jit(solution)/shard_map/ppermute | solution.py:364
  8.2 4.3 %collective-permute-start.3 = (f32[40,128]{1,0:T(8,128)}, f32[40,128]{1,0:T(8,128)S(1)}, u32[]{:S(2)}, u32[]{:S(2)}) collective-permute-start(f32[40,128]{1,0:T(8,128)} %norm.1.own), channel_id=1, source_target_pairs={{0,2},{1,3},{2,0},{3,1},{4,6},{5,7},{6,4},{7,5},{8,10},{9,11},{10,... | collective-permute-start | bytes 61448 | tf_op jit(solution)/shard_map/ppermute | solution.py:364
  10.6 2.8 %collective-permute-start.2 = (f32[40,128]{1,0:T(8,128)}, f32[40,128]{1,0:T(8,128)S(1)}, u32[]{:S(2)}, u32[]{:S(2)}) collective-permute-start(f32[40,128]{1,0:T(8,128)} %norm.1.own), channel_id=1, source_target_pairs={{0,1},{1,0},{2,3},{3,2},{4,5},{5,4},{6,7},{7,6},{8,9},{9,8},{10,11... | collective-permute-start | bytes 61448 | tf_op jit(solution)/shard_map/ppermute | solution.py:364
  13.5 1.6 copy-start
  15.1 1.6 copy-start.2
  16.7 0.9 copy-start.5
  17.6 0.7 copy-start.11
  18.9 0.7 copy-start.17
  19.6 0.7 copy-start.18
  20.3 0.7 copy-start.19
  27.1 64.5 %copy-start.1 = (bf16[16,4,128,128]{3,2,1,0:T(8,128)(2,1)S(1)}, bf16[16,4,128,128]{3,2,1,0:T(8,128)(2,1)}, u32[]{:S(2)}) copy-start(bf16[16,4,128,128]{3,2,1,0:T(8,128)(2,1)} %left.5) | copy-start | bytes 6291460
  27.1 64.5 %copy-start.13 = (s32[2]{0:T(128)S(1)}, s32[2]{0:T(128)}, u32[]{:S(2)}) copy-start(s32[2]{0:T(128)} %pad_add_fusion.ids) | copy-start | bytes 28
  27.1 64.5 %copy-start.20 = (s32[16]{0:T(128)S(1)}, s32[16]{0:T(128)}, u32[]{:S(2)}) copy-start(s32[16]{0:T(128)} %shift.5) | copy-start | bytes 196
  91.6 1.6 copy-start.3
  99.0 0.8 copy-start.6
  100.4 61.3 %copy-start.14 = (s32[2]{0:T(128)S(1)}, s32[2]{0:T(128)}, u32[]{:S(2)}) copy-start(s32[2]{0:T(128)} %pad_add_fusion.ids) | copy-start | bytes 28
  100.4 61.3 %copy-start.16 = (f32[8,128]{1,0:T(8,128)S(1)}, f32[8,128]{1,0:T(8,128)}, u32[]{:S(2)}) copy-start(f32[8,128]{1,0:T(8,128)} %copy-done.15) | copy-start | bytes 12292
  161.7 1.6 copy-start.4
  163.3 1.0 copy-start.7
  168.3 0.7 copy-start.8
  169.0 0.7 copy-start.9
  169.7 27.7 %copy-start.21 = (f32[8,128]{1,0:T(8,128)}, f32[8,128]{1,0:T(8,128)S(1)}, u32[]{:S(2)}) copy-start(f32[8,128]{1,0:T(8,128)S(1)} %get-tuple-element.29.scalars) | copy-start | bytes 12292
  (3 other events, 1.8 us)

commit v2 on v1

v2 whole, which is shorter than its diff:
```python
import jax
import jax.numpy as jnp
from jax import lax
from jax.experimental import pallas as pl
from jax.experimental.pallas import tpu as pltpu
from jax.sharding import Mesh, PartitionSpec as P

EPS = 1e-06
SECTORS = 16
BLOCK = 128
PAIRS = 16
OWN = 4
WINDOW = 8
PLANE = 32
CHUNK = 32
EXTRA = 8
ENTRIES = float(SECTORS * BLOCK * BLOCK)
PLANE_AXES = ("y", "z")
CROSS_AXES = ("c", "wf")
OP_AXES = ("y", "z", "c")

f32 = jnp.float32
bf16 = jnp.bfloat16


def dot(first, second, first_dim=1, second_dim=0):
    return lax.dot_general(
        first, second, (((first_dim,), (second_dim,)), ((), ())), preferred_element_type=f32
    )


def total(values):
    return jnp.sum(values, axis=(0, 1), keepdims=True)


def ratio(top, bottom):
    return jnp.where(bottom > 0, top / jnp.where(bottom > 0, bottom, 1.0), 0.0)


def place_here():
    return lax.axis_index("wf"), lax.axis_index("y") * lax.axis_size("z") + lax.axis_index("z")


def sector_at(wf, position):
    base = OWN * wf - 2
    return base + ((position - base) & 7)


def live(left_dims, right_dims, sector, first_row, rows):
    held = jnp.clip(sector, 0, SECTORS - 1)
    inside = (sector >= 0) & (sector < SECTORS)
    height = jnp.where(inside, left_dims[held], 0)
    width = right_dims[SECTORS - 1 - held]
    row = lax.broadcasted_iota(jnp.int32, (rows, BLOCK), 0) + first_row
    column = lax.broadcasted_iota(jnp.int32, (rows, BLOCK), 1)
    return (row < height) & (column < width)


def pack(values):
    lane = lax.broadcasted_iota(jnp.int32, (EXTRA, BLOCK), 1)
    packed = jnp.zeros((EXTRA, BLOCK), f32)
    for place, value in enumerate(values):
        packed = jnp.where(lane == place, value, packed)
    return packed


def lanes(rows, count):
    return [rows[:, place : place + 1] for place in range(count)]


def fetch(pairs, sems):
    copies = [
        pltpu.make_async_copy(source, target, sems.at[place])
        for place, (source, target) in enumerate(pairs)
    ]
    for copy in copies:
        copy.start()
    return copies


def norm_kernel(left_dims_hbm, right_dims_hbm, guess, out, side_one, side_three, *scratch):
    left_dims, right_dims, sems = scratch
    wf, chunk = place_here()
    copies = fetch([(left_dims_hbm, left_dims), (right_dims_hbm, right_dims)], sems)
    odd = wf & 1
    for i in range(2):
        side_one[i] = guess[2 - 2 * odd + i]
        side_three[i] = guess[2 * odd + i]
    for copy in copies:
        copy.wait()
    sums = jnp.zeros((1, 1), f32)
    for i in range(OWN):
        mask = live(left_dims, right_dims, OWN * wf + i, 0, BLOCK)
        block = jnp.where(mask, guess[i], 0.0)
        sums = sums + total(block * block)
    block, first_row = (chunk // 4) & 3, pl.multiple_of((chunk & 3) * CHUNK, CHUNK)
    mask = live(left_dims, right_dims, OWN * wf + block, first_row, CHUNK)
    out[0:EXTRA] = jnp.broadcast_to(sums, (EXTRA, BLOCK))
    out[EXTRA:] = jnp.where(mask, guess[block, pl.ds(first_row, CHUNK)], 0.0)


def half_step(shift, mask, left, right, vec_half, back, sector, index):
    for k in range(PAIRS):
        position = (sector + shift[k]) & 7
        weight = mask[k, index].astype(f32)
        value = dot(left[index, k].T, vec_half[position])
        back[:, k * BLOCK : (k + 1) * BLOCK] = (value * weight).astype(bf16)
    return dot(back[...], right[index].reshape(PAIRS * BLOCK, BLOCK))


def full_step(shift, mask, left, right, vec_half, back, out, sector, index):
    middle = dot(left[index].reshape(PAIRS * BLOCK, BLOCK), vec_half[sector & 7])
    for k in range(PAIRS):
        position = (sector + shift[k]) & 7
        weight = mask[k, index].astype(f32)
        term = (middle[k * BLOCK : (k + 1) * BLOCK] * weight).astype(bf16)
        out[position] += dot(term, right[index, k], 1, 1)
    out[sector & 7] += half_step(shift, mask, left, right, vec_half, back, sector, index)


def start_operators(hbm, held, sems, ints):
    pairs = [(source, target) for source, target in ints]
    for i in range(OWN):
        for source, target in zip(hbm, held):
            pairs.append((source.at[:, i], target.at[i]))
    copies = fetch(pairs, sems)
    return copies[: len(ints)], copies[len(ints) :]


def sweep(copies, body):
    for i in range(OWN):
        for copy in copies[2 * i : 2 * i + 2]:
            copy.wait()
        body(i)


def first_kernel(
    left_hbm, right_hbm, shift_hbm, mask_hbm, left_dims_hbm, right_dims_hbm,
    guess, side_one, side_three, own, one, two, three, out, vector, pieces,
    left, right, shift, mask, sems, vec_half, back, left_dims, right_dims,
):
    ints = [
        (left_dims_hbm, left_dims), (right_dims_hbm, right_dims),
        (shift_hbm, shift), (mask_hbm, mask),
    ]
    waits, copies = start_operators((left_hbm, right_hbm), (left, right), sems, ints)
    wf, chunk = place_here()
    sums = (own[0:1, 0:1] + one[0:1, 0:1]) + (two[0:1, 0:1] + three[0:1, 0:1])
    scale = 1.0 / jnp.sqrt(sums / ENTRIES + EPS)
    for copy in waits:
        copy.wait()

    def put(position, block):
        alive = live(left_dims, right_dims, sector_at(wf, position), 0, BLOCK)
        value = jnp.where(alive, block, 0.0) * scale
        vector[position] = value
        vec_half[position] = value.astype(bf16)

    odd = wf & 1
    for i in range(OWN):
        put(4 * odd + i, guess[i])
    for i in range(2):
        put(4 - 2 * odd + i, side_one[i])
        put(6 - 6 * odd + i, side_three[i])
    held = [own[EXTRA:], one[EXTRA:], two[EXTRA:], three[EXTRA:]]
    for place in range(2):
        source = (chunk // 16 + 2 * place) ^ wf
        value = held[0]
        for other in range(1, 4):
            value = jnp.where(source == other, held[other], value)
        pieces[place] = value * scale
    out[...] = jnp.zeros_like(out)

    def body(i):
        full_step(shift, mask, left, right, vec_half, back, out, OWN * wf + i, i)

    sweep(copies, body)


def spread_kernel(parts, out):
    summed = jnp.sum(parts[...], axis=0)
    for target in range(out.shape[0]):
        out[target] = summed


def combined(left_dims, right_dims, parts):
    _, chunk = place_here()
    position, first_row = chunk // 4, (chunk & 3) * CHUNK
    values = []
    for place in range(2):
        sector = position + 8 * place
        value = jnp.zeros((CHUNK, BLOCK), f32)
        for other in range(4):
            here = sector_at(other, position) == sector
            value = value + jnp.where(here, parts[other] + parts[4 + other], 0.0)
        values.append(jnp.where(live(left_dims, right_dims, sector, first_row, CHUNK), value, 0.0))
    return values


def send(values, sums, out):
    wf, chunk = place_here()
    position = chunk // 4
    sector = sector_at(wf, position)
    chosen = jnp.where(sector == position, values[0], 0.0)
    chosen = jnp.where(sector == position + 8, values[1], chosen)
    packed = pack(sums)
    for target in range(PLANE):
        out[target, 0:CHUNK] = chosen
        out[target, CHUNK:] = packed


def image_kernel(
    left_dims_hbm, right_dims_hbm, parts, pieces, out, image_pieces, left_dims, right_dims, sems
):
    for copy in fetch([(left_dims_hbm, left_dims), (right_dims_hbm, right_dims)], sems):
        copy.wait()
    image = combined(left_dims, right_dims, parts)
    vec = [pieces[0], pieces[1]]

    def inner(first, second):
        return total(first[0] * second[0] + first[1] * second[1])

    vec_vec, vec_image = inner(vec, vec), inner(vec, image)
    part = ratio(vec_image, vec_vec)
    rest = [image[i] - part * vec[i] for i in range(2)]
    for i in range(2):
        image_pieces[i] = image[i]
    send(image, [vec_image, vec_vec, part, inner(rest, rest)], out)


def second_kernel(
    left_hbm, right_hbm, shift_hbm, mask_hbm, gathered, vector,
    out, direction, image, scalars, left, right, shift, mask, sems, vec_half, back,
):
    ints = [(shift_hbm, shift), (mask_hbm, mask)]
    waits, copies = start_operators((left_hbm, right_hbm), (left, right), sems, ints)
    wf, _ = place_here()
    vec_image, vec_vec, part, rest = lanes(gathered[:, CHUNK, :], 4)
    ritz = total(vec_image) / ENTRIES
    apart = ritz - part
    norm = total(rest + apart * apart * vec_vec) / ENTRIES
    scale = 1.0 / jnp.sqrt(norm + EPS)
    scalars[...] = pack([ritz, norm])
    for position in range(WINDOW):
        held = gathered[4 * position : 4 * position + 4, 0:CHUNK, :].reshape(BLOCK, BLOCK)
        value = (held - ritz * vector[position]) * scale
        image[position] = held
        direction[position] = value
        vec_half[position] = value.astype(bf16)
    out[...] = jnp.zeros_like(out)
    for copy in waits:
        copy.wait()

    def body(i):
        full_step(shift, mask, left, right, vec_half, back, out, OWN * wf + i, i)

    sweep(copies, body)


def turned_kernel(
    left_dims_hbm, right_dims_hbm, parts, pieces, image_pieces, scalars, out,
    left_dims, right_dims, sems,
):
    for copy in fetch([(left_dims_hbm, left_dims), (right_dims_hbm, right_dims)], sems):
        copy.wait()
    turned = combined(left_dims, right_dims, parts)
    ritz, norm = scalars[0:1, 0:1], scalars[0:1, 1:2]
    scale = 1.0 / jnp.sqrt(norm + EPS)
    vec = [pieces[i] for i in range(2)]
    image = [image_pieces[i] for i in range(2)]
    turn = [(image[i] - ritz * vec[i]) * scale for i in range(2)]

    def inner(first, second):
        return total(first[0] * second[0] + first[1] * second[1])

    vec_vec, vec_turned = inner(vec, vec), inner(vec, turned)
    along = ratio(inner(vec, turn), vec_vec)
    new = [turn[i] - along * vec[i] for i in range(2)]
    on_vec = ratio(vec_turned, vec_vec)
    rest = [turned[i] - on_vec * vec[i] for i in range(2)]
    new_new = inner(new, new)
    on_new = ratio(inner(new, rest), new_new)
    rest = [rest[i] - on_new * new[i] for i in range(2)]
    sums = [
        vec_turned, inner(turn, image), inner(turn, turned),
        vec_vec, along, on_vec, new_new, on_new, inner(rest, rest),
    ]
    send(turned, sums, out)


def mixing(ritz, curvature, norm):
    gap = ritz - curvature
    lowest = 0.5 * (ritz + curvature) - jnp.sqrt(0.25 * gap * gap + norm)
    keep = curvature - lowest
    take = -jnp.sqrt(norm)
    scale = jnp.sqrt(keep * keep + take * take)
    return lowest, keep / scale, take / scale


def third_kernel(
    left_hbm, right_hbm, shift_hbm, mask_hbm, gathered, vector, direction, image, scalars,
    out, new_vector, new_direction, new_scalars, left, right, shift, mask, sems, vec_half, back,
):
    ints = [(shift_hbm, shift), (mask_hbm, mask)]
    waits, copies = start_operators((left_hbm, right_hbm), (left, right), sems, ints)
    wf, _ = place_here()
    (
        vec_turned, turn_image, turn_turned, vec_vec, along, on_vec, new_new, on_new, rest,
    ) = lanes(gathered[:, CHUNK, :], 9)
    ritz, norm = scalars[0:1, 0:1], scalars[0:1, 1:2]
    curvature = total(turn_turned) / ENTRIES
    lowest, keep, take = mixing(ritz, curvature, norm)
    mixed = (total(vec_turned) + total(turn_image)) / ENTRIES
    next_ritz = keep * keep * ritz + keep * take * mixed + take * take * curvature
    first = keep * (ritz - next_ritz)
    second = keep * jnp.sqrt(norm + EPS) - take * next_ritz
    on_first = first + second * along + take * on_vec
    on_second = second + take * on_new
    squares = on_first * on_first * vec_vec + on_second * on_second * new_new
    next_norm = total(squares + take * take * rest) / ENTRIES
    scale = 1.0 / jnp.sqrt(next_norm + EPS)
    new_scalars[...] = pack([next_ritz, next_norm, lowest])
    for position in range(WINDOW):
        turned = gathered[4 * position : 4 * position + 4, 0:CHUNK, :].reshape(BLOCK, BLOCK)
        mixed_vec = keep * vector[position] + take * direction[position]
        mixed_image = keep * image[position] + take * turned
        value = (mixed_image - next_ritz * mixed_vec) * scale
        vec_half[position] = value.astype(bf16)

        @pl.when((position // 4) == (wf & 1))
        def _():
            new_vector[position % 4] = mixed_vec
            new_direction[position % 4] = value

    for copy in waits:
        copy.wait()
    sums = []

    def body(i):
        half = half_step(shift, mask, left, right, vec_half, back, OWN * wf + i, i)
        sums.append(total(half * new_direction[i]))

    sweep(copies, body)
    value = jnp.broadcast_to(2.0 * (sums[0] + sums[1] + sums[2] + sums[3]), out.shape)
    out[...] = value


def last_kernel(parts, vector, direction, scalars, out, energies):
    curvature = total(parts[...])[0:1] / (BLOCK * ENTRIES)
    ritz, norm, first_lowest = lanes(scalars[0:1], 3)
    lowest, keep, take = mixing(ritz, curvature, norm)
    for i in range(OWN):
        out[i] = keep * vector[i] + take * direction[i]
    energies[0] = first_lowest[0, 0]
    energies[1] = lowest[0, 0]


def sums_kernel(parts, out):
    out[...] = jnp.broadcast_to(jnp.sum(parts[...], axis=0, keepdims=True), out.shape)


HBM = pl.BlockSpec(memory_space=pltpu.HBM)
VMEM = pl.BlockSpec(memory_space=pltpu.VMEM)
SMEM = pl.BlockSpec(memory_space=pltpu.SMEM)


def struct(*shape):
    return jax.ShapeDtypeStruct(shape, f32)


def small(kernel, name, outs, dims, *arrays, out_specs=None):
    scratch = [pltpu.SMEM((SECTORS,), jnp.int32)] * 2 + [pltpu.SemaphoreType.DMA((2,))]
    return pl.pallas_call(
        kernel,
        name=name,
        in_specs=[HBM] * len(dims) + [VMEM] * len(arrays),
        out_specs=out_specs or [VMEM] * len(outs),
        out_shape=outs,
        scratch_shapes=scratch if dims else [],
        compiler_params=pltpu.CompilerParams(vmem_limit_bytes=6 << 20),
    )(*dims, *arrays)


def step(kernel, name, outs, ints, arrays, operators, extra=()):
    held = pltpu.VMEM((OWN, PAIRS, BLOCK, BLOCK), bf16)
    return pl.pallas_call(
        kernel,
        name=name,
        in_specs=[HBM] * (2 + len(ints)) + [VMEM] * len(arrays),
        out_specs=[VMEM] * len(outs),
        out_shape=outs,
        scratch_shapes=[
            held,
            held,
            pltpu.SMEM((PAIRS,), jnp.int32),
            pltpu.SMEM((PAIRS, OWN), jnp.int32),
            pltpu.SemaphoreType.DMA((len(ints) + 2 * OWN,)),
            pltpu.VMEM((WINDOW, BLOCK, BLOCK), bf16),
            pltpu.VMEM((BLOCK, PAIRS * BLOCK), bf16),
            *extra,
        ],
        compiler_params=pltpu.CompilerParams(vmem_limit_bytes=20 << 20),
    )(*operators, *ints, *arrays)


def exchange(value, axes):
    return lax.all_to_all(value, axes, 0, 0, tiled=True)


def shards(guess, left_ops, right_ops, op_shift, op_mask, left_dims, right_dims):
    operators = (left_ops, right_ops)
    dims = (left_dims, right_dims)
    ints = (op_shift, op_mask)
    blocks = struct(WINDOW, BLOCK, BLOCK)
    pair = struct(2, BLOCK, BLOCK)

    def partner(value, distance):
        return lax.ppermute(value, "wf", [(i, i ^ distance) for i in range(4)])

    own, side_one, side_three = small(
        norm_kernel, "norm", [struct(EXTRA + CHUNK, BLOCK), pair, pair], dims, guess
    )
    side_one, side_three = partner(side_one, 1), partner(side_three, 3)
    others = [partner(own, distance) for distance in (1, 2, 3)]

    def reduced(partial):
        parts = exchange(partial.reshape(PLANE, CHUNK, BLOCK), PLANE_AXES)
        (tiled,) = small(spread_kernel, "spread", [struct(8, CHUNK, BLOCK)], (), parts)
        return exchange(tiled, CROSS_AXES)

    partial, vector, pieces = step(
        first_kernel, "first", [blocks, blocks, struct(2, CHUNK, BLOCK)], (*ints, *dims),
        (guess, side_one, side_three, own, *others), operators,
        [pltpu.SMEM((SECTORS,), jnp.int32)] * 2,
    )
    packet = struct(PLANE, CHUNK + EXTRA, BLOCK)
    packets, image_pieces = small(
        image_kernel, "image", [packet, struct(2, CHUNK, BLOCK)], dims, reduced(partial), pieces
    )
    gathered = exchange(packets, PLANE_AXES)
    partial, direction, image, scalars = step(
        second_kernel, "second", [blocks, blocks, blocks, struct(EXTRA, BLOCK)], ints,
        (gathered, vector), operators,
    )
    (packets,) = small(
        turned_kernel, "turned", [packet], dims, reduced(partial), pieces, image_pieces, scalars
    )
    gathered = exchange(packets, PLANE_AXES)
    own_blocks = struct(OWN, BLOCK, BLOCK)
    sums, vector, direction, scalars = step(
        third_kernel, "third",
        [struct(8, BLOCK), own_blocks, own_blocks, struct(EXTRA, BLOCK)], ints,
        (gathered, vector, direction, image, scalars), operators,
    )
    sums = exchange(sums, CROSS_AXES)
    (sums,) = small(sums_kernel, "sums", [struct(PLANE, BLOCK)], (), sums)
    sums = exchange(sums, PLANE_AXES)
    result, energies = small(
        last_kernel, "last", [own_blocks, struct(2)], (), sums, vector, direction, scalars,
        out_specs=[VMEM, SMEM],
    )
    return result, energies


def solution(mesh):
    split = Mesh(mesh.devices.reshape(4, 8, 2, 4), (*OP_AXES, "wf"))
    in_specs = (
        P("wf", None, None),
        P(OP_AXES, "wf", None, None),
        P(OP_AXES, "wf", None, None),
        P(OP_AXES),
        P(OP_AXES, "wf"),
        P(),
        P(),
    )
    out_specs = (P("wf", None, None), P())
    return jax.shard_map(
        shards, mesh=split, in_specs=in_specs, out_specs=out_specs, check_vma=False
    )
```

time: 202 us -> 177 us (0.88)
  Pallas kernels: 28.4 us -> 18.8 us
  local copies, waits for them, and re-layouts: 18.1 us -> 9.13 us
  blocking collectives: 144 us -> 139 us
    pallas_call x10, Pallas kernels: 28.4 us -> 18.8 us  [the longest x3 15 us: step(): pl.pallas_call(kernel, name=name, in_specs=[HBM] * (2 + len(ints)) + [VME...]
    unnamed x45 -> x29, local copies, waits for them, and re-layouts: 15.8 us -> 9.13 us
    all_to_all x8, blocking collectives: 144 us -> 139 us  [exchange(): return lax.all_to_all(value, axes, 0, 0, tiled=True)]
  transfers between devices with their start and end apart: 5 -> 5, of which waited for: 2 -> 2; matrix products, arithmetic and copies ran while one was open for 1% -> 0% of each run, Pallas kernels for 1% -> 0%
where the time goes in v2:
time: 177 us; the launch traced here: 176 us
  blocking collectives  139 us (79%)
  Pallas kernels  18.8 us (11%)
  local copies, waits for them, and re-layouts  9.13 us (5%)
  starting transfers between devices  7.2 us (4%)
    all_to_all x8, blocking collectives, exchange(): return lax.all_to_all(value, axes, 0, 0, tiled=True)  139 us
    pallas_call x3, Pallas kernels, step(): pl.pallas_call(kernel, name=name, in_specs=[HBM] * (2 + len(ints)) + [VME...  15 us
    unnamed x29, local copies, waits for them, and re-layouts  9.13 us
    ppermute x5, starting transfers between devices, partner(): return lax.ppermute(value, 'wf', [(i, i ^ distance) for i in range(4)])  7.2 us
    pallas_call x7, Pallas kernels, small(): pl.pallas_call(kernel, name=name, in_specs=[HBM] * len(dims) + [VMEM] * l...  3.84 us
  transfers between devices with their start and end apart: 5, of which 2 were waited for; matrix products, arithmetic and copies ran while one was open for 0% of the time, Pallas kernels for 0%

profile of v2, /device:TPU:1, one launch (start us, length us, event | category | flops | bytes accessed | tf_op | source)
XLA Modules:
  0.0 176.2 jit_solution(3253651073122636229)
XLA Ops:
  0.6 0.9 copy-done.4
  3.6 2.1 %collective-permute-start = (f32[2,128,128]{2,1,0:T(8,128)S(1)}, f32[2,128,128]{2,1,0:T(8,128)S(1)}, u32[]{:S(2)}, u32[]{:S(2)}) collective-permute-start(f32[2,128,128]{2,1,0:T(8,128)S(1)} %get-tuple-element.18), channel_id=1, source_target_pairs={{0,1},{1,0},{2,3},{3,2},{4,5},{5,4},{6,7},{7,6},{8,9},{9,8},{10,11... | collective-permute-start | bytes 393224 | tf_op jit(solution)/shard_map/ppermute | solution.py:418
  5.8 1.8 %collective-permute-start.1 = (f32[2,128,128]{2,1,0:T(8,128)S(1)}, f32[2,128,128]{2,1,0:T(8,128)S(1)}, u32[]{:S(2)}, u32[]{:S(2)}) collective-permute-start(f32[2,128,128]{2,1,0:T(8,128)S(1)} %get-tuple-element.19), channel_id=1, source_target_pairs={{0,3},{1,2},{2,1},{3,0},{4,7},{5,6},{6,5},{7,4},{8,11},{9,10},{10,... | collective-permute-start | bytes 393224 | tf_op jit(solution)/shard_map/ppermute | solution.py:418
  7.6 0.9 collective-permute-start.4
  8.5 1.2 collective-permute-start.3
  9.7 1.2 collective-permute-start.2
  12.0 0.8 collective-permute-done.3.two
  12.7 1.6 copy-done
  14.3 1.6 copy-done.2
  15.9 0.9 copy-done.5
  18.8 5.6 %first.1 = (f32[8,128,128]{2,1,0:T(8,128)S(1)}, f32[8,128,128]{2,1,0:T(8,128)S(1)}, f32[2,32,128]{2,1,0:T(8,128)S(1)}) custom-call(bf16[16,4,128,128]{3,2,1,0:T(8,128)(2,1)S(1)} %copy-done, bf16[16,4,128,128]{3,2,1,0:T(8,128)(2,1)S(1)} %copy-done.2, s32[16]{0:T(128)S(1)} %copy-done.12, s32[16,4]{1,0:T(8,128)S(1)} %copy.14.mask_hbm, s32[16]{0:T(128)S(1)} %copy-done.7, ...), custom_call_target="tpu_custom_call" | custom-call | tf_op jit(solution)/shard_map/first/pallas_call | solution.py:386
  24.5 23.3 %all_to_all.52.parts = f32[32,32,128]{2,1,0:T(8,128)S(1)} all-to-all(f32[32,32,128]{2,1,0:T(8,128)S(1)} %bitcast.10), channel_id=1, replica_groups=mesh['y'=4,'z'=8,'c'=2,'wf'=4] {'y','z'}, dimensions={0} | all-to-all | bytes 1048576 | tf_op jit(solution)/shard_map/all_to_all | solution.py:407
  47.9 13.7 %all_to_all.53.parts = f32[8,32,128]{2,1,0:T(8,128)S(1)} all-to-all(f32[8,32,128]{2,1,0:T(8,128)S(1)} %spread.2), channel_id=1, replica_groups=mesh['y'=4,'z'=8,'c'=2,'wf'=4] {'c','wf'}, dimensions={0} | all-to-all | bytes 262144 | tf_op jit(solution)/shard_map/all_to_all | solution.py:407
  61.6 0.9 image.1
  62.5 22.2 %all_to_all.54.gathered = f32[32,40,128]{2,1,0:T(8,128)S(1)} all-to-all(f32[32,40,128]{2,1,0:T(8,128)S(1)} %get-tuple-element.23), channel_id=1, replica_groups=mesh['y'=4,'z'=8,'c'=2,'wf'=4] {'y','z'}, dimensions={0} | all-to-all | bytes 1310720 | tf_op jit(solution)/shard_map/all_to_all | solution.py:407
  84.7 5.6 %second.1 = (f32[8,128,128]{2,1,0:T(8,128)S(1)}, f32[8,128,128]{2,1,0:T(8,128)S(1)}, f32[8,128,128]{2,1,0:T(8,128)S(1)}, f32[8,128]{1,0:T(8,128)S(1)}) custom-call(bf16[16,4,128,128]{3,2,1,0:T(8,128)(2,1)S(1)} %copy-done.1, bf16[16,4,128,128]{3,2,1,0:T(8,128)(2,1)S(1)} %copy-done.3, s32[16]{0:T(128)S(1)} %copy-done.13, s32[16,4]{1,0:T(8,128)S(1)} %copy.14.mask_hbm, ...), custom_call_target="tpu_custom_call" | custom-call | tf_op jit(solution)/shard_map/second/pallas_call | solution.py:386
  90.3 22.0 %all_to_all.55.parts = f32[32,32,128]{2,1,0:T(8,128)S(1)} all-to-all(f32[32,32,128]{2,1,0:T(8,128)S(1)} %bitcast.11), channel_id=1, replica_groups=mesh['y'=4,'z'=8,'c'=2,'wf'=4] {'y','z'}, dimensions={0} | all-to-all | bytes 1048576 | tf_op jit(solution)/shard_map/all_to_all | solution.py:407
  112.3 11.7 %all_to_all.56.parts = f32[8,32,128]{2,1,0:T(8,128)S(1)} all-to-all(f32[8,32,128]{2,1,0:T(8,128)S(1)} %spread.3), channel_id=1, replica_groups=mesh['y'=4,'z'=8,'c'=2,'wf'=4] {'c','wf'}, dimensions={0} | all-to-all | bytes 262144 | tf_op jit(solution)/shard_map/all_to_all | solution.py:407
  124.0 1.1 turned.1
  125.1 21.6 %all_to_all.57.gathered = f32[32,40,128]{2,1,0:T(8,128)S(1)} all-to-all(f32[32,40,128]{2,1,0:T(8,128)S(1)} %turned.1), channel_id=1, replica_groups=mesh['y'=4,'z'=8,'c'=2,'wf'=4] {'y','z'}, dimensions={0} | all-to-all | bytes 1310720 | tf_op jit(solution)/shard_map/all_to_all | solution.py:407
  146.7 3.8 %third.1 = (f32[8,128]{1,0:T(8,128)S(1)}, f32[4,128,128]{2,1,0:T(8,128)S(1)}, f32[4,128,128]{2,1,0:T(8,128)S(1)}, f32[8,128]{1,0:T(8,128)S(1)}) custom-call(bf16[16,4,128,128]{3,2,1,0:T(8,128)(2,1)S(1)} %copy-done.1, bf16[16,4,128,128]{3,2,1,0:T(8,128)(2,1)S(1)} %copy-done.3, s32[16]{0:T(128)S(1)} %copy-done.13, s32[16,4]{1,0:T(8,128)S(1)} %copy.14.mask_hbm, ...), custom_call_target="tpu_custom_call" | custom-call | tf_op jit(solution)/shard_map/third/pallas_call | solution.py:386
  150.5 11.6 %all_to_all.58 = f32[8,1,128]{2,1,0:T(1,128)S(1)} all-to-all(f32[8,1,128]{2,1,0:T(1,128)S(1)} %bitcast.15), channel_id=1, replica_groups=mesh['y'=4,'z'=8,'c'=2,'wf'=4] {'c','wf'}, dimensions={0} | all-to-all | bytes 8192 | tf_op jit(solution)/shard_map/all_to_all | solution.py:407
  162.1 12.9 %all_to_all.59 = f32[32,1,128]{2,1,0:T(1,128)S(1)} all-to-all(f32[32,1,128]{2,1,0:T(1,128)S(1)} %bitcast.13), channel_id=1, replica_groups=mesh['y'=4,'z'=8,'c'=2,'wf'=4] {'y','z'}, dimensions={0} | all-to-all | bytes 32768 | tf_op jit(solution)/shard_map/all_to_all | solution.py:407
  174.9 1.1 last.1
  (33 shorter events, 5.3 us)
Async XLA Ops:
  0.6 1.0 copy-start.4
  1.6 0.7 copy-start.6
  2.2 0.7 copy-start.9
  3.6 9.1 %collective-permute-start = (f32[2,128,128]{2,1,0:T(8,128)S(1)}, f32[2,128,128]{2,1,0:T(8,128)S(1)}, u32[]{:S(2)}, u32[]{:S(2)}) collective-permute-start(f32[2,128,128]{2,1,0:T(8,128)S(1)} %get-tuple-element.18), channel_id=1, source_target_pairs={{0,1},{1,0},{2,3},{3,2},{4,5},{5,4},{6,7},{7,6},{8,9},{9,8},{10,11... | collective-permute-start | bytes 393224 | tf_op jit(solution)/shard_map/ppermute | solution.py:418
  5.8 6.9 %collective-permute-start.1 = (f32[2,128,128]{2,1,0:T(8,128)S(1)}, f32[2,128,128]{2,1,0:T(8,128)S(1)}, u32[]{:S(2)}, u32[]{:S(2)}) collective-permute-start(f32[2,128,128]{2,1,0:T(8,128)S(1)} %get-tuple-element.19), channel_id=1, source_target_pairs={{0,3},{1,2},{2,1},{3,0},{4,7},{5,6},{6,5},{7,4},{8,11},{9,10},{10,... | collective-permute-start | bytes 393224 | tf_op jit(solution)/shard_map/ppermute | solution.py:418
  7.6 4.4 %collective-permute-start.4 = (f32[40,128]{1,0:T(8,128)S(1)}, f32[40,128]{1,0:T(8,128)S(1)}, u32[]{:S(2)}, u32[]{:S(2)}) collective-permute-start(f32[40,128]{1,0:T(8,128)S(1)} %get-tuple-element.20.own), channel_id=1, source_target_pairs={{0,3},{1,2},{2,1},{3,0},{4,7},{5,6},{6,5},{7,4},{8,11},{9,10},{10,... | collective-permute-start | bytes 61448 | tf_op jit(solution)/shard_map/ppermute | solution.py:418
  8.5 4.2 %collective-permute-start.3 = (f32[40,128]{1,0:T(8,128)S(1)}, f32[40,128]{1,0:T(8,128)S(1)}, u32[]{:S(2)}, u32[]{:S(2)}) collective-permute-start(f32[40,128]{1,0:T(8,128)S(1)} %get-tuple-element.20.own), channel_id=1, source_target_pairs={{0,2},{1,3},{2,0},{3,1},{4,6},{5,7},{6,4},{7,5},{8,10},{9,11},{10,... | collective-permute-start | bytes 61448 | tf_op jit(solution)/shard_map/ppermute | solution.py:418
  9.7 3.0 %collective-permute-start.2 = (f32[40,128]{1,0:T(8,128)S(1)}, f32[40,128]{1,0:T(8,128)S(1)}, u32[]{:S(2)}, u32[]{:S(2)}) collective-permute-start(f32[40,128]{1,0:T(8,128)S(1)} %get-tuple-element.20.own), channel_id=1, source_target_pairs={{0,1},{1,0},{2,3},{3,2},{4,5},{5,4},{6,7},{7,6},{8,9},{9,8},{10,11... | collective-permute-start | bytes 61448 | tf_op jit(solution)/shard_map/ppermute | solution.py:418
  12.7 1.6 copy-start
  14.3 1.6 copy-start.2
  15.9 0.9 copy-start.5
  16.9 0.7 copy-start.7
  17.5 0.7 copy-start.10
  18.2 0.7 copy-start.12
  18.8 65.9 %copy-start.3 = (bf16[16,4,128,128]{3,2,1,0:T(8,128)(2,1)S(1)}, bf16[16,4,128,128]{3,2,1,0:T(8,128)(2,1)}, u32[]{:S(2)}) copy-start(bf16[16,4,128,128]{3,2,1,0:T(8,128)(2,1)} %right_hbm.5) | copy-start | bytes 6291460
  24.5 60.2 %copy-start.1 = (bf16[16,4,128,128]{3,2,1,0:T(8,128)(2,1)S(1)}, bf16[16,4,128,128]{3,2,1,0:T(8,128)(2,1)}, u32[]{:S(2)}) copy-start(bf16[16,4,128,128]{3,2,1,0:T(8,128)(2,1)} %left_hbm.5) | copy-start | bytes 6291460
  24.5 60.2 %copy-start.13 = (s32[16]{0:T(128)S(1)}, s32[16]{0:T(128)}, u32[]{:S(2)}) copy-start(s32[16]{0:T(128)} %shift_hbm.5) | copy-start | bytes 196
  84.7 39.3 %copy-start.8 = (s32[16]{0:T(128)S(1)}, s32[16]{0:T(128)}, u32[]{:S(2)}) copy-start(s32[16]{0:T(128)} %left_dims_hbm.7) | copy-start | bytes 196
  84.7 39.3 %copy-start.11 = (s32[16]{0:T(128)S(1)}, s32[16]{0:T(128)}, u32[]{:S(2)}) copy-start(s32[16]{0:T(128)} %right_dims_hbm.7) | copy-start | bytes 196

commit v3 on v2

v3 whole, which is shorter than its diff:
```python
import jax
import jax.numpy as jnp
from jax import lax
from jax.experimental import pallas as pl
from jax.experimental.pallas import tpu as pltpu
from jax.sharding import Mesh, PartitionSpec as P

EPS = 1e-06
SECTORS = 16
BLOCK = 128
PAIRS = 16
OWN = 4
WINDOW = 8
PLANE = 32
HALF = 4
CHUNK = 16
SIDE = 2 * BLOCK
EXTRA = 8
ENTRIES = float(SECTORS * BLOCK * BLOCK)
PLANE_AXES = ("y", "z")
CROSS_AXES = ("c", "wf")
OP_AXES = ("y", "z", "c")

f32 = jnp.float32
bf16 = jnp.bfloat16


def dot(first, second, first_dim=1, second_dim=0):
    return lax.dot_general(
        first, second, (((first_dim,), (second_dim,)), ((), ())), preferred_element_type=f32
    )


def total(values):
    return jnp.sum(values, axis=(0, 1), keepdims=True)


def ratio(top, bottom):
    return jnp.where(bottom > 0, top / jnp.where(bottom > 0, bottom, 1.0), 0.0)


def place_here():
    chunk = lax.axis_index("y") * lax.axis_size("z") + lax.axis_index("z")
    first_row = pl.multiple_of((chunk & 7) * CHUNK, CHUNK)
    return lax.axis_index("wf"), HALF * lax.axis_index("c") + chunk // 8, first_row


def sector_at(wf, position):
    base = OWN * wf - 2
    return base + ((position - base) & 7)


def live(left_dims, right_dims, sector, first_row, rows):
    held = jnp.clip(sector, 0, SECTORS - 1)
    inside = (sector >= 0) & (sector < SECTORS)
    height = jnp.where(inside, left_dims[held], 0)
    width = right_dims[SECTORS - 1 - held]
    row = lax.broadcasted_iota(jnp.int32, (rows, BLOCK), 0) + first_row
    column = lax.broadcasted_iota(jnp.int32, (rows, BLOCK), 1)
    return (row < height) & (column < width)


def pack(values):
    lane = lax.broadcasted_iota(jnp.int32, (EXTRA, BLOCK), 1)
    packed = jnp.zeros((EXTRA, BLOCK), f32)
    for place, value in enumerate(values):
        packed = jnp.where(lane == place, value, packed)
    return packed


def lanes(rows, count):
    return [rows[:, place : place + 1] for place in range(count)]


def load_kernel(left_hbm, right_hbm, left, right, sems):
    copies = []
    for i in range(OWN):
        for source, target in ((left_hbm, left), (right_hbm, right)):
            copies.append(
                pltpu.make_async_copy(source.at[:, i], target.at[i], sems.at[len(copies)])
            )
    for copy in copies:
        copy.start()
    for copy in copies:
        copy.wait()


def norm_kernel(left_dims, right_dims, guess, start, masks, one, two, three):
    wf, position, first_row = place_here()
    sums = jnp.zeros((1, 1), f32)
    for i in range(OWN):
        mask = live(left_dims, right_dims, OWN * wf + i, 0, BLOCK)
        block = jnp.where(mask, guess[i], 0.0)
        start[i] = block
        sums = sums + total(block * block)
    odd = wf & 1
    for i in range(2):
        one[i * BLOCK : (i + 1) * BLOCK] = start[2 - 2 * odd + i]
        three[i * BLOCK : (i + 1) * BLOCK] = start[2 * odd + i]
    for out, first in ((one, SIDE), (two, 0), (three, SIDE)):
        out[first : first + EXTRA] = jnp.broadcast_to(sums, (EXTRA, BLOCK))
        out[first + EXTRA :] = start[position & 3, pl.ds(first_row, CHUNK)]
    for i in range(2):
        mask = live(left_dims, right_dims, position + 8 * i, first_row, CHUNK)
        masks[i] = jnp.where(mask, 1.0, 0.0)


def half_step(table, left, right, vec_half, back, sector, index):
    for k in range(PAIRS):
        entry = table[k * OWN + index]
        position = (sector + (entry >> 1)) & 7
        weight = (entry & 1).astype(f32)
        value = dot(left[index, k].T, vec_half[position])
        back[:, k * BLOCK : (k + 1) * BLOCK] = (value * weight).astype(bf16)
    return dot(back[...], right[index].reshape(PAIRS * BLOCK, BLOCK))


def full_step(table, left, right, vec_half, back, sums, sector, index):
    middle = dot(left[index].reshape(PAIRS * BLOCK, BLOCK), vec_half[sector & 7])
    for k in range(PAIRS):
        entry = table[k * OWN + index]
        position = (sector + (entry >> 1)) & 7
        weight = (entry & 1).astype(f32)
        term = (middle[k * BLOCK : (k + 1) * BLOCK] * weight).astype(bf16)
        sums[position] += dot(term, right[index, k], 1, 1)
    sums[sector & 7] += half_step(table, left, right, vec_half, back, sector, index)


def full_sweep(table, left, right, vec_half, back, sums, keep, give):
    sums[...] = jnp.zeros_like(sums)
    first_sector = OWN * lax.axis_index("wf")
    for i in range(OWN):
        full_step(table, left, right, vec_half, back, sums, first_sector + i, i)
    core = lax.axis_index("c")
    for i in range(HALF):
        keep[i] = sums[HALF * core + i]
        give[i] = sums[HALF - HALF * core + i]


def first_kernel(
    table, left, right, start, own, one, two, three, keep, give, vector, pieces,
    vec_half, back, sums,
):
    wf = lax.axis_index("wf")
    squares = (own[0:1, 0:1] + one[SIDE : SIDE + 1, 0:1]) + (
        two[0:1, 0:1] + three[SIDE : SIDE + 1, 0:1]
    )
    scale = 1.0 / jnp.sqrt(squares / ENTRIES + EPS)

    def put(position, block):
        sector = sector_at(wf, position)
        inside = (sector >= 0) & (sector < SECTORS)
        value = jnp.where(inside, block * scale, 0.0)
        vector[position] = value
        vec_half[position] = value.astype(bf16)

    odd = wf & 1
    for i in range(OWN):
        put(4 * odd + i, start[i])
    for i in range(2):
        rows = slice(i * BLOCK, (i + 1) * BLOCK)
        put(4 - 2 * odd + i, one[rows])
        put(6 - 6 * odd + i, three[rows])
    held = [own[EXTRA:], one[SIDE + EXTRA :], two[EXTRA:], three[SIDE + EXTRA :]]
    for place in range(2):
        source = (lax.axis_index("c") + 2 * place) ^ wf
        value = held[0]
        for other in range(1, 4):
            value = jnp.where(source == other, held[other], value)
        pieces[place] = value * scale
    full_sweep(table, left, right, vec_half, back, sums, keep, give)


def join_kernel(first, second, out):
    out[...] = first[...] + second[...]


def spread_kernel(parts, out):
    summed = jnp.sum(parts[...], axis=0)
    for target in range(out.shape[0]):
        out[target] = summed


def combined(masks, parts):
    _, position, _ = place_here()
    values = []
    for place in range(2):
        value = jnp.zeros((CHUNK, BLOCK), f32)
        for other in range(4):
            here = sector_at(other, position) == position + 8 * place
            value = value + jnp.where(here, parts[other], 0.0)
        values.append(value * masks[place])
    return values


def send(values, sums, out):
    wf, position, _ = place_here()
    sector = sector_at(wf, position)
    chosen = jnp.where(sector == position, values[0], 0.0)
    chosen = jnp.where(sector == position + 8, values[1], chosen)
    packed = pack(sums)
    for target in range(PLANE):
        out[target, 0:CHUNK] = chosen
        out[target, CHUNK:] = packed


def image_kernel(parts, masks, pieces, out, image_pieces):
    image = combined(masks, parts)
    vec = [pieces[0], pieces[1]]

    def inner(first, second):
        return total(first[0] * second[0] + first[1] * second[1])

    vec_vec, vec_image = inner(vec, vec), inner(vec, image)
    part = ratio(vec_image, vec_vec)
    rest = [image[i] - part * vec[i] for i in range(2)]
    for i in range(2):
        image_pieces[i] = image[i]
    send(image, [vec_image, vec_vec, part, inner(rest, rest)], out)


def both(cores, count):
    return zip(*[lanes(held[:, CHUNK, :], count) for held in cores])


def add(values):
    return total(values[0]) + total(values[1])


def held_block(cores, position):
    rows = slice(8 * (position % HALF), 8 * (position % HALF) + 8)
    own, other = (held[rows, 0:CHUNK, :].reshape(BLOCK, BLOCK) for held in cores)
    return jnp.where(lax.axis_index("c") == position // HALF, own, other)


def second_kernel(
    table, left, right, own, other, vector, keep, give, direction, image, scalars,
    vec_half, back, sums,
):
    cores = (own, other)
    vec_image, vec_vec, part, rest = both(cores, 4)
    ritz = add(vec_image) / ENTRIES
    norm = add([rest[i] + (ritz - part[i]) * (ritz - part[i]) * vec_vec[i] for i in range(2)])
    norm = norm / ENTRIES
    scale = 1.0 / jnp.sqrt(norm + EPS)
    scalars[...] = pack([ritz, norm])
    for position in range(WINDOW):
        held = held_block(cores, position)
        value = (held - ritz * vector[position]) * scale
        image[position] = held
        direction[position] = value
        vec_half[position] = value.astype(bf16)
    full_sweep(table, left, right, vec_half, back, sums, keep, give)


def turned_kernel(parts, masks, pieces, image_pieces, scalars, out):
    turned = combined(masks, parts)
    ritz, norm = scalars[0:1, 0:1], scalars[0:1, 1:2]
    scale = 1.0 / jnp.sqrt(norm + EPS)
    vec = [pieces[i] for i in range(2)]
    image = [image_pieces[i] for i in range(2)]
    turn = [(image[i] - ritz * vec[i]) * scale for i in range(2)]

    def inner(first, second):
        return total(first[0] * second[0] + first[1] * second[1])

    vec_vec, vec_turned = inner(vec, vec), inner(vec, turned)
    along = ratio(inner(vec, turn), vec_vec)
    new = [turn[i] - along * vec[i] for i in range(2)]
    on_vec = ratio(vec_turned, vec_vec)
    rest = [turned[i] - on_vec * vec[i] for i in range(2)]
    new_new = inner(new, new)
    on_new = ratio(inner(new, rest), new_new)
    rest = [rest[i] - on_new * new[i] for i in range(2)]
    sums = [
        vec_turned, inner(turn, image), inner(turn, turned),
        vec_vec, along, on_vec, new_new, on_new, inner(rest, rest),
    ]
    send(turned, sums, out)


def mixing(ritz, curvature, norm):
    gap = ritz - curvature
    lowest = 0.5 * (ritz + curvature) - jnp.sqrt(0.25 * gap * gap + norm)
    keep = curvature - lowest
    take = -jnp.sqrt(norm)
    scale = jnp.sqrt(keep * keep + take * take)
    return lowest, keep / scale, take / scale


def third_kernel(
    table, left, right, gathered, swapped, vector, direction, image, scalars,
    out, new_vector, new_direction, new_scalars, vec_half, back,
):
    cores = (gathered, swapped)
    wf = lax.axis_index("wf")
    (
        vec_turned, turn_image, turn_turned, vec_vec, along, on_vec, new_new, on_new, rest,
    ) = both(cores, 9)
    ritz, norm = scalars[0:1, 0:1], scalars[0:1, 1:2]
    curvature = add(turn_turned) / ENTRIES
    lowest, keep, take = mixing(ritz, curvature, norm)
    mixed = (add(vec_turned) + add(turn_image)) / ENTRIES
    next_ritz = keep * keep * ritz + keep * take * mixed + take * take * curvature
    first = keep * (ritz - next_ritz)
    second = keep * jnp.sqrt(norm + EPS) - take * next_ritz
    squares = []
    for i in range(2):
        on_first = first + second * along[i] + take * on_vec[i]
        on_second = second + take * on_new[i]
        square = on_first * on_first * vec_vec[i] + on_second * on_second * new_new[i]
        squares.append(square + take * take * rest[i])
    next_norm = add(squares) / ENTRIES
    scale = 1.0 / jnp.sqrt(next_norm + EPS)
    new_scalars[...] = pack([next_ritz, next_norm, lowest])
    for position in range(WINDOW):
        turned = held_block(cores, position)
        mixed_vec = keep * vector[position] + take * direction[position]
        mixed_image = keep * image[position] + take * turned
        value = (mixed_image - next_ritz * mixed_vec) * scale
        vec_half[position] = value.astype(bf16)

        @pl.when((position // 4) == (wf & 1))
        def _():
            new_vector[position % 4] = mixed_vec
            new_direction[position % 4] = value

    value = jnp.zeros((1, 1), f32)
    for i in range(OWN):
        half = half_step(table, left, right, vec_half, back, OWN * wf + i, i)
        value = value + total(half * new_direction[i])
    out[...] = jnp.broadcast_to(2.0 * value, out.shape)


def last_kernel(parts, vector, direction, scalars, out, energies):
    curvature = total(parts[...])[0:1] / (BLOCK * ENTRIES)
    ritz, norm, first_lowest = lanes(scalars[0:1], 3)
    lowest, keep, take = mixing(ritz, curvature, norm)
    for i in range(OWN):
        out[i] = keep * vector[i] + take * direction[i]
    energies[0] = first_lowest[0, 0]
    energies[1] = lowest[0, 0]


def sums_kernel(parts, out):
    out[...] = jnp.broadcast_to(jnp.sum(parts[...], axis=0, keepdims=True), out.shape)


HBM = pl.BlockSpec(memory_space=pltpu.HBM)
VMEM = pl.BlockSpec(memory_space=pltpu.VMEM)
SMEM = pl.BlockSpec(memory_space=pltpu.SMEM)
MIB = 1 << 20


def struct(*shape, dtype=f32):
    return jax.ShapeDtypeStruct(shape, dtype)


def call(kernel, name, outs, in_specs, args, out_specs=None, scratch=(), limit=6):
    return pl.pallas_call(
        kernel,
        name=name,
        in_specs=in_specs,
        out_specs=out_specs or [VMEM] * len(outs),
        out_shape=outs,
        scratch_shapes=scratch,
        compiler_params=pltpu.CompilerParams(vmem_limit_bytes=limit * MIB),
    )(*args)


def small(kernel, name, outs, *arrays, out_specs=None):
    return call(kernel, name, outs, [VMEM] * len(arrays), arrays, out_specs)


def step(kernel, name, outs, operators, arrays, sums=True):
    scratch = [
        pltpu.VMEM((WINDOW, BLOCK, BLOCK), bf16),
        pltpu.VMEM((BLOCK, PAIRS * BLOCK), bf16),
    ]
    if sums:
        scratch.append(pltpu.VMEM((WINDOW, BLOCK, BLOCK), f32))
    args = (*operators, *arrays)
    in_specs = [SMEM] + [VMEM] * (len(args) - 1)
    return call(kernel, name, outs, in_specs, args, scratch=scratch, limit=16)


def exchange(value, axes):
    return lax.all_to_all(value, axes, 0, 0, tiled=True)


def shards(guess, left_ops, right_ops, op_shift, op_mask, left_dims, right_dims):
    blocks = struct(WINDOW, BLOCK, BLOCK)
    half = struct(HALF, BLOCK, BLOCK)
    own_blocks = struct(OWN, BLOCK, BLOCK)
    pair = struct(2, CHUNK, BLOCK)
    scalar_row = struct(EXTRA, BLOCK)
    packet = struct(PLANE, CHUNK + EXTRA, BLOCK)

    def partner(value, distance):
        return lax.ppermute(value, "wf", [(i, i ^ distance) for i in range(4)])

    def swapped(value):
        return lax.ppermute(value, "c", [(0, 1), (1, 0)])

    table = (2 * op_shift[:, None] + op_mask).reshape(-1)
    tail = EXTRA + CHUNK
    start, masks, one, own, three = call(
        norm_kernel, "norm",
        [own_blocks, pair, struct(SIDE + tail, BLOCK), struct(tail, BLOCK),
         struct(SIDE + tail, BLOCK)],
        [SMEM, SMEM, VMEM], (left_dims, right_dims, guess), limit=60,
    )
    one, two, three = partner(one, 1), partner(own, 2), partner(three, 3)
    held = struct(OWN, PAIRS, BLOCK, BLOCK, dtype=bf16)
    left, right = call(
        load_kernel, "load", [held, held], [HBM, HBM], (left_ops, right_ops),
        scratch=[pltpu.SemaphoreType.DMA((2 * OWN,))], limit=58,
    )
    operators = (table, left, right)

    def reduced(keep, give):
        (summed,) = small(join_kernel, "join", [half], keep, swapped(give))
        parts = exchange(summed.reshape(PLANE, CHUNK, BLOCK), PLANE_AXES)
        (tiled,) = small(spread_kernel, "spread", [struct(4, CHUNK, BLOCK)], parts)
        return exchange(tiled, "wf")

    def gathered(packets):
        packets = exchange(packets, PLANE_AXES)
        return packets, swapped(packets)

    keep, give, vector, pieces = step(
        first_kernel, "first", [half, half, blocks, pair], operators,
        (start, own, one, two, three),
    )
    packets, image_pieces = small(
        image_kernel, "image", [packet, pair], reduced(keep, give), masks, pieces
    )
    keep, give, direction, image, scalars = step(
        second_kernel, "second", [half, half, blocks, blocks, scalar_row], operators,
        (*gathered(packets), vector),
    )
    (packets,) = small(
        turned_kernel, "turned", [packet], reduced(keep, give), masks, pieces, image_pieces, scalars
    )
    sums, vector, direction, scalars = step(
        third_kernel, "third", [struct(8, BLOCK), own_blocks, own_blocks, scalar_row], operators,
        (*gathered(packets), vector, direction, image, scalars), sums=False,
    )
    sums = exchange(sums, CROSS_AXES)
    (sums,) = small(sums_kernel, "sums", [struct(PLANE, BLOCK)], sums)
    sums = exchange(sums, PLANE_AXES)
    result, energies = small(
        last_kernel, "last", [own_blocks, struct(2)], sums, vector, direction, scalars,
        out_specs=[VMEM, SMEM],
    )
    return result, energies


def solution(mesh):
    split = Mesh(mesh.devices.reshape(4, 8, 2, 4), (*OP_AXES, "wf"))
    in_specs = (
        P("wf", None, None),
        P(OP_AXES, "wf", None, None),
        P(OP_AXES, "wf", None, None),
        P(OP_AXES),
        P(OP_AXES, "wf"),
        P(),
        P(),
    )
    out_specs = (P("wf", None, None), P())
    return jax.shard_map(
        shards, mesh=split, in_specs=in_specs, out_specs=out_specs, check_vma=False
    )
```

time: 177 us -> 153 us (0.86)
  blocking collectives: 139 us -> 102 us
  starting transfers between devices: 7.2 us -> 18.6 us
  local copies, waits for them, and re-layouts: 9.13 us -> 3.36 us
  waiting for transfers between devices: 1.11 us -> 5.03 us
  Pallas kernels: 18.8 us -> 21.1 us
    all_to_all x8, blocking collectives: 139 us -> 102 us  [exchange(): return lax.all_to_all(value, axes, 0, 0, tiled=True)]
    ppermute x0 -> x4, starting transfers between devices: none -> 14.1 us  [swapped(): return lax.ppermute(value, 'c', [(0, 1), (1, 0)])]
    unnamed x29 -> x10, local copies, waits for them, and re-layouts: 9.13 us -> 3.19 us
    ppermute x0 -> x4, waiting for transfers between devices: none -> 5.02 us  [swapped(): return lax.ppermute(value, 'c', [(0, 1), (1, 0)])]
    ppermute x5 -> x3, starting transfers between devices: 7.2 us -> 4.44 us  [partner(): return lax.ppermute(value, 'wf', [(i, i ^ distance) for i in range(4)])]
    pallas_call x10 -> x13, Pallas kernels: 18.8 us -> 21.1 us  [call(): pl.pallas_call(kernel, name=name, in_specs=in_specs, out_specs=out_specs...]
  transfers between devices with their start and end apart: 5 -> 7, of which waited for: 2 -> 4; matrix products, arithmetic and copies ran while one was open for 0% -> 1% of each run, Pallas kernels for 0% -> 3%
where the time goes in v3:
time: 153 us
  blocking collectives  102 us (67%)
  Pallas kernels  21.1 us (14%)
  starting transfers between devices  18.6 us (12%)
  waiting for transfers between devices  5.03 us (3%)
  local copies, waits for them, and re-layouts  3.36 us (2%)
    all_to_all x8, blocking collectives, exchange(): return lax.all_to_all(value, axes, 0, 0, tiled=True)  102 us
    pallas_call x13, Pallas kernels, call(): pl.pallas_call(kernel, name=name, in_specs=in_specs, out_specs=out_specs...  21.1 us
    ppermute x4, starting transfers between devices, swapped(): return lax.ppermute(value, 'c', [(0, 1), (1, 0)])  14.1 us
    ppermute x4, waiting for transfers between devices, swapped(): return lax.ppermute(value, 'c', [(0, 1), (1, 0)])  5.02 us
    ppermute x3, starting transfers between devices, partner(): return lax.ppermute(value, 'wf', [(i, i ^ distance) for i in range(4)])  4.44 us
    unnamed x10, local copies, waits for them, and re-layouts  3.19 us
  transfers between devices with their start and end apart: 7, of which 4 were waited for; matrix products, arithmetic and copies ran while one was open for 1% of the time, Pallas kernels for 3%

profile of v3, /device:TPU:1, one launch (start us, length us, event | category | flops | bytes accessed | tf_op | source)
XLA Modules:
  0.0 152.5 jit_solution(8538712528532099209)
XLA Ops:
  0.6 1.9 %norm.1 = (f32[4,128,128]{2,1,0:T(8,128)}, f32[2,16,128]{2,1,0:T(8,128)}, f32[280,128]{1,0:T(8,128)}, f32[24,128]{1,0:T(8,128)}, f32[280,128]{1,0:T(8,128)}) custom-call(s32[16]{0:T(128)} %left_dims.1, s32[16]{0:T(128)} %right_dims.1, f32[4,128,128]{2,1,0:T(8,128)} %guess.1), custom_call_target="tpu_custom_call" | custom-call | tf_op jit(solution)/shard_map/norm/pallas_call | solution.py:360
  2.5 3.6 %collective-permute-start.1 = (f32[24,128]{1,0:T(8,128)}, f32[24,128]{1,0:T(8,128)S(1)}, u32[]{:S(2)}, u32[]{:S(2)}) collective-permute-start(f32[24,128]{1,0:T(8,128)} %get-tuple-element.27.own), channel_id=1, source_target_pairs={{0,2},{1,3},{2,0},{3,1},{4,6},{5,7},{6,4},{7,5},{8,10},{9,11},{10,... | collective-permute-start | bytes 36872 | tf_op jit(solution)/shard_map/ppermute | solution.py:400
  8.5 4.2 %load.1 = (bf16[4,16,128,128]{3,2,1,0:T(8,128)(2,1)}, bf16[4,16,128,128]{3,2,1,0:T(8,128)(2,1)}) custom-call(bf16[16,4,128,128]{3,2,1,0:T(8,128)(2,1)} %left_hbm.1, bf16[16,4,128,128]{3,2,1,0:T(8,128)(2,1)} %right_hbm.1), custom_call_target="tpu_custom_call" | custom-call | tf_op jit(solution)/shard_map/load/pallas_call | solution.py:360
  12.8 1.6 %copy-done = bf16[4,16,128,128]{3,2,1,0:T(8,128)(2,1)S(1)} copy-done((bf16[4,16,128,128]{3,2,1,0:T(8,128)(2,1)S(1)}, bf16[4,16,128,128]{3,2,1,0:T(8,128)(2,1)}, u32[]{:S(2)}) %copy-start) | copy-done | bytes 2097176
  14.4 1.6 %copy-done.1 = bf16[4,16,128,128]{3,2,1,0:T(8,128)(2,1)S(1)} copy-done((bf16[4,16,128,128]{3,2,1,0:T(8,128)(2,1)S(1)}, bf16[4,16,128,128]{3,2,1,0:T(8,128)(2,1)}, u32[]{:S(2)}) %copy-start.1) | copy-done | bytes 2097176
  16.0 4.8 %first.1 = (f32[4,128,128]{2,1,0:T(8,128)S(1)}, f32[4,128,128]{2,1,0:T(8,128)S(1)}, f32[8,128,128]{2,1,0:T(8,128)S(1)}, f32[2,16,128]{2,1,0:T(8,128)S(1)}) custom-call(s32[64]{0:T(128)S(1)} %reshape.19.table, bf16[4,16,128,128]{3,2,1,0:T(8,128)(2,1)S(1)} %copy-done, bf16[4,16,128,128]{3,2,1,0:T(8,128)(2,1)S(1)} %copy-done.1, f32[4,128,128]{2,1,0:T(8,128)S(1)} %copy-done.2, ...), custom_call_target="tpu_custom_call" | custom-call | tf_op jit(solution)/shard_map/first/pallas_call | solution.py:360
  20.8 3.0 %collective-permute-start.3 = (f32[4,128,128]{2,1,0:T(8,128)S(1)}, f32[4,128,128]{2,1,0:T(8,128)S(1)}, u32[]{:S(2)}, u32[]{:S(2)}) collective-permute-start(f32[4,128,128]{2,1,0:T(8,128)S(1)} %get-tuple-element.31), channel_id=1, source_target_pairs={{0,4},{4,0},{1,5},{5,1},{2,6},{6,2},{3,7},{7,3},{8,12},{12,8},{9,1... | collective-permute-start | bytes 786440 | tf_op jit(solution)/shard_map/ppermute | solution.py:403
  23.7 1.2 collective-permute-done.3.second
  24.9 19.2 %all_to_all.52.parts = f32[32,16,128]{2,1,0:T(8,128)S(1)} all-to-all(f32[32,16,128]{2,1,0:T(8,128)S(1)} %bitcast.10), channel_id=1, replica_groups=mesh['y'=4,'z'=8,'c'=2,'wf'=4] {'y','z'}, dimensions={0} | all-to-all | bytes 524288 | tf_op jit(solution)/shard_map/all_to_all | solution.py:388
  44.1 7.9 %all_to_all.53.parts = f32[4,16,128]{2,1,0:T(8,128)S(1)} all-to-all(f32[4,16,128]{2,1,0:T(8,128)S(1)} %spread.2), channel_id=1, replica_groups=mesh['y'=4,'z'=8,'c'=2,'wf'=4] {'wf'}, dimensions={0} | all-to-all | bytes 65536 | tf_op jit(solution)/shard_map/all_to_all | solution.py:388
  52.3 16.8 %all_to_all.54.own = f32[32,24,128]{2,1,0:T(8,128)S(1)} all-to-all(f32[32,24,128]{2,1,0:T(8,128)S(1)} %get-tuple-element.34), channel_id=1, replica_groups=mesh['y'=4,'z'=8,'c'=2,'wf'=4] {'y','z'}, dimensions={0} | all-to-all | bytes 786432 | tf_op jit(solution)/shard_map/all_to_all | solution.py:388
  69.1 5.3 %collective-permute-start.4 = (f32[32,24,128]{2,1,0:T(8,128)S(1)}, f32[32,24,128]{2,1,0:T(8,128)S(1)}, u32[]{:S(2)}, u32[]{:S(2)}) collective-permute-start(f32[32,24,128]{2,1,0:T(8,128)S(1)} %all_to_all.54.own), channel_id=1, source_target_pairs={{0,4},{4,0},{1,5},{5,1},{2,6},{6,2},{3,7},{7,3},{8,12},{12,8},{9,1... | collective-permute-start | bytes 1179656 | tf_op jit(solution)/shard_map/ppermute | solution.py:403
  74.3 1.3 collective-permute-done.4.other
  75.7 5.2 %second.1 = (f32[4,128,128]{2,1,0:T(8,128)S(1)}, f32[4,128,128]{2,1,0:T(8,128)S(1)}, f32[8,128,128]{2,1,0:T(8,128)S(1)}, f32[8,128,128]{2,1,0:T(8,128)S(1)}, f32[8,128]{1,0:T(8,128)S(1)}) custom-call(s32[64]{0:T(128)S(1)} %reshape.19.table, bf16[4,16,128,128]{3,2,1,0:T(8,128)(2,1)S(1)} %copy-done, bf16[4,16,128,128]{3,2,1,0:T(8,128)(2,1)S(1)} %copy-done.1, ...), custom_call_target="tpu_custom_call" | custom-call | tf_op jit(solution)/shard_map/second/pallas_call | solution.py:360
  81.5 1.2 collective-permute-done.5.second
  82.7 14.3 %all_to_all.55.parts = f32[32,16,128]{2,1,0:T(8,128)S(1)} all-to-all(f32[32,16,128]{2,1,0:T(8,128)S(1)} %bitcast.11), channel_id=1, replica_groups=mesh['y'=4,'z'=8,'c'=2,'wf'=4] {'y','z'}, dimensions={0} | all-to-all | bytes 524288 | tf_op jit(solution)/shard_map/all_to_all | solution.py:388
  97.1 6.7 %all_to_all.56.parts = f32[4,16,128]{2,1,0:T(8,128)S(1)} all-to-all(f32[4,16,128]{2,1,0:T(8,128)S(1)} %spread.3), channel_id=1, replica_groups=mesh['y'=4,'z'=8,'c'=2,'wf'=4] {'wf'}, dimensions={0} | all-to-all | bytes 65536 | tf_op jit(solution)/shard_map/all_to_all | solution.py:388
  104.3 16.8 %all_to_all.57.gathered = f32[32,24,128]{2,1,0:T(8,128)S(1)} all-to-all(f32[32,24,128]{2,1,0:T(8,128)S(1)} %turned.1), channel_id=1, replica_groups=mesh['y'=4,'z'=8,'c'=2,'wf'=4] {'y','z'}, dimensions={0} | all-to-all | bytes 786432 | tf_op jit(solution)/shard_map/all_to_all | solution.py:388
  121.0 5.3 %collective-permute-start.6 = (f32[32,24,128]{2,1,0:T(8,128)S(1)}, f32[32,24,128]{2,1,0:T(8,128)S(1)}, u32[]{:S(2)}, u32[]{:S(2)}) collective-permute-start(f32[32,24,128]{2,1,0:T(8,128)S(1)} %all_to_all.57.gathered), channel_id=1, source_target_pairs={{0,4},{4,0},{1,5},{5,1},{2,6},{6,2},{3,7},{7,3},{8,12},{12,8},{9,1... | collective-permute-start | bytes 1179656 | tf_op jit(solution)/shard_map/ppermute | solution.py:403
  126.3 1.3 collective-permute-done.6.swapped
  127.6 3.0 %third.1 = (f32[8,128]{1,0:T(8,128)S(1)}, f32[4,128,128]{2,1,0:T(8,128)S(1)}, f32[4,128,128]{2,1,0:T(8,128)S(1)}, f32[8,128]{1,0:T(8,128)S(1)}) custom-call(s32[64]{0:T(128)S(1)} %reshape.19.table, bf16[4,16,128,128]{3,2,1,0:T(8,128)(2,1)S(1)} %copy-done, bf16[4,16,128,128]{3,2,1,0:T(8,128)(2,1)S(1)} %copy-done.1, f32[32,24,128]{2,1,0:T(8,128)S(1)} %all_to_all.57.gathered, ...), custom_call_target="tpu_custom_call" | custom-call | tf_op jit(solution)/shard_map/third/pallas_call | solution.py:360
  130.6 7.4 %all_to_all.58 = f32[8,1,128]{2,1,0:T(1,128)S(1)} all-to-all(f32[8,1,128]{2,1,0:T(1,128)S(1)} %bitcast.15), channel_id=1, replica_groups=mesh['y'=4,'z'=8,'c'=2,'wf'=4] {'c','wf'}, dimensions={0} | all-to-all | bytes 8192 | tf_op jit(solution)/shard_map/all_to_all | solution.py:388
  138.0 13.3 %all_to_all.59 = f32[32,1,128]{2,1,0:T(1,128)S(1)} all-to-all(f32[32,1,128]{2,1,0:T(1,128)S(1)} %bitcast.13), channel_id=1, replica_groups=mesh['y'=4,'z'=8,'c'=2,'wf'=4] {'y','z'}, dimensions={0} | all-to-all | bytes 32768 | tf_op jit(solution)/shard_map/all_to_all | solution.py:388
  151.3 1.1 last.1
  (25 shorter events, 4.0 us)
Async XLA Ops:
  2.5 10.2 %collective-permute-start.1 = (f32[24,128]{1,0:T(8,128)}, f32[24,128]{1,0:T(8,128)S(1)}, u32[]{:S(2)}, u32[]{:S(2)}) collective-permute-start(f32[24,128]{1,0:T(8,128)} %get-tuple-element.27.own), channel_id=1, source_target_pairs={{0,2},{1,3},{2,0},{3,1},{4,6},{5,7},{6,4},{7,5},{8,10},{9,11},{10,... | collective-permute-start | bytes 36872 | tf_op jit(solution)/shard_map/ppermute | solution.py:400
  6.1 6.7 %collective-permute-start = (f32[280,128]{1,0:T(8,128)}, f32[280,128]{1,0:T(8,128)S(1)}, u32[]{:S(2)}, u32[]{:S(2)}) collective-permute-start(f32[280,128]{1,0:T(8,128)} %get-tuple-element.28), channel_id=1, source_target_pairs={{0,1},{1,0},{2,3},{3,2},{4,5},{5,4},{6,7},{7,6},{8,9},{9,8},{10,11... | collective-permute-start | bytes 430088 | tf_op jit(solution)/shard_map/ppermute | solution.py:400
  6.4 6.3 %collective-permute-start.2 = (f32[280,128]{1,0:T(8,128)}, f32[280,128]{1,0:T(8,128)S(1)}, u32[]{:S(2)}, u32[]{:S(2)}) collective-permute-start(f32[280,128]{1,0:T(8,128)} %get-tuple-element.29), channel_id=1, source_target_pairs={{0,3},{1,2},{2,1},{3,0},{4,7},{5,6},{6,5},{7,4},{8,11},{9,10},{10,... | collective-permute-start | bytes 430088 | tf_op jit(solution)/shard_map/ppermute | solution.py:400
  8.5 4.3 %copy-start.2 = (f32[4,128,128]{2,1,0:T(8,128)S(1)}, f32[4,128,128]{2,1,0:T(8,128)}, u32[]{:S(2)}) copy-start(f32[4,128,128]{2,1,0:T(8,128)} %get-tuple-element.26.start) | copy-start | bytes 786436
  8.5 4.3 %copy-start.4 = (f32[24,128]{1,0:T(8,128)S(1)}, f32[24,128]{1,0:T(8,128)}, u32[]{:S(2)}) copy-start(f32[24,128]{1,0:T(8,128)} %get-tuple-element.27.own) | copy-start | bytes 36868
  12.8 1.6 %copy-start = (bf16[4,16,128,128]{3,2,1,0:T(8,128)(2,1)S(1)}, bf16[4,16,128,128]{3,2,1,0:T(8,128)(2,1)}, u32[]{:S(2)}) copy-start(bf16[4,16,128,128]{3,2,1,0:T(8,128)(2,1)} %get-tuple-element.24.left) | copy-start | bytes 6291460
  14.4 1.6 %copy-start.1 = (bf16[4,16,128,128]{3,2,1,0:T(8,128)(2,1)S(1)}, bf16[4,16,128,128]{3,2,1,0:T(8,128)(2,1)}, u32[]{:S(2)}) copy-start(bf16[4,16,128,128]{3,2,1,0:T(8,128)(2,1)} %get-tuple-element.25.right) | copy-start | bytes 6291460
  16.0 36.1 %copy-start.3 = (f32[2,16,128]{2,1,0:T(8,128)S(1)}, f32[2,16,128]{2,1,0:T(8,128)}, u32[]{:S(2)}) copy-start(f32[2,16,128]{2,1,0:T(8,128)} %get-tuple-element.32.masks) | copy-start | bytes 49156
  20.8 4.2 %collective-permute-start.3 = (f32[4,128,128]{2,1,0:T(8,128)S(1)}, f32[4,128,128]{2,1,0:T(8,128)S(1)}, u32[]{:S(2)}, u32[]{:S(2)}) collective-permute-start(f32[4,128,128]{2,1,0:T(8,128)S(1)} %get-tuple-element.31), channel_id=1, source_target_pairs={{0,4},{4,0},{1,5},{5,1},{2,6},{6,2},{3,7},{7,3},{8,12},{12,8},{9,1... | collective-permute-start | bytes 786440 | tf_op jit(solution)/shard_map/ppermute | solution.py:403
  69.1 6.6 %collective-permute-start.4 = (f32[32,24,128]{2,1,0:T(8,128)S(1)}, f32[32,24,128]{2,1,0:T(8,128)S(1)}, u32[]{:S(2)}, u32[]{:S(2)}) collective-permute-start(f32[32,24,128]{2,1,0:T(8,128)S(1)} %all_to_all.54.own), channel_id=1, source_target_pairs={{0,4},{4,0},{1,5},{5,1},{2,6},{6,2},{3,7},{7,3},{8,12},{12,8},{9,1... | collective-permute-start | bytes 1179656 | tf_op jit(solution)/shard_map/ppermute | solution.py:403
  80.9 1.8 %collective-permute-start.5 = (f32[4,128,128]{2,1,0:T(8,128)S(1)}, f32[4,128,128]{2,1,0:T(8,128)S(1)}, u32[]{:S(2)}, u32[]{:S(2)}) collective-permute-start(f32[4,128,128]{2,1,0:T(8,128)S(1)} %get-tuple-element.37), channel_id=1, source_target_pairs={{0,4},{4,0},{1,5},{5,1},{2,6},{6,2},{3,7},{7,3},{8,12},{12,8},{9,1... | collective-permute-start | bytes 786440 | tf_op jit(solution)/shard_map/ppermute | solution.py:403
  121.0 6.6 %collective-permute-start.6 = (f32[32,24,128]{2,1,0:T(8,128)S(1)}, f32[32,24,128]{2,1,0:T(8,128)S(1)}, u32[]{:S(2)}, u32[]{:S(2)}) collective-permute-start(f32[32,24,128]{2,1,0:T(8,128)S(1)} %all_to_all.57.gathered), channel_id=1, source_target_pairs={{0,4},{4,0},{1,5},{5,1},{2,6},{6,2},{3,7},{7,3},{8,12},{12,8},{9,1... | collective-permute-start | bytes 1179656 | tf_op jit(solution)/shard_map/ppermute | solution.py:403

commit v4 on v3

--- a/solution.py
+++ b/solution.py
@@ -11,14 +11,15 @@
 PAIRS = 16
 OWN = 4
 WINDOW = 8
-PLANE = 32
+LINE = 8
+CROSS = 16
 HALF = 4
-CHUNK = 16
+ROWS = 16
+CHUNK = HALF * ROWS
 SIDE = 2 * BLOCK
 EXTRA = 8
 ENTRIES = float(SECTORS * BLOCK * BLOCK)
-PLANE_AXES = ("y", "z")
-CROSS_AXES = ("c", "wf")
+CROSS_AXES = ("y", "wf")
 OP_AXES = ("y", "z", "c")
 
 f32 = jnp.float32
@@ -40,9 +41,8 @@
 
 
 def place_here():
-    chunk = lax.axis_index("y") * lax.axis_size("z") + lax.axis_index("z")
-    first_row = pl.multiple_of((chunk & 7) * CHUNK, CHUNK)
-    return lax.axis_index("wf"), HALF * lax.axis_index("c") + chunk // 8, first_row
+    first_row = pl.multiple_of(lax.axis_index("z") * ROWS, ROWS)
+    return lax.axis_index("wf"), HALF * lax.axis_index("c"), first_row
 
 
 def sector_at(wf, position):
@@ -86,7 +86,7 @@
 
 
 def norm_kernel(left_dims, right_dims, guess, start, masks, one, two, three):
-    wf, position, first_row = place_here()
+    wf, base, first_row = place_here()
     sums = jnp.zeros((1, 1), f32)
     for i in range(OWN):
         mask = live(left_dims, right_dims, OWN * wf + i, 0, BLOCK)
@@ -99,10 +99,11 @@
         three[i * BLOCK : (i + 1) * BLOCK] = start[2 * odd + i]
     for out, first in ((one, SIDE), (two, 0), (three, SIDE)):
         out[first : first + EXTRA] = jnp.broadcast_to(sums, (EXTRA, BLOCK))
-        out[first + EXTRA :] = start[position & 3, pl.ds(first_row, CHUNK)]
+        out[first + EXTRA :] = start[:, pl.ds(first_row, ROWS)].reshape(CHUNK, BLOCK)
     for i in range(2):
-        mask = live(left_dims, right_dims, position + 8 * i, first_row, CHUNK)
-        masks[i] = jnp.where(mask, 1.0, 0.0)
+        for k in range(HALF):
+            mask = live(left_dims, right_dims, base + k + 8 * i, first_row, ROWS)
+            masks[i, k * ROWS : (k + 1) * ROWS] = jnp.where(mask, 1.0, 0.0)
 
 
 def half_step(table, left, right, vec_half, back, sector, index):
@@ -132,9 +133,9 @@
     for i in range(OWN):
         full_step(table, left, right, vec_half, back, sums, first_sector + i, i)
     core = lax.axis_index("c")
-    for i in range(HALF):
-        keep[i] = sums[HALF * core + i]
-        give[i] = sums[HALF - HALF * core + i]
+    for out, first in ((keep, HALF * core), (give, HALF - HALF * core)):
+        for i in range(HALF):
+            out[:, i * ROWS : (i + 1) * ROWS] = sums[first + i].reshape(LINE, ROWS, BLOCK)
 
 
 def first_kernel(
@@ -182,24 +183,35 @@
 
 
 def combined(masks, parts):
-    _, position, _ = place_here()
+    base = HALF * lax.axis_index("c")
+    sums = []
+    for other in range(4):
+        rows = parts[other] + parts[4 + other] + (parts[8 + other] + parts[12 + other])
+        sums.append(rows.reshape(HALF, ROWS, BLOCK))
     values = []
     for place in range(2):
-        value = jnp.zeros((CHUNK, BLOCK), f32)
-        for other in range(4):
-            here = sector_at(other, position) == position + 8 * place
-            value = value + jnp.where(here, parts[other], 0.0)
-        values.append(value * masks[place])
+        blocks = []
+        for k in range(HALF):
+            value = jnp.zeros((ROWS, BLOCK), f32)
+            for other in range(4):
+                here = sector_at(other, base + k) == base + k + 8 * place
+                value = value + jnp.where(here, sums[other][k], 0.0)
+            blocks.append(value)
+        values.append(jnp.concatenate(blocks, axis=0) * masks[place])
     return values
 
 
 def send(values, sums, out):
-    wf, position, _ = place_here()
-    sector = sector_at(wf, position)
-    chosen = jnp.where(sector == position, values[0], 0.0)
-    chosen = jnp.where(sector == position + 8, values[1], chosen)
+    wf, base, _ = place_here()
+    chosen = []
+    for k in range(HALF):
+        sector = sector_at(wf, base + k)
+        rows = slice(k * ROWS, (k + 1) * ROWS)
+        block = jnp.where(sector == base + k, values[0][rows], 0.0)
+        chosen.append(jnp.where(sector == base + k + 8, values[1][rows], block))
+    chosen = jnp.concatenate(chosen, axis=0)
     packed = pack(sums)
-    for target in range(PLANE):
+    for target in range(LINE):
         out[target, 0:CHUNK] = chosen
         out[target, CHUNK:] = packed
 
@@ -228,8 +240,8 @@
 
 
 def held_block(cores, position):
-    rows = slice(8 * (position % HALF), 8 * (position % HALF) + 8)
-    own, other = (held[rows, 0:CHUNK, :].reshape(BLOCK, BLOCK) for held in cores)
+    rows = slice(ROWS * (position % HALF), ROWS * (position % HALF) + ROWS)
+    own, other = (held[:, rows, :].reshape(BLOCK, BLOCK) for held in cores)
     return jnp.where(lax.axis_index("c") == position // HALF, own, other)
 
 
@@ -333,17 +345,13 @@
 
 
 def last_kernel(parts, vector, direction, scalars, out, energies):
-    curvature = total(parts[...])[0:1] / (BLOCK * ENTRIES)
+    curvature = total(parts[:, 0:1]) / ENTRIES
     ritz, norm, first_lowest = lanes(scalars[0:1], 3)
     lowest, keep, take = mixing(ritz, curvature, norm)
     for i in range(OWN):
         out[i] = keep * vector[i] + take * direction[i]
     energies[0] = first_lowest[0, 0]
     energies[1] = lowest[0, 0]
-
-
-def sums_kernel(parts, out):
-    out[...] = jnp.broadcast_to(jnp.sum(parts[...], axis=0, keepdims=True), out.shape)
 
 
 HBM = pl.BlockSpec(memory_space=pltpu.HBM)
@@ -364,7 +372,7 @@
         out_specs=out_specs or [VMEM] * len(outs),
         out_shape=outs,
         scratch_shapes=scratch,
-        compiler_params=pltpu.CompilerParams(vmem_limit_bytes=limit * MIB),
+        compiler_params=pltpu.CompilerParams(vmem_limit_bytes=int(limit * MIB)),
     )(*args)
 
 
@@ -390,11 +398,11 @@
 
 def shards(guess, left_ops, right_ops, op_shift, op_mask, left_dims, right_dims):
     blocks = struct(WINDOW, BLOCK, BLOCK)
-    half = struct(HALF, BLOCK, BLOCK)
+    half = struct(LINE, CHUNK, BLOCK)
     own_blocks = struct(OWN, BLOCK, BLOCK)
     pair = struct(2, CHUNK, BLOCK)
     scalar_row = struct(EXTRA, BLOCK)
-    packet = struct(PLANE, CHUNK + EXTRA, BLOCK)
+    packet = struct(LINE, CHUNK + EXTRA, BLOCK)
 
     def partner(value, distance):
         return lax.ppermute(value, "wf", [(i, i ^ distance) for i in range(4)])
@@ -414,18 +422,18 @@
     held = struct(OWN, PAIRS, BLOCK, BLOCK, dtype=bf16)
     left, right = call(
         load_kernel, "load", [held, held], [HBM, HBM], (left_ops, right_ops),
-        scratch=[pltpu.SemaphoreType.DMA((2 * OWN,))], limit=58,
+        scratch=[pltpu.SemaphoreType.DMA((2 * OWN,))], limit=55.5,
     )
     operators = (table, left, right)
 
     def reduced(keep, give):
         (summed,) = small(join_kernel, "join", [half], keep, swapped(give))
-        parts = exchange(summed.reshape(PLANE, CHUNK, BLOCK), PLANE_AXES)
-        (tiled,) = small(spread_kernel, "spread", [struct(4, CHUNK, BLOCK)], parts)
-        return exchange(tiled, "wf")
+        parts = exchange(summed, "z")
+        (tiled,) = small(spread_kernel, "spread", [struct(CROSS, CHUNK, BLOCK)], parts)
+        return exchange(tiled, CROSS_AXES)
 
     def gathered(packets):
-        packets = exchange(packets, PLANE_AXES)
+        packets = exchange(packets, "z")
         return packets, swapped(packets)
 
     keep, give, vector, pieces = step(
@@ -443,12 +451,10 @@
         turned_kernel, "turned", [packet], reduced(keep, give), masks, pieces, image_pieces, scalars
     )
     sums, vector, direction, scalars = step(
-        third_kernel, "third", [struct(8, BLOCK), own_blocks, own_blocks, scalar_row], operators,
+        third_kernel, "third", [struct(256, BLOCK), own_blocks, own_blocks, scalar_row], operators,
         (*gathered(packets), vector, direction, image, scalars), sums=False,
     )
-    sums = exchange(sums, CROSS_AXES)
-    (sums,) = small(sums_kernel, "sums", [struct(PLANE, BLOCK)], sums)
-    sums = exchange(sums, PLANE_AXES)
+    sums = exchange(sums, (*OP_AXES, "wf"))
     result, energies = small(
         last_kernel, "last", [own_blocks, struct(2)], sums, vector, direction, scalars,
         out_specs=[VMEM, SMEM],

time: 153 us -> 152 us (level)
  starting transfers between devices: 18.6 us -> 15.1 us
  blocking collectives: 102 us -> 104 us
    ppermute x4, starting transfers between devices: 14.1 us -> 10.7 us  [swapped(): return lax.ppermute(value, 'c', [(0, 1), (1, 0)])]
    all_to_all x8 -> x7, blocking collectives: 102 us -> 104 us  [exchange(): return lax.all_to_all(value, axes, 0, 0, tiled=True)]
    pallas_call x13 -> x12, Pallas kernels: 21.1 us -> 21.2 us  [call(): pl.pallas_call(kernel, name=name, in_specs=in_specs, out_specs=out_specs...]
  transfers between devices with their start and end apart: 7 -> 7, of which waited for: 4 -> 5; matrix products, arithmetic and copies ran while one was open for 1% -> 1% of each run, Pallas kernels for 3% -> 3%
where the time goes in v4:
time: 152 us; the launch traced here: 151 us
  blocking collectives  104 us (68%)
  Pallas kernels  21.2 us (14%)
  starting transfers between devices  15.1 us (10%)
  waiting for transfers between devices  5.15 us (3%)
  local copies, waits for them, and re-layouts  3.37 us (2%)
    all_to_all x7, blocking collectives, exchange(): return lax.all_to_all(value, axes, 0, 0, tiled=True)  104 us
    pallas_call x12, Pallas kernels, call(): pl.pallas_call(kernel, name=name, in_specs=in_specs, out_specs=out_specs...  21.2 us
    ppermute x4, starting transfers between devices, swapped(): return lax.ppermute(value, 'c', [(0, 1), (1, 0)])  10.7 us
    ppermute x4, waiting for transfers between devices, swapped(): return lax.ppermute(value, 'c', [(0, 1), (1, 0)])  4.74 us
    ppermute x3, starting transfers between devices, partner(): return lax.ppermute(value, 'wf', [(i, i ^ distance) for i in range(4)])  4.44 us
    unnamed x10, local copies, waits for them, and re-layouts  3.2 us
  transfers between devices with their start and end apart: 7, of which 5 were waited for; matrix products, arithmetic and copies ran while one was open for 1% of the time, Pallas kernels for 3%

profile of v4, /device:TPU:1, one launch (start us, length us, event | category | flops | bytes accessed | tf_op | source)
XLA Modules:
  0.0 151.3 jit_solution(16835635970097048095)
XLA Ops:
  0.6 1.9 %norm.1 = (f32[4,128,128]{2,1,0:T(8,128)}, f32[2,64,128]{2,1,0:T(8,128)}, f32[328,128]{1,0:T(8,128)}, f32[72,128]{1,0:T(8,128)}, f32[328,128]{1,0:T(8,128)}) custom-call(s32[16]{0:T(128)} %left_dims.1, s32[16]{0:T(128)} %right_dims.1, f32[4,128,128]{2,1,0:T(8,128)} %guess.1), custom_call_target="tpu_custom_call" | custom-call | tf_op jit(solution)/shard_map/norm/pallas_call | solution.py:368
  2.6 3.6 %collective-permute-start.1 = (f32[72,128]{1,0:T(8,128)}, f32[72,128]{1,0:T(8,128)S(1)}, u32[]{:S(2)}, u32[]{:S(2)}) collective-permute-start(f32[72,128]{1,0:T(8,128)} %get-tuple-element.27.own), channel_id=1, source_target_pairs={{0,2},{1,3},{2,0},{3,1},{4,6},{5,7},{6,4},{7,5},{8,10},{9,11},{10,... | collective-permute-start | bytes 110600 | tf_op jit(solution)/shard_map/ppermute | solution.py:408
  7.6 0.7 broadcast_add_fusion
  8.5 4.2 %load.1 = (bf16[4,16,128,128]{3,2,1,0:T(8,128)(2,1)}, bf16[4,16,128,128]{3,2,1,0:T(8,128)(2,1)}) custom-call(bf16[16,4,128,128]{3,2,1,0:T(8,128)(2,1)} %left_hbm.1, bf16[16,4,128,128]{3,2,1,0:T(8,128)(2,1)} %right_hbm.1), custom_call_target="tpu_custom_call" | custom-call | tf_op jit(solution)/shard_map/load/pallas_call | solution.py:368
  13.2 1.6 %copy-done = bf16[4,16,128,128]{3,2,1,0:T(8,128)(2,1)S(1)} copy-done((bf16[4,16,128,128]{3,2,1,0:T(8,128)(2,1)S(1)}, bf16[4,16,128,128]{3,2,1,0:T(8,128)(2,1)}, u32[]{:S(2)}) %copy-start) | copy-done | bytes 2097176
  14.8 1.6 %copy-done.1 = bf16[4,16,128,128]{3,2,1,0:T(8,128)(2,1)S(1)} copy-done((bf16[4,16,128,128]{3,2,1,0:T(8,128)(2,1)S(1)}, bf16[4,16,128,128]{3,2,1,0:T(8,128)(2,1)}, u32[]{:S(2)}) %copy-start.1) | copy-done | bytes 2097176
  16.4 4.8 %first.1 = (f32[8,64,128]{2,1,0:T(8,128)S(1)}, f32[8,64,128]{2,1,0:T(8,128)S(1)}, f32[8,128,128]{2,1,0:T(8,128)S(1)}, f32[2,64,128]{2,1,0:T(8,128)S(1)}) custom-call(s32[64]{0:T(128)S(1)} %reshape.11.table, bf16[4,16,128,128]{3,2,1,0:T(8,128)(2,1)S(1)} %copy-done, bf16[4,16,128,128]{3,2,1,0:T(8,128)(2,1)S(1)} %copy-done.1, f32[4,128,128]{2,1,0:T(8,128)S(1)} %copy-done.2, ...), custom_call_target="tpu_custom_call" | custom-call | tf_op jit(solution)/shard_map/first/pallas_call | solution.py:368
  21.2 2.6 %collective-permute-start.3 = (f32[8,64,128]{2,1,0:T(8,128)S(1)}, f32[8,64,128]{2,1,0:T(8,128)S(1)}, u32[]{:S(2)}, u32[]{:S(2)}) collective-permute-start(f32[8,64,128]{2,1,0:T(8,128)S(1)} %get-tuple-element.31), channel_id=1, source_target_pairs={{0,4},{4,0},{1,5},{5,1},{2,6},{6,2},{3,7},{7,3},{8,12},{12,8},{9,1... | collective-permute-start | bytes 786440 | tf_op jit(solution)/shard_map/ppermute | solution.py:411
  23.8 1.2 collective-permute-done.3.second
  25.0 17.9 %all_to_all.41.parts = f32[8,64,128]{2,1,0:T(8,128)S(1)} all-to-all(f32[8,64,128]{2,1,0:T(8,128)S(1)} %join.2), channel_id=1, replica_groups=mesh['y'=4,'z'=8,'c'=2,'wf'=4] {'z'}, dimensions={0} | all-to-all | bytes 524288 | tf_op jit(solution)/shard_map/all_to_all | solution.py:396
  43.0 15.6 %all_to_all.42.parts = f32[16,64,128]{2,1,0:T(8,128)S(1)} all-to-all(f32[16,64,128]{2,1,0:T(8,128)S(1)} %spread.2), channel_id=1, replica_groups=mesh['y'=4,'z'=8,'c'=2,'wf'=4] {'y','wf'}, dimensions={0} | all-to-all | bytes 1048576 | tf_op jit(solution)/shard_map/all_to_all | solution.py:396
  58.9 12.1 %all_to_all.43.own = f32[8,72,128]{2,1,0:T(8,128)S(1)} all-to-all(f32[8,72,128]{2,1,0:T(8,128)S(1)} %get-tuple-element.34), channel_id=1, replica_groups=mesh['y'=4,'z'=8,'c'=2,'wf'=4] {'z'}, dimensions={0} | all-to-all | bytes 589824 | tf_op jit(solution)/shard_map/all_to_all | solution.py:396
  71.0 4.0 %collective-permute-start.4 = (f32[8,72,128]{2,1,0:T(8,128)S(1)}, f32[8,72,128]{2,1,0:T(8,128)S(1)}, u32[]{:S(2)}, u32[]{:S(2)}) collective-permute-start(f32[8,72,128]{2,1,0:T(8,128)S(1)} %all_to_all.43.own), channel_id=1, source_target_pairs={{0,4},{4,0},{1,5},{5,1},{2,6},{6,2},{3,7},{7,3},{8,12},{12,8},{9,1... | collective-permute-start | bytes 884744 | tf_op jit(solution)/shard_map/ppermute | solution.py:411
  75.0 1.2 collective-permute-done.4.other
  76.2 5.2 %second.1 = (f32[8,64,128]{2,1,0:T(8,128)S(1)}, f32[8,64,128]{2,1,0:T(8,128)S(1)}, f32[8,128,128]{2,1,0:T(8,128)S(1)}, f32[8,128,128]{2,1,0:T(8,128)S(1)}, f32[8,128]{1,0:T(8,128)S(1)}) custom-call(s32[64]{0:T(128)S(1)} %reshape.11.table, bf16[4,16,128,128]{3,2,1,0:T(8,128)(2,1)S(1)} %copy-done, bf16[4,16,128,128]{3,2,1,0:T(8,128)(2,1)S(1)} %copy-done.1, ...), custom_call_target="tpu_custom_call" | custom-call | tf_op jit(solution)/shard_map/second/pallas_call | solution.py:368
  81.8 1.2 collective-permute-done.5.second
  83.0 14.9 %all_to_all.44.parts = f32[8,64,128]{2,1,0:T(8,128)S(1)} all-to-all(f32[8,64,128]{2,1,0:T(8,128)S(1)} %join.3), channel_id=1, replica_groups=mesh['y'=4,'z'=8,'c'=2,'wf'=4] {'z'}, dimensions={0} | all-to-all | bytes 524288 | tf_op jit(solution)/shard_map/all_to_all | solution.py:396
  98.0 13.4 %all_to_all.45.parts = f32[16,64,128]{2,1,0:T(8,128)S(1)} all-to-all(f32[16,64,128]{2,1,0:T(8,128)S(1)} %spread.3), channel_id=1, replica_groups=mesh['y'=4,'z'=8,'c'=2,'wf'=4] {'y','wf'}, dimensions={0} | all-to-all | bytes 1048576 | tf_op jit(solution)/shard_map/all_to_all | solution.py:396
  111.9 12.3 %all_to_all.46.gathered = f32[8,72,128]{2,1,0:T(8,128)S(1)} all-to-all(f32[8,72,128]{2,1,0:T(8,128)S(1)} %turned.1), channel_id=1, replica_groups=mesh['y'=4,'z'=8,'c'=2,'wf'=4] {'z'}, dimensions={0} | all-to-all | bytes 589824 | tf_op jit(solution)/shard_map/all_to_all | solution.py:396
  124.2 3.6 %collective-permute-start.6 = (f32[8,72,128]{2,1,0:T(8,128)S(1)}, f32[8,72,128]{2,1,0:T(8,128)S(1)}, u32[]{:S(2)}, u32[]{:S(2)}) collective-permute-start(f32[8,72,128]{2,1,0:T(8,128)S(1)} %all_to_all.46.gathered), channel_id=1, source_target_pairs={{0,4},{4,0},{1,5},{5,1},{2,6},{6,2},{3,7},{7,3},{8,12},{12,8},{9,1... | collective-permute-start | bytes 884744 | tf_op jit(solution)/shard_map/ppermute | solution.py:411
  127.8 1.2 collective-permute-done.6.swapped
  129.0 3.0 %third.1 = (f32[256,128]{1,0:T(8,128)S(1)}, f32[4,128,128]{2,1,0:T(8,128)S(1)}, f32[4,128,128]{2,1,0:T(8,128)S(1)}, f32[8,128]{1,0:T(8,128)S(1)}) custom-call(s32[64]{0:T(128)S(1)} %reshape.11.table, bf16[4,16,128,128]{3,2,1,0:T(8,128)(2,1)S(1)} %copy-done, bf16[4,16,128,128]{3,2,1,0:T(8,128)(2,1)S(1)} %copy-done.1, f32[8,72,128]{2,1,0:T(8,128)S(1)} %all_to_all.46.gathered, ...), custom_call_target="tpu_custom_call" | custom-call | tf_op jit(solution)/shard_map/third/pallas_call | solution.py:368
  132.1 18.0 %all_to_all.47 = f32[256,1,128]{2,1,0:T(1,128)S(1)} all-to-all(f32[256,1,128]{2,1,0:T(1,128)S(1)} %bitcast.5), channel_id=1, replica_groups=mesh['y'=4,'z'=8,'c'=2,'wf'=4] {'y','z','c','wf'}, dimensions={0} | all-to-all | bytes 262144 | tf_op jit(solution)/shard_map/all_to_all | solution.py:396
  150.0 1.1 last.1
  (23 shorter events, 3.6 us)
Async XLA Ops:
  2.6 10.2 %collective-permute-start.1 = (f32[72,128]{1,0:T(8,128)}, f32[72,128]{1,0:T(8,128)S(1)}, u32[]{:S(2)}, u32[]{:S(2)}) collective-permute-start(f32[72,128]{1,0:T(8,128)} %get-tuple-element.27.own), channel_id=1, source_target_pairs={{0,2},{1,3},{2,0},{3,1},{4,6},{5,7},{6,4},{7,5},{8,10},{9,11},{10,... | collective-permute-start | bytes 110600 | tf_op jit(solution)/shard_map/ppermute | solution.py:408
  6.1 6.7 %collective-permute-start = (f32[328,128]{1,0:T(8,128)}, f32[328,128]{1,0:T(8,128)S(1)}, u32[]{:S(2)}, u32[]{:S(2)}) collective-permute-start(f32[328,128]{1,0:T(8,128)} %get-tuple-element.28), channel_id=1, source_target_pairs={{0,1},{1,0},{2,3},{3,2},{4,5},{5,4},{6,7},{7,6},{8,9},{9,8},{10,11... | collective-permute-start | bytes 503816 | tf_op jit(solution)/shard_map/ppermute | solution.py:408
  6.4 6.8 %collective-permute-start.2 = (f32[328,128]{1,0:T(8,128)}, f32[328,128]{1,0:T(8,128)S(1)}, u32[]{:S(2)}, u32[]{:S(2)}) collective-permute-start(f32[328,128]{1,0:T(8,128)} %get-tuple-element.29), channel_id=1, source_target_pairs={{0,3},{1,2},{2,1},{3,0},{4,7},{5,6},{6,5},{7,4},{8,11},{9,10},{10,... | collective-permute-start | bytes 503816 | tf_op jit(solution)/shard_map/ppermute | solution.py:408
  8.5 4.7 %copy-start.2 = (f32[4,128,128]{2,1,0:T(8,128)S(1)}, f32[4,128,128]{2,1,0:T(8,128)}, u32[]{:S(2)}) copy-start(f32[4,128,128]{2,1,0:T(8,128)} %get-tuple-element.26.start) | copy-start | bytes 786436
  8.5 4.7 %copy-start.4 = (f32[72,128]{1,0:T(8,128)S(1)}, f32[72,128]{1,0:T(8,128)}, u32[]{:S(2)}) copy-start(f32[72,128]{1,0:T(8,128)} %get-tuple-element.27.own) | copy-start | bytes 110596
  13.2 1.6 %copy-start = (bf16[4,16,128,128]{3,2,1,0:T(8,128)(2,1)S(1)}, bf16[4,16,128,128]{3,2,1,0:T(8,128)(2,1)}, u32[]{:S(2)}) copy-start(bf16[4,16,128,128]{3,2,1,0:T(8,128)(2,1)} %get-tuple-element.24.left) | copy-start | bytes 6291460
  14.8 1.6 %copy-start.1 = (bf16[4,16,128,128]{3,2,1,0:T(8,128)(2,1)S(1)}, bf16[4,16,128,128]{3,2,1,0:T(8,128)(2,1)}, u32[]{:S(2)}) copy-start(bf16[4,16,128,128]{3,2,1,0:T(8,128)(2,1)} %get-tuple-element.25.right) | copy-start | bytes 6291460
  21.2 37.4 %copy-start.3 = (f32[2,64,128]{2,1,0:T(8,128)S(1)}, f32[2,64,128]{2,1,0:T(8,128)}, u32[]{:S(2)}) copy-start(f32[2,64,128]{2,1,0:T(8,128)} %get-tuple-element.32.masks) | copy-start | bytes 196612
  21.2 3.8 %collective-permute-start.3 = (f32[8,64,128]{2,1,0:T(8,128)S(1)}, f32[8,64,128]{2,1,0:T(8,128)S(1)}, u32[]{:S(2)}, u32[]{:S(2)}) collective-permute-start(f32[8,64,128]{2,1,0:T(8,128)S(1)} %get-tuple-element.31), channel_id=1, source_target_pairs={{0,4},{4,0},{1,5},{5,1},{2,6},{6,2},{3,7},{7,3},{8,12},{12,8},{9,1... | collective-permute-start | bytes 786440 | tf_op jit(solution)/shard_map/ppermute | solution.py:411
  71.0 5.2 %collective-permute-start.4 = (f32[8,72,128]{2,1,0:T(8,128)S(1)}, f32[8,72,128]{2,1,0:T(8,128)S(1)}, u32[]{:S(2)}, u32[]{:S(2)}) collective-permute-start(f32[8,72,128]{2,1,0:T(8,128)S(1)} %all_to_all.43.own), channel_id=1, source_target_pairs={{0,4},{4,0},{1,5},{5,1},{2,6},{6,2},{3,7},{7,3},{8,12},{12,8},{9,1... | collective-permute-start | bytes 884744 | tf_op jit(solution)/shard_map/ppermute | solution.py:411
  81.4 1.6 %collective-permute-start.5 = (f32[8,64,128]{2,1,0:T(8,128)S(1)}, f32[8,64,128]{2,1,0:T(8,128)S(1)}, u32[]{:S(2)}, u32[]{:S(2)}) collective-permute-start(f32[8,64,128]{2,1,0:T(8,128)S(1)} %get-tuple-element.37), channel_id=1, source_target_pairs={{0,4},{4,0},{1,5},{5,1},{2,6},{6,2},{3,7},{7,3},{8,12},{12,8},{9,1... | collective-permute-start | bytes 786440 | tf_op jit(solution)/shard_map/ppermute | solution.py:411
  124.2 4.8 %collective-permute-start.6 = (f32[8,72,128]{2,1,0:T(8,128)S(1)}, f32[8,72,128]{2,1,0:T(8,128)S(1)}, u32[]{:S(2)}, u32[]{:S(2)}) collective-permute-start(f32[8,72,128]{2,1,0:T(8,128)S(1)} %all_to_all.46.gathered), channel_id=1, source_target_pairs={{0,4},{4,0},{1,5},{5,1},{2,6},{6,2},{3,7},{7,3},{8,12},{12,8},{9,1... | collective-permute-start | bytes 884744 | tf_op jit(solution)/shard_map/ppermute | solution.py:411

commit v5 on v4

--- a/solution.py
+++ b/solution.py
@@ -11,16 +11,17 @@
 PAIRS = 16
 OWN = 4
 WINDOW = 8
-LINE = 8
-CROSS = 16
+LINE = 16
+CROSS = 8
 HALF = 4
-ROWS = 16
+ROWS = 8
 CHUNK = HALF * ROWS
 SIDE = 2 * BLOCK
 EXTRA = 8
 ENTRIES = float(SECTORS * BLOCK * BLOCK)
-CROSS_AXES = ("y", "wf")
-OP_AXES = ("y", "z", "c")
+LINE_AXES = ("y_far", "z")
+CROSS_AXES = ("y_near", "wf")
+OP_AXES = ("y_far", "y_near", "z", "c")
 
 f32 = jnp.float32
 bf16 = jnp.bfloat16
@@ -41,7 +42,8 @@
 
 
 def place_here():
-    first_row = pl.multiple_of(lax.axis_index("z") * ROWS, ROWS)
+    chunk = lax.axis_index("y_far") * lax.axis_size("z") + lax.axis_index("z")
+    first_row = pl.multiple_of(chunk * ROWS, ROWS)
     return lax.axis_index("wf"), HALF * lax.axis_index("c"), first_row
 
 
@@ -186,8 +188,7 @@
     base = HALF * lax.axis_index("c")
     sums = []
     for other in range(4):
-        rows = parts[other] + parts[4 + other] + (parts[8 + other] + parts[12 + other])
-        sums.append(rows.reshape(HALF, ROWS, BLOCK))
+        sums.append((parts[other] + parts[4 + other]).reshape(HALF, ROWS, BLOCK))
     values = []
     for place in range(2):
         blocks = []
@@ -422,18 +423,18 @@
     held = struct(OWN, PAIRS, BLOCK, BLOCK, dtype=bf16)
     left, right = call(
         load_kernel, "load", [held, held], [HBM, HBM], (left_ops, right_ops),
-        scratch=[pltpu.SemaphoreType.DMA((2 * OWN,))], limit=55.5,
+        scratch=[pltpu.SemaphoreType.DMA((2 * OWN,))], limit=49,
     )
     operators = (table, left, right)
 
     def reduced(keep, give):
         (summed,) = small(join_kernel, "join", [half], keep, swapped(give))
-        parts = exchange(summed, "z")
+        parts = exchange(summed, LINE_AXES)
         (tiled,) = small(spread_kernel, "spread", [struct(CROSS, CHUNK, BLOCK)], parts)
         return exchange(tiled, CROSS_AXES)
 
     def gathered(packets):
-        packets = exchange(packets, "z")
+        packets = exchange(packets, LINE_AXES)
         return packets, swapped(packets)
 
     keep, give, vector, pieces = step(
@@ -463,7 +464,7 @@
 
 
 def solution(mesh):
-    split = Mesh(mesh.devices.reshape(4, 8, 2, 4), (*OP_AXES, "wf"))
+    split = Mesh(mesh.devices.reshape(2, 2, 8, 2, 4), (*OP_AXES, "wf"))
     in_specs = (
         P("wf", None, None),
         P(OP_AXES, "wf", None, None),

time: 152 us -> 144 us (0.947)
  blocking collectives: 104 us -> 99.9 us
  local copies, waits for them, and re-layouts: 3.37 us -> 0.19 us
  Pallas kernels: 21.2 us -> 19.1 us
    all_to_all x7, blocking collectives: 104 us -> 99.9 us  [exchange(): return lax.all_to_all(value, axes, 0, 0, tiled=True)]
    unnamed x10 -> x6, local copies, waits for them, and re-layouts: 3.2 us -> 0.01 us
    pallas_call x12, Pallas kernels: 21.2 us -> 19.1 us  [call(): pl.pallas_call(kernel, name=name, in_specs=in_specs, out_specs=out_specs...]
  transfers between devices with their start and end apart: 7 -> 7, of which waited for: 5 -> 6; matrix products, arithmetic and copies ran while one was open for 1% -> 1% of each run, Pallas kernels for 3% -> 2%
where the time goes in v5:
time: 144 us
  blocking collectives  99.9 us (69%)
  Pallas kernels  19.1 us (13%)
  starting transfers between devices  15.6 us (11%)
  waiting for transfers between devices  6.52 us (5%)
    all_to_all x7, blocking collectives, exchange(): return lax.all_to_all(value, axes, 0, 0, tiled=True)  99.9 us
    pallas_call x12, Pallas kernels, call(): pl.pallas_call(kernel, name=name, in_specs=in_specs, out_specs=out_specs...  19.1 us
    ppermute x4, starting transfers between devices, swapped(): return lax.ppermute(value, 'c', [(0, 1), (1, 0)])  11.1 us
    ppermute x4, waiting for transfers between devices, swapped(): return lax.ppermute(value, 'c', [(0, 1), (1, 0)])  4.84 us
    ppermute x3, starting transfers between devices, partner(): return lax.ppermute(value, 'wf', [(i, i ^ distance) for i in range(4)])  4.44 us
  transfers between devices with their start and end apart: 7, of which 6 were waited for; matrix products, arithmetic and copies ran while one was open for 1% of the time, Pallas kernels for 2%

profile of v5, /device:TPU:1, one launch (start us, length us, event | category | flops | bytes accessed | tf_op | source)
XLA Modules:
  0.0 143.5 jit_solution(16586481390058534528)
XLA Ops:
  0.6 1.9 %norm.1 = (f32[4,128,128]{2,1,0:T(8,128)}, f32[2,32,128]{2,1,0:T(8,128)}, f32[296,128]{1,0:T(8,128)}, f32[40,128]{1,0:T(8,128)}, f32[296,128]{1,0:T(8,128)}) custom-call(s32[16]{0:T(128)} %left_dims.1, s32[16]{0:T(128)} %right_dims.1, f32[4,128,128]{2,1,0:T(8,128)} %guess.1), custom_call_target="tpu_custom_call" | custom-call | tf_op jit(solution)/shard_map/norm/pallas_call | solution.py:369
  2.5 3.6 %collective-permute-start.1 = (f32[40,128]{1,0:T(8,128)}, f32[40,128]{1,0:T(8,128)S(1)}, u32[]{:S(2)}, u32[]{:S(2)}) collective-permute-start(f32[40,128]{1,0:T(8,128)} %get-tuple-element.27.own), channel_id=1, source_target_pairs={{0,2},{1,3},{2,0},{3,1},{4,6},{5,7},{6,4},{7,5},{8,10},{9,11},{10,... | collective-permute-start | bytes 61448 | tf_op jit(solution)/shard_map/ppermute | solution.py:409
  6.9 0.7 broadcast_multiply_fusion
  7.6 0.7 broadcast_add_fusion
  8.5 2.3 %load.1 = (bf16[4,16,128,128]{3,2,1,0:T(8,128)(2,1)S(1)}, bf16[4,16,128,128]{3,2,1,0:T(8,128)(2,1)S(1)}) custom-call(bf16[16,4,128,128]{3,2,1,0:T(8,128)(2,1)} %left_hbm.1, bf16[16,4,128,128]{3,2,1,0:T(8,128)(2,1)} %right_hbm.1), custom_call_target="tpu_custom_call" | custom-call | tf_op jit(solution)/shard_map/load/pallas_call | solution.py:369
  11.2 1.3 collective-permute-done.2.three
  12.5 4.8 %first.1 = (f32[16,32,128]{2,1,0:T(8,128)S(1)}, f32[16,32,128]{2,1,0:T(8,128)S(1)}, f32[8,128,128]{2,1,0:T(8,128)S(1)}, f32[2,32,128]{2,1,0:T(8,128)S(1)}) custom-call(s32[64]{0:T(128)S(1)} %reshape.11.table, bf16[4,16,128,128]{3,2,1,0:T(8,128)(2,1)S(1)} %get-tuple-element.24.left, bf16[4,16,128,128]{3,2,1,0:T(8,128)(2,1)S(1)} %get-tuple-element.25.right, ...), custom_call_target="tpu_custom_call" | custom-call | tf_op jit(solution)/shard_map/first/pallas_call | solution.py:369
  17.3 2.0 %collective-permute-start.3 = (f32[16,32,128]{2,1,0:T(8,128)S(1)}, f32[16,32,128]{2,1,0:T(8,128)S(1)}, u32[]{:S(2)}, u32[]{:S(2)}) collective-permute-start(f32[16,32,128]{2,1,0:T(8,128)S(1)} %get-tuple-element.31), channel_id=1, source_target_pairs={{0,4},{4,0},{1,5},{5,1},{2,6},{6,2},{3,7},{7,3},{8,12},{12,8},{9,1... | collective-permute-start | bytes 786440 | tf_op jit(solution)/shard_map/ppermute | solution.py:412
  19.3 1.2 collective-permute-done.3.second
  20.5 21.0 %all_to_all.41.parts = f32[16,32,128]{2,1,0:T(8,128)S(1)} all-to-all(f32[16,32,128]{2,1,0:T(8,128)S(1)} %join.2), channel_id=1, replica_groups=mesh['y_far'=2,'y_near'=2,'z'=8,'c'=2,'wf'=4] {'y_far','z'}, dimensions={0} | all-to-all | bytes 524288 | tf_op jit(solution)/shard_map/all_to_all | solution.py:397
  41.5 7.9 %all_to_all.42.parts = f32[8,32,128]{2,1,0:T(8,128)S(1)} all-to-all(f32[8,32,128]{2,1,0:T(8,128)S(1)} %spread.2), channel_id=1, replica_groups=mesh['y_far'=2,'y_near'=2,'z'=8,'c'=2,'wf'=4] {'y_near','wf'}, dimensions={0} | all-to-all | bytes 262144 | tf_op jit(solution)/shard_map/all_to_all | solution.py:397
  49.8 14.9 %all_to_all.43.own = f32[16,40,128]{2,1,0:T(8,128)S(1)} all-to-all(f32[16,40,128]{2,1,0:T(8,128)S(1)} %get-tuple-element.34), channel_id=1, replica_groups=mesh['y_far'=2,'y_near'=2,'z'=8,'c'=2,'wf'=4] {'y_far','z'}, dimensions={0} | all-to-all | bytes 655360 | tf_op jit(solution)/shard_map/all_to_all | solution.py:397
  64.7 4.2 %collective-permute-start.4 = (f32[16,40,128]{2,1,0:T(8,128)S(1)}, f32[16,40,128]{2,1,0:T(8,128)S(1)}, u32[]{:S(2)}, u32[]{:S(2)}) collective-permute-start(f32[16,40,128]{2,1,0:T(8,128)S(1)} %all_to_all.43.own), channel_id=1, source_target_pairs={{0,4},{4,0},{1,5},{5,1},{2,6},{6,2},{3,7},{7,3},{8,12},{12,8},{9,1... | collective-permute-start | bytes 983048 | tf_op jit(solution)/shard_map/ppermute | solution.py:412
  68.8 1.3 collective-permute-done.4.other
  70.1 5.2 %second.1 = (f32[16,32,128]{2,1,0:T(8,128)S(1)}, f32[16,32,128]{2,1,0:T(8,128)S(1)}, f32[8,128,128]{2,1,0:T(8,128)S(1)}, f32[8,128,128]{2,1,0:T(8,128)S(1)}, f32[8,128]{1,0:T(8,128)S(1)}) custom-call(s32[64]{0:T(128)S(1)} %reshape.11.table, bf16[4,16,128,128]{3,2,1,0:T(8,128)(2,1)S(1)} %get-tuple-element.24.left, ...), custom_call_target="tpu_custom_call" | custom-call | tf_op jit(solution)/shard_map/second/pallas_call | solution.py:369
  75.9 1.2 collective-permute-done.5.second
  77.1 14.7 %all_to_all.44.parts = f32[16,32,128]{2,1,0:T(8,128)S(1)} all-to-all(f32[16,32,128]{2,1,0:T(8,128)S(1)} %join.3), channel_id=1, replica_groups=mesh['y_far'=2,'y_near'=2,'z'=8,'c'=2,'wf'=4] {'y_far','z'}, dimensions={0} | all-to-all | bytes 524288 | tf_op jit(solution)/shard_map/all_to_all | solution.py:397
  91.8 7.9 %all_to_all.45.parts = f32[8,32,128]{2,1,0:T(8,128)S(1)} all-to-all(f32[8,32,128]{2,1,0:T(8,128)S(1)} %spread.3), channel_id=1, replica_groups=mesh['y_far'=2,'y_near'=2,'z'=8,'c'=2,'wf'=4] {'y_near','wf'}, dimensions={0} | all-to-all | bytes 262144 | tf_op jit(solution)/shard_map/all_to_all | solution.py:397
  100.3 14.8 %all_to_all.46.gathered = f32[16,40,128]{2,1,0:T(8,128)S(1)} all-to-all(f32[16,40,128]{2,1,0:T(8,128)S(1)} %turned.1), channel_id=1, replica_groups=mesh['y_far'=2,'y_near'=2,'z'=8,'c'=2,'wf'=4] {'y_far','z'}, dimensions={0} | all-to-all | bytes 655360 | tf_op jit(solution)/shard_map/all_to_all | solution.py:397
  115.1 4.3 %collective-permute-start.6 = (f32[16,40,128]{2,1,0:T(8,128)S(1)}, f32[16,40,128]{2,1,0:T(8,128)S(1)}, u32[]{:S(2)}, u32[]{:S(2)}) collective-permute-start(f32[16,40,128]{2,1,0:T(8,128)S(1)} %all_to_all.46.gathered), channel_id=1, source_target_pairs={{0,4},{4,0},{1,5},{5,1},{2,6},{6,2},{3,7},{7,3},{8,12},{12,8},{9,1... | collective-permute-start | bytes 983048 | tf_op jit(solution)/shard_map/ppermute | solution.py:412
  119.5 1.3 collective-permute-done.6.swapped
  120.7 3.0 %third.1 = (f32[256,128]{1,0:T(8,128)S(1)}, f32[4,128,128]{2,1,0:T(8,128)S(1)}, f32[4,128,128]{2,1,0:T(8,128)S(1)}, f32[8,128]{1,0:T(8,128)S(1)}) custom-call(s32[64]{0:T(128)S(1)} %reshape.11.table, bf16[4,16,128,128]{3,2,1,0:T(8,128)(2,1)S(1)} %get-tuple-element.24.left, bf16[4,16,128,128]{3,2,1,0:T(8,128)(2,1)S(1)} %get-tuple-element.25.right, ...), custom_call_target="tpu_custom_call" | custom-call | tf_op jit(solution)/shard_map/third/pallas_call | solution.py:369
  123.7 18.6 %all_to_all.47 = f32[256,1,128]{2,1,0:T(1,128)S(1)} all-to-all(f32[256,1,128]{2,1,0:T(1,128)S(1)} %bitcast.5), channel_id=1, replica_groups=mesh['y_far'=2,'y_near'=2,'z'=8,'c'=2,'wf'=4] {'y_far','y_near','z','c',..., dimensions={0} | all-to-all | bytes 262144 | tf_op jit(solution)/shard_map/all_to_all | solution.py:397
  142.3 1.1 last.1
  (19 shorter events, 3.0 us)
Async XLA Ops:
  2.5 8.3 %collective-permute-start.1 = (f32[40,128]{1,0:T(8,128)}, f32[40,128]{1,0:T(8,128)S(1)}, u32[]{:S(2)}, u32[]{:S(2)}) collective-permute-start(f32[40,128]{1,0:T(8,128)} %get-tuple-element.27.own), channel_id=1, source_target_pairs={{0,2},{1,3},{2,0},{3,1},{4,6},{5,7},{6,4},{7,5},{8,10},{9,11},{10,... | collective-permute-start | bytes 61448 | tf_op jit(solution)/shard_map/ppermute | solution.py:409
  6.1 5.1 %collective-permute-start = (f32[296,128]{1,0:T(8,128)}, f32[296,128]{1,0:T(8,128)S(1)}, u32[]{:S(2)}, u32[]{:S(2)}) collective-permute-start(f32[296,128]{1,0:T(8,128)} %get-tuple-element.28), channel_id=1, source_target_pairs={{0,1},{1,0},{2,3},{3,2},{4,5},{5,4},{6,7},{7,6},{8,9},{9,8},{10,11... | collective-permute-start | bytes 454664 | tf_op jit(solution)/shard_map/ppermute | solution.py:409
  6.4 6.0 %collective-permute-start.2 = (f32[296,128]{1,0:T(8,128)}, f32[296,128]{1,0:T(8,128)S(1)}, u32[]{:S(2)}, u32[]{:S(2)}) collective-permute-start(f32[296,128]{1,0:T(8,128)} %get-tuple-element.29), channel_id=1, source_target_pairs={{0,3},{1,2},{2,1},{3,0},{4,7},{5,6},{6,5},{7,4},{8,11},{9,10},{10,... | collective-permute-start | bytes 454664 | tf_op jit(solution)/shard_map/ppermute | solution.py:409
  8.5 4.0 %copy-start = (f32[4,128,128]{2,1,0:T(8,128)S(1)}, f32[4,128,128]{2,1,0:T(8,128)}, u32[]{:S(2)}) copy-start(f32[4,128,128]{2,1,0:T(8,128)} %get-tuple-element.26.start) | copy-start | bytes 786436
  8.5 4.0 %copy-start.2 = (f32[40,128]{1,0:T(8,128)S(1)}, f32[40,128]{1,0:T(8,128)}, u32[]{:S(2)}) copy-start(f32[40,128]{1,0:T(8,128)} %get-tuple-element.27.own) | copy-start | bytes 61444
  12.4 37.0 %copy-start.1 = (f32[2,32,128]{2,1,0:T(8,128)S(1)}, f32[2,32,128]{2,1,0:T(8,128)}, u32[]{:S(2)}) copy-start(f32[2,32,128]{2,1,0:T(8,128)} %get-tuple-element.32.masks) | copy-start | bytes 98308
  17.3 3.2 %collective-permute-start.3 = (f32[16,32,128]{2,1,0:T(8,128)S(1)}, f32[16,32,128]{2,1,0:T(8,128)S(1)}, u32[]{:S(2)}, u32[]{:S(2)}) collective-permute-start(f32[16,32,128]{2,1,0:T(8,128)S(1)} %get-tuple-element.31), channel_id=1, source_target_pairs={{0,4},{4,0},{1,5},{5,1},{2,6},{6,2},{3,7},{7,3},{8,12},{12,8},{9,1... | collective-permute-start | bytes 786440 | tf_op jit(solution)/shard_map/ppermute | solution.py:412
  64.7 5.4 %collective-permute-start.4 = (f32[16,40,128]{2,1,0:T(8,128)S(1)}, f32[16,40,128]{2,1,0:T(8,128)S(1)}, u32[]{:S(2)}, u32[]{:S(2)}) collective-permute-start(f32[16,40,128]{2,1,0:T(8,128)S(1)} %all_to_all.43.own), channel_id=1, source_target_pairs={{0,4},{4,0},{1,5},{5,1},{2,6},{6,2},{3,7},{7,3},{8,12},{12,8},{9,1... | collective-permute-start | bytes 983048 | tf_op jit(solution)/shard_map/ppermute | solution.py:412
  75.2 1.8 %collective-permute-start.5 = (f32[16,32,128]{2,1,0:T(8,128)S(1)}, f32[16,32,128]{2,1,0:T(8,128)S(1)}, u32[]{:S(2)}, u32[]{:S(2)}) collective-permute-start(f32[16,32,128]{2,1,0:T(8,128)S(1)} %get-tuple-element.37), channel_id=1, source_target_pairs={{0,4},{4,0},{1,5},{5,1},{2,6},{6,2},{3,7},{7,3},{8,12},{12,8},{9,1... | collective-permute-start | bytes 786440 | tf_op jit(solution)/shard_map/ppermute | solution.py:412
  115.1 5.6 %collective-permute-start.6 = (f32[16,40,128]{2,1,0:T(8,128)S(1)}, f32[16,40,128]{2,1,0:T(8,128)S(1)}, u32[]{:S(2)}, u32[]{:S(2)}) collective-permute-start(f32[16,40,128]{2,1,0:T(8,128)S(1)} %all_to_all.46.gathered), channel_id=1, source_target_pairs={{0,4},{4,0},{1,5},{5,1},{2,6},{6,2},{3,7},{7,3},{8,12},{12,8},{9,1... | collective-permute-start | bytes 983048 | tf_op jit(solution)/shard_map/ppermute | solution.py:412

commit v6 on v5

--- a/solution.py
+++ b/solution.py
@@ -110,7 +110,7 @@
 
 def half_step(table, left, right, vec_half, back, sector, index):
     for k in range(PAIRS):
-        entry = table[k * OWN + index]
+        entry = table[index * PAIRS + k]
         position = (sector + (entry >> 1)) & 7
         weight = (entry & 1).astype(f32)
         value = dot(left[index, k].T, vec_half[position])
@@ -121,7 +121,7 @@
 def full_step(table, left, right, vec_half, back, sums, sector, index):
     middle = dot(left[index].reshape(PAIRS * BLOCK, BLOCK), vec_half[sector & 7])
     for k in range(PAIRS):
-        entry = table[k * OWN + index]
+        entry = table[index * PAIRS + k]
         position = (sector + (entry >> 1)) & 7
         weight = (entry & 1).astype(f32)
         term = (middle[k * BLOCK : (k + 1) * BLOCK] * weight).astype(bf16)
@@ -175,11 +175,11 @@
 
 
 def join_kernel(first, second, out):
-    out[...] = first[...] + second[...]
+    out[...] = (first[...] + second[...]).astype(out.dtype)
 
 
 def spread_kernel(parts, out):
-    summed = jnp.sum(parts[...], axis=0)
+    summed = jnp.sum(parts[...].astype(f32), axis=0)
     for target in range(out.shape[0]):
         out[target] = summed
 
@@ -400,6 +400,7 @@
 def shards(guess, left_ops, right_ops, op_shift, op_mask, left_dims, right_dims):
     blocks = struct(WINDOW, BLOCK, BLOCK)
     half = struct(LINE, CHUNK, BLOCK)
+    sent = struct(LINE, CHUNK, BLOCK, dtype=bf16)
     own_blocks = struct(OWN, BLOCK, BLOCK)
     pair = struct(2, CHUNK, BLOCK)
     scalar_row = struct(EXTRA, BLOCK)
@@ -411,7 +412,7 @@
     def swapped(value):
         return lax.ppermute(value, "c", [(0, 1), (1, 0)])
 
-    table = (2 * op_shift[:, None] + op_mask).reshape(-1)
+    table = (2 * op_shift[None, :] + op_mask.T).reshape(-1)
     tail = EXTRA + CHUNK
     start, masks, one, own, three = call(
         norm_kernel, "norm",
@@ -428,7 +429,7 @@
     operators = (table, left, right)
 
     def reduced(keep, give):
-        (summed,) = small(join_kernel, "join", [half], keep, swapped(give))
+        (summed,) = small(join_kernel, "join", [sent], keep, swapped(give))
         parts = exchange(summed, LINE_AXES)
         (tiled,) = small(spread_kernel, "spread", [struct(CROSS, CHUNK, BLOCK)], parts)
         return exchange(tiled, CROSS_AXES)

time: 144 us -> 138 us (0.958)
  blocking collectives: 99.9 us -> 94.3 us
    all_to_all x7, blocking collectives: 99.9 us -> 94.3 us  [exchange(): return lax.all_to_all(value, axes, 0, 0, tiled=True)]
where the time goes in v6:
time: 138 us
  blocking collectives  94.3 us (68%)
  Pallas kernels  19.1 us (14%)
  starting transfers between devices  15.6 us (11%)
  waiting for transfers between devices  6.63 us (5%)
    all_to_all x7, blocking collectives, exchange(): return lax.all_to_all(value, axes, 0, 0, tiled=True)  94.3 us
    pallas_call x12, Pallas kernels, call(): pl.pallas_call(kernel, name=name, in_specs=in_specs, out_specs=out_specs...  19.1 us
    ppermute x4, starting transfers between devices, swapped(): return lax.ppermute(value, 'c', [(0, 1), (1, 0)])  11.1 us
    ppermute x4, waiting for transfers between devices, swapped(): return lax.ppermute(value, 'c', [(0, 1), (1, 0)])  4.84 us
    ppermute x3, starting transfers between devices, partner(): return lax.ppermute(value, 'wf', [(i, i ^ distance) for i in range(4)])  4.44 us
  transfers between devices with their start and end apart: 7, of which 6 were waited for; matrix products, arithmetic and copies ran while one was open for 1% of the time, Pallas kernels for 2%

profile of v6, /device:TPU:1, one launch (start us, length us, event | category | flops | bytes accessed | tf_op | source)
XLA Modules:
  0.0 137.9 jit_solution(5888775182278641001)
XLA Ops:
  0.6 1.9 %norm.1 = (f32[4,128,128]{2,1,0:T(8,128)}, f32[2,32,128]{2,1,0:T(8,128)}, f32[296,128]{1,0:T(8,128)}, f32[40,128]{1,0:T(8,128)}, f32[296,128]{1,0:T(8,128)}) custom-call(s32[16]{0:T(128)} %left_dims.1, s32[16]{0:T(128)} %right_dims.1, f32[4,128,128]{2,1,0:T(8,128)} %guess.1), custom_call_target="tpu_custom_call" | custom-call | tf_op jit(solution)/shard_map/norm/pallas_call | solution.py:369
  2.5 3.6 %collective-permute-start.1 = (f32[40,128]{1,0:T(8,128)}, f32[40,128]{1,0:T(8,128)S(1)}, u32[]{:S(2)}, u32[]{:S(2)}) collective-permute-start(f32[40,128]{1,0:T(8,128)} %get-tuple-element.27.own), channel_id=1, source_target_pairs={{0,2},{1,3},{2,0},{3,1},{4,6},{5,7},{6,4},{7,5},{8,10},{9,11},{10,... | collective-permute-start | bytes 61448 | tf_op jit(solution)/shard_map/ppermute | solution.py:410
  6.9 0.7 broadcast_multiply_fusion
  7.6 0.7 add_bitcast_fusion
  8.4 2.3 %load.1 = (bf16[4,16,128,128]{3,2,1,0:T(8,128)(2,1)S(1)}, bf16[4,16,128,128]{3,2,1,0:T(8,128)(2,1)S(1)}) custom-call(bf16[16,4,128,128]{3,2,1,0:T(8,128)(2,1)} %left_hbm.1, bf16[16,4,128,128]{3,2,1,0:T(8,128)(2,1)} %right_hbm.1), custom_call_target="tpu_custom_call" | custom-call | tf_op jit(solution)/shard_map/load/pallas_call | solution.py:369
  11.2 1.3 collective-permute-done.2.three
  12.5 4.8 %first.1 = (f32[16,32,128]{2,1,0:T(8,128)S(1)}, f32[16,32,128]{2,1,0:T(8,128)S(1)}, f32[8,128,128]{2,1,0:T(8,128)S(1)}, f32[2,32,128]{2,1,0:T(8,128)S(1)}) custom-call(s32[64]{0:T(128)S(1)} %reshape.11.table, bf16[4,16,128,128]{3,2,1,0:T(8,128)(2,1)S(1)} %get-tuple-element.24.left, bf16[4,16,128,128]{3,2,1,0:T(8,128)(2,1)S(1)} %get-tuple-element.25.right, ...), custom_call_target="tpu_custom_call" | custom-call | tf_op jit(solution)/shard_map/first/pallas_call | solution.py:369
  17.3 2.0 %collective-permute-start.3 = (f32[16,32,128]{2,1,0:T(8,128)S(1)}, f32[16,32,128]{2,1,0:T(8,128)S(1)}, u32[]{:S(2)}, u32[]{:S(2)}) collective-permute-start(f32[16,32,128]{2,1,0:T(8,128)S(1)} %get-tuple-element.31), channel_id=1, source_target_pairs={{0,4},{4,0},{1,5},{5,1},{2,6},{6,2},{3,7},{7,3},{8,12},{12,8},{9,1... | collective-permute-start | bytes 786440 | tf_op jit(solution)/shard_map/ppermute | solution.py:413
  19.3 1.2 collective-permute-done.3.second
  20.5 19.5 %all_to_all.41.parts = bf16[16,32,128]{2,1,0:T(8,128)(2,1)S(1)} all-to-all(bf16[16,32,128]{2,1,0:T(8,128)(2,1)S(1)} %join.2), channel_id=1, replica_groups=mesh['y_far'=2,'y_near'=2,'z'=8,'c'=2,'wf'=4] {'y_far','z'}, dimensions={0} | all-to-all | bytes 262144 | tf_op jit(solution)/shard_map/all_to_all | solution.py:397
  40.0 7.8 %all_to_all.42.parts = f32[8,32,128]{2,1,0:T(8,128)S(1)} all-to-all(f32[8,32,128]{2,1,0:T(8,128)S(1)} %spread.2), channel_id=1, replica_groups=mesh['y_far'=2,'y_near'=2,'z'=8,'c'=2,'wf'=4] {'y_near','wf'}, dimensions={0} | all-to-all | bytes 262144 | tf_op jit(solution)/shard_map/all_to_all | solution.py:397
  48.2 13.8 %all_to_all.43.own = f32[16,40,128]{2,1,0:T(8,128)S(1)} all-to-all(f32[16,40,128]{2,1,0:T(8,128)S(1)} %get-tuple-element.34), channel_id=1, replica_groups=mesh['y_far'=2,'y_near'=2,'z'=8,'c'=2,'wf'=4] {'y_far','z'}, dimensions={0} | all-to-all | bytes 655360 | tf_op jit(solution)/shard_map/all_to_all | solution.py:397
  62.0 4.3 %collective-permute-start.4 = (f32[16,40,128]{2,1,0:T(8,128)S(1)}, f32[16,40,128]{2,1,0:T(8,128)S(1)}, u32[]{:S(2)}, u32[]{:S(2)}) collective-permute-start(f32[16,40,128]{2,1,0:T(8,128)S(1)} %all_to_all.43.own), channel_id=1, source_target_pairs={{0,4},{4,0},{1,5},{5,1},{2,6},{6,2},{3,7},{7,3},{8,12},{12,8},{9,1... | collective-permute-start | bytes 983048 | tf_op jit(solution)/shard_map/ppermute | solution.py:413
  66.3 1.3 collective-permute-done.4.other
  67.6 5.2 %second.1 = (f32[16,32,128]{2,1,0:T(8,128)S(1)}, f32[16,32,128]{2,1,0:T(8,128)S(1)}, f32[8,128,128]{2,1,0:T(8,128)S(1)}, f32[8,128,128]{2,1,0:T(8,128)S(1)}, f32[8,128]{1,0:T(8,128)S(1)}) custom-call(s32[64]{0:T(128)S(1)} %reshape.11.table, bf16[4,16,128,128]{3,2,1,0:T(8,128)(2,1)S(1)} %get-tuple-element.24.left, ...), custom_call_target="tpu_custom_call" | custom-call | tf_op jit(solution)/shard_map/second/pallas_call | solution.py:369
  73.2 1.2 collective-permute-done.5.second
  74.4 13.2 %all_to_all.44.parts = bf16[16,32,128]{2,1,0:T(8,128)(2,1)S(1)} all-to-all(bf16[16,32,128]{2,1,0:T(8,128)(2,1)S(1)} %join.3), channel_id=1, replica_groups=mesh['y_far'=2,'y_near'=2,'z'=8,'c'=2,'wf'=4] {'y_far','z'}, dimensions={0} | all-to-all | bytes 262144 | tf_op jit(solution)/shard_map/all_to_all | solution.py:397
  87.7 7.8 %all_to_all.45.parts = f32[8,32,128]{2,1,0:T(8,128)S(1)} all-to-all(f32[8,32,128]{2,1,0:T(8,128)S(1)} %spread.3), channel_id=1, replica_groups=mesh['y_far'=2,'y_near'=2,'z'=8,'c'=2,'wf'=4] {'y_near','wf'}, dimensions={0} | all-to-all | bytes 262144 | tf_op jit(solution)/shard_map/all_to_all | solution.py:397
  96.0 13.5 %all_to_all.46.gathered = f32[16,40,128]{2,1,0:T(8,128)S(1)} all-to-all(f32[16,40,128]{2,1,0:T(8,128)S(1)} %turned.1), channel_id=1, replica_groups=mesh['y_far'=2,'y_near'=2,'z'=8,'c'=2,'wf'=4] {'y_far','z'}, dimensions={0} | all-to-all | bytes 655360 | tf_op jit(solution)/shard_map/all_to_all | solution.py:397
  109.5 4.3 %collective-permute-start.6 = (f32[16,40,128]{2,1,0:T(8,128)S(1)}, f32[16,40,128]{2,1,0:T(8,128)S(1)}, u32[]{:S(2)}, u32[]{:S(2)}) collective-permute-start(f32[16,40,128]{2,1,0:T(8,128)S(1)} %all_to_all.46.gathered), channel_id=1, source_target_pairs={{0,4},{4,0},{1,5},{5,1},{2,6},{6,2},{3,7},{7,3},{8,12},{12,8},{9,1... | collective-permute-start | bytes 983048 | tf_op jit(solution)/shard_map/ppermute | solution.py:413
  113.8 1.3 collective-permute-done.6.swapped
  115.1 3.0 %third.1 = (f32[256,128]{1,0:T(8,128)S(1)}, f32[4,128,128]{2,1,0:T(8,128)S(1)}, f32[4,128,128]{2,1,0:T(8,128)S(1)}, f32[8,128]{1,0:T(8,128)S(1)}) custom-call(s32[64]{0:T(128)S(1)} %reshape.11.table, bf16[4,16,128,128]{3,2,1,0:T(8,128)(2,1)S(1)} %get-tuple-element.24.left, bf16[4,16,128,128]{3,2,1,0:T(8,128)(2,1)S(1)} %get-tuple-element.25.right, ...), custom_call_target="tpu_custom_call" | custom-call | tf_op jit(solution)/shard_map/third/pallas_call | solution.py:369
  118.1 18.6 %all_to_all.47 = f32[256,1,128]{2,1,0:T(1,128)S(1)} all-to-all(f32[256,1,128]{2,1,0:T(1,128)S(1)} %bitcast.7), channel_id=1, replica_groups=mesh['y_far'=2,'y_near'=2,'z'=8,'c'=2,'wf'=4] {'y_far','y_near','z','c',..., dimensions={0} | all-to-all | bytes 262144 | tf_op jit(solution)/shard_map/all_to_all | solution.py:397
  136.7 1.1 last.1
  (18 shorter events, 2.8 us)
Async XLA Ops:
  2.5 8.1 %collective-permute-start.1 = (f32[40,128]{1,0:T(8,128)}, f32[40,128]{1,0:T(8,128)S(1)}, u32[]{:S(2)}, u32[]{:S(2)}) collective-permute-start(f32[40,128]{1,0:T(8,128)} %get-tuple-element.27.own), channel_id=1, source_target_pairs={{0,2},{1,3},{2,0},{3,1},{4,6},{5,7},{6,4},{7,5},{8,10},{9,11},{10,... | collective-permute-start | bytes 61448 | tf_op jit(solution)/shard_map/ppermute | solution.py:410
  6.1 5.1 %collective-permute-start = (f32[296,128]{1,0:T(8,128)}, f32[296,128]{1,0:T(8,128)S(1)}, u32[]{:S(2)}, u32[]{:S(2)}) collective-permute-start(f32[296,128]{1,0:T(8,128)} %get-tuple-element.28), channel_id=1, source_target_pairs={{0,1},{1,0},{2,3},{3,2},{4,5},{5,4},{6,7},{7,6},{8,9},{9,8},{10,11... | collective-permute-start | bytes 454664 | tf_op jit(solution)/shard_map/ppermute | solution.py:410
  6.4 6.0 %collective-permute-start.2 = (f32[296,128]{1,0:T(8,128)}, f32[296,128]{1,0:T(8,128)S(1)}, u32[]{:S(2)}, u32[]{:S(2)}) collective-permute-start(f32[296,128]{1,0:T(8,128)} %get-tuple-element.29), channel_id=1, source_target_pairs={{0,3},{1,2},{2,1},{3,0},{4,7},{5,6},{6,5},{7,4},{8,11},{9,10},{10,... | collective-permute-start | bytes 454664 | tf_op jit(solution)/shard_map/ppermute | solution.py:410
  8.4 4.1 %copy-start = (f32[4,128,128]{2,1,0:T(8,128)S(1)}, f32[4,128,128]{2,1,0:T(8,128)}, u32[]{:S(2)}) copy-start(f32[4,128,128]{2,1,0:T(8,128)} %get-tuple-element.26.start) | copy-start | bytes 786436
  8.4 4.1 %copy-start.2 = (f32[40,128]{1,0:T(8,128)S(1)}, f32[40,128]{1,0:T(8,128)}, u32[]{:S(2)}) copy-start(f32[40,128]{1,0:T(8,128)} %get-tuple-element.27.own) | copy-start | bytes 61444
  12.4 35.4 %copy-start.1 = (f32[2,32,128]{2,1,0:T(8,128)S(1)}, f32[2,32,128]{2,1,0:T(8,128)}, u32[]{:S(2)}) copy-start(f32[2,32,128]{2,1,0:T(8,128)} %get-tuple-element.32.masks) | copy-start | bytes 98308
  17.3 3.2 %collective-permute-start.3 = (f32[16,32,128]{2,1,0:T(8,128)S(1)}, f32[16,32,128]{2,1,0:T(8,128)S(1)}, u32[]{:S(2)}, u32[]{:S(2)}) collective-permute-start(f32[16,32,128]{2,1,0:T(8,128)S(1)} %get-tuple-element.31), channel_id=1, source_target_pairs={{0,4},{4,0},{1,5},{5,1},{2,6},{6,2},{3,7},{7,3},{8,12},{12,8},{9,1... | collective-permute-start | bytes 786440 | tf_op jit(solution)/shard_map/ppermute | solution.py:413
  62.0 5.6 %collective-permute-start.4 = (f32[16,40,128]{2,1,0:T(8,128)S(1)}, f32[16,40,128]{2,1,0:T(8,128)S(1)}, u32[]{:S(2)}, u32[]{:S(2)}) collective-permute-start(f32[16,40,128]{2,1,0:T(8,128)S(1)} %all_to_all.43.own), channel_id=1, source_target_pairs={{0,4},{4,0},{1,5},{5,1},{2,6},{6,2},{3,7},{7,3},{8,12},{12,8},{9,1... | collective-permute-start | bytes 983048 | tf_op jit(solution)/shard_map/ppermute | solution.py:413
  72.8 1.6 %collective-permute-start.5 = (f32[16,32,128]{2,1,0:T(8,128)S(1)}, f32[16,32,128]{2,1,0:T(8,128)S(1)}, u32[]{:S(2)}, u32[]{:S(2)}) collective-permute-start(f32[16,32,128]{2,1,0:T(8,128)S(1)} %get-tuple-element.37), channel_id=1, source_target_pairs={{0,4},{4,0},{1,5},{5,1},{2,6},{6,2},{3,7},{7,3},{8,12},{12,8},{9,1... | collective-permute-start | bytes 786440 | tf_op jit(solution)/shard_map/ppermute | solution.py:413
  109.5 5.6 %collective-permute-start.6 = (f32[16,40,128]{2,1,0:T(8,128)S(1)}, f32[16,40,128]{2,1,0:T(8,128)S(1)}, u32[]{:S(2)}, u32[]{:S(2)}) collective-permute-start(f32[16,40,128]{2,1,0:T(8,128)S(1)} %all_to_all.46.gathered), channel_id=1, source_target_pairs={{0,4},{4,0},{1,5},{5,1},{2,6},{6,2},{3,7},{7,3},{8,12},{12,8},{9,1... | collective-permute-start | bytes 983048 | tf_op jit(solution)/shard_map/ppermute | solution.py:413

commit v7 on v6

--- a/solution.py
+++ b/solution.py
@@ -16,6 +16,7 @@
 HALF = 4
 ROWS = 8
 CHUNK = HALF * ROWS
+PACKET = CHUNK + 1
 SIDE = 2 * BLOCK
 EXTRA = 8
 ENTRIES = float(SECTORS * BLOCK * BLOCK)
@@ -62,9 +63,9 @@
     return (row < height) & (column < width)
 
 
-def pack(values):
-    lane = lax.broadcasted_iota(jnp.int32, (EXTRA, BLOCK), 1)
-    packed = jnp.zeros((EXTRA, BLOCK), f32)
+def pack(values, rows=EXTRA):
+    lane = lax.broadcasted_iota(jnp.int32, (rows, BLOCK), 1)
+    packed = jnp.zeros((rows, BLOCK), f32)
     for place, value in enumerate(values):
         packed = jnp.where(lane == place, value, packed)
     return packed
@@ -211,10 +212,9 @@
         block = jnp.where(sector == base + k, values[0][rows], 0.0)
         chosen.append(jnp.where(sector == base + k + 8, values[1][rows], block))
     chosen = jnp.concatenate(chosen, axis=0)
-    packed = pack(sums)
+    packet = jnp.concatenate([chosen, pack(sums, 1)], axis=0)
     for target in range(LINE):
-        out[target, 0:CHUNK] = chosen
-        out[target, CHUNK:] = packed
+        out[target * PACKET : (target + 1) * PACKET] = packet
 
 
 def image_kernel(parts, masks, pieces, out, image_pieces):
@@ -233,7 +233,9 @@
 
 
 def both(cores, count):
-    return zip(*[lanes(held[:, CHUNK, :], count) for held in cores])
+    ends = range(CHUNK, LINE * PACKET, PACKET)
+    rows = [jnp.concatenate([held[end : end + 1] for end in ends], axis=0) for held in cores]
+    return zip(*[lanes(held, count) for held in rows])
 
 
 def add(values):
@@ -241,8 +243,10 @@
 
 
 def held_block(cores, position):
-    rows = slice(ROWS * (position % HALF), ROWS * (position % HALF) + ROWS)
-    own, other = (held[:, rows, :].reshape(BLOCK, BLOCK) for held in cores)
+    firsts = range(ROWS * (position % HALF), LINE * PACKET, PACKET)
+    own, other = (
+        jnp.concatenate([held[first : first + ROWS] for first in firsts], axis=0) for held in cores
+    )
     return jnp.where(lax.axis_index("c") == position // HALF, own, other)
 
 
@@ -404,7 +408,7 @@
     own_blocks = struct(OWN, BLOCK, BLOCK)
     pair = struct(2, CHUNK, BLOCK)
     scalar_row = struct(EXTRA, BLOCK)
-    packet = struct(LINE, CHUNK + EXTRA, BLOCK)
+    packet = struct(LINE * PACKET, BLOCK)
 
     def partner(value, distance):
         return lax.ppermute(value, "wf", [(i, i ^ distance) for i in range(4)])
@@ -435,7 +439,7 @@
         return exchange(tiled, CROSS_AXES)
 
     def gathered(packets):
-        packets = exchange(packets, LINE_AXES)
+        packets = exchange(packets.reshape(-1, 1, BLOCK), LINE_AXES).reshape(-1, BLOCK)
         return packets, swapped(packets)
 
     keep, give, vector, pieces = step(

time: 138 us -> 136 us (0.986)
  starting transfers between devices: 15.6 us -> 14.1 us
    ppermute x4, starting transfers between devices: 11.1 us -> 9.7 us  [swapped(): return lax.ppermute(value, 'c', [(0, 1), (1, 0)])]
where the time goes in v7:
time: 136 us
  blocking collectives  93.6 us (69%)
  Pallas kernels  19.2 us (14%)
  starting transfers between devices  14.1 us (10%)
  waiting for transfers between devices  6.46 us (5%)
    all_to_all x7, blocking collectives, exchange(): return lax.all_to_all(value, axes, 0, 0, tiled=True)  93.6 us
    pallas_call x12, Pallas kernels, call(): pl.pallas_call(kernel, name=name, in_specs=in_specs, out_specs=out_specs...  19.2 us
    ppermute x4, starting transfers between devices, swapped(): return lax.ppermute(value, 'c', [(0, 1), (1, 0)])  9.7 us
    ppermute x4, waiting for transfers between devices, swapped(): return lax.ppermute(value, 'c', [(0, 1), (1, 0)])  4.67 us
    ppermute x3, starting transfers between devices, partner(): return lax.ppermute(value, 'wf', [(i, i ^ distance) for i in range(4)])  4.44 us
  transfers between devices with their start and end apart: 7, of which 6 were waited for; matrix products, arithmetic and copies ran while one was open for 1% of the time, Pallas kernels for 2%

profile of v7, /device:TPU:1, one launch (start us, length us, event | category | flops | bytes accessed | tf_op | source)
XLA Modules:
  0.0 135.6 jit_solution(5595471120615693642)
XLA Ops:
  0.6 1.9 %norm.1 = (f32[4,128,128]{2,1,0:T(8,128)}, f32[2,32,128]{2,1,0:T(8,128)}, f32[296,128]{1,0:T(8,128)}, f32[40,128]{1,0:T(8,128)}, f32[296,128]{1,0:T(8,128)}) custom-call(s32[16]{0:T(128)} %left_dims.1, s32[16]{0:T(128)} %right_dims.1, f32[4,128,128]{2,1,0:T(8,128)} %guess.1), custom_call_target="tpu_custom_call" | custom-call | tf_op jit(solution)/shard_map/norm/pallas_call | solution.py:373
  2.5 3.6 %collective-permute-start.1 = (f32[40,128]{1,0:T(8,128)}, f32[40,128]{1,0:T(8,128)S(1)}, u32[]{:S(2)}, u32[]{:S(2)}) collective-permute-start(f32[40,128]{1,0:T(8,128)} %get-tuple-element.27.own), channel_id=1, source_target_pairs={{0,2},{1,3},{2,0},{3,1},{4,6},{5,7},{6,4},{7,5},{8,10},{9,11},{10,... | collective-permute-start | bytes 61448 | tf_op jit(solution)/shard_map/ppermute | solution.py:414
  6.9 0.7 broadcast_multiply_fusion
  7.6 0.7 add_bitcast_fusion
  8.4 2.3 %load.1 = (bf16[4,16,128,128]{3,2,1,0:T(8,128)(2,1)S(1)}, bf16[4,16,128,128]{3,2,1,0:T(8,128)(2,1)S(1)}) custom-call(bf16[16,4,128,128]{3,2,1,0:T(8,128)(2,1)} %left_hbm.1, bf16[16,4,128,128]{3,2,1,0:T(8,128)(2,1)} %right_hbm.1), custom_call_target="tpu_custom_call" | custom-call | tf_op jit(solution)/shard_map/load/pallas_call | solution.py:373
  11.2 1.3 collective-permute-done.2.three
  12.5 4.8 %first.1 = (f32[16,32,128]{2,1,0:T(8,128)S(1)}, f32[16,32,128]{2,1,0:T(8,128)S(1)}, f32[8,128,128]{2,1,0:T(8,128)S(1)}, f32[2,32,128]{2,1,0:T(8,128)S(1)}) custom-call(s32[64]{0:T(128)S(1)} %reshape.23.table, bf16[4,16,128,128]{3,2,1,0:T(8,128)(2,1)S(1)} %get-tuple-element.24.left, bf16[4,16,128,128]{3,2,1,0:T(8,128)(2,1)S(1)} %get-tuple-element.25.right, ...), custom_call_target="tpu_custom_call" | custom-call | tf_op jit(solution)/shard_map/first/pallas_call | solution.py:373
  17.3 2.0 %collective-permute-start.3 = (f32[16,32,128]{2,1,0:T(8,128)S(1)}, f32[16,32,128]{2,1,0:T(8,128)S(1)}, u32[]{:S(2)}, u32[]{:S(2)}) collective-permute-start(f32[16,32,128]{2,1,0:T(8,128)S(1)} %get-tuple-element.31), channel_id=1, source_target_pairs={{0,4},{4,0},{1,5},{5,1},{2,6},{6,2},{3,7},{7,3},{8,12},{12,8},{9,1... | collective-permute-start | bytes 786440 | tf_op jit(solution)/shard_map/ppermute | solution.py:417
  19.3 1.2 collective-permute-done.3.second
  20.5 19.5 %all_to_all.41.parts = bf16[16,32,128]{2,1,0:T(8,128)(2,1)S(1)} all-to-all(bf16[16,32,128]{2,1,0:T(8,128)(2,1)S(1)} %join.2), channel_id=1, replica_groups=mesh['y_far'=2,'y_near'=2,'z'=8,'c'=2,'wf'=4] {'y_far','z'}, dimensions={0} | all-to-all | bytes 262144 | tf_op jit(solution)/shard_map/all_to_all | solution.py:401
  40.0 7.8 %all_to_all.42.parts = f32[8,32,128]{2,1,0:T(8,128)S(1)} all-to-all(f32[8,32,128]{2,1,0:T(8,128)S(1)} %spread.2), channel_id=1, replica_groups=mesh['y_far'=2,'y_near'=2,'z'=8,'c'=2,'wf'=4] {'y_near','wf'}, dimensions={0} | all-to-all | bytes 262144 | tf_op jit(solution)/shard_map/all_to_all | solution.py:401
  48.2 13.6 %all_to_all.43 = f32[528,1,128]{2,1,0:T(1,128)S(1)} all-to-all(f32[528,1,128]{2,1,0:T(1,128)S(1)} %bitcast.20), channel_id=1, replica_groups=mesh['y_far'=2,'y_near'=2,'z'=8,'c'=2,'wf'=4] {'y_far','z'}, dimensions={0} | all-to-all | bytes 540672 | tf_op jit(solution)/shard_map/all_to_all | solution.py:401
  61.8 3.6 %collective-permute-start.4 = (f32[528,128]{1,0:T(8,128)S(1)}, f32[528,128]{1,0:T(8,128)S(1)}, u32[]{:S(2)}, u32[]{:S(2)}) collective-permute-start(f32[528,128]{1,0:T(8,128)S(1)} %bitcast.17), channel_id=1, source_target_pairs={{0,4},{4,0},{1,5},{5,1},{2,6},{6,2},{3,7},{7,3},{8,12},{12,8},{9,1... | collective-permute-start | bytes 811016 | tf_op jit(solution)/shard_map/ppermute | solution.py:417
  65.4 1.2 collective-permute-done.4.other
  66.5 5.1 %second.1 = (f32[16,32,128]{2,1,0:T(8,128)S(1)}, f32[16,32,128]{2,1,0:T(8,128)S(1)}, f32[8,128,128]{2,1,0:T(8,128)S(1)}, f32[8,128,128]{2,1,0:T(8,128)S(1)}, f32[8,128]{1,0:T(8,128)S(1)}) custom-call(s32[64]{0:T(128)S(1)} %reshape.23.table, bf16[4,16,128,128]{3,2,1,0:T(8,128)(2,1)S(1)} %get-tuple-element.24.left, ...), custom_call_target="tpu_custom_call" | custom-call | tf_op jit(solution)/shard_map/second/pallas_call | solution.py:373
  72.2 1.2 collective-permute-done.5.second
  73.4 13.0 %all_to_all.44.parts = bf16[16,32,128]{2,1,0:T(8,128)(2,1)S(1)} all-to-all(bf16[16,32,128]{2,1,0:T(8,128)(2,1)S(1)} %join.3), channel_id=1, replica_groups=mesh['y_far'=2,'y_near'=2,'z'=8,'c'=2,'wf'=4] {'y_far','z'}, dimensions={0} | all-to-all | bytes 262144 | tf_op jit(solution)/shard_map/all_to_all | solution.py:401
  86.4 7.8 %all_to_all.45.parts = f32[8,32,128]{2,1,0:T(8,128)S(1)} all-to-all(f32[8,32,128]{2,1,0:T(8,128)S(1)} %spread.3), channel_id=1, replica_groups=mesh['y_far'=2,'y_near'=2,'z'=8,'c'=2,'wf'=4] {'y_near','wf'}, dimensions={0} | all-to-all | bytes 262144 | tf_op jit(solution)/shard_map/all_to_all | solution.py:401
  94.7 13.4 %all_to_all.46 = f32[528,1,128]{2,1,0:T(1,128)S(1)} all-to-all(f32[528,1,128]{2,1,0:T(1,128)S(1)} %bitcast.16), channel_id=1, replica_groups=mesh['y_far'=2,'y_near'=2,'z'=8,'c'=2,'wf'=4] {'y_far','z'}, dimensions={0} | all-to-all | bytes 540672 | tf_op jit(solution)/shard_map/all_to_all | solution.py:401
  108.2 3.6 %collective-permute-start.6 = (f32[528,128]{1,0:T(8,128)S(1)}, f32[528,128]{1,0:T(8,128)S(1)}, u32[]{:S(2)}, u32[]{:S(2)}) collective-permute-start(f32[528,128]{1,0:T(8,128)S(1)} %bitcast.14), channel_id=1, source_target_pairs={{0,4},{4,0},{1,5},{5,1},{2,6},{6,2},{3,7},{7,3},{8,12},{12,8},{9,1... | collective-permute-start | bytes 811016 | tf_op jit(solution)/shard_map/ppermute | solution.py:417
  111.8 1.2 collective-permute-done.6.swapped
  112.9 3.0 %third.1 = (f32[256,128]{1,0:T(8,128)S(1)}, f32[4,128,128]{2,1,0:T(8,128)S(1)}, f32[4,128,128]{2,1,0:T(8,128)S(1)}, f32[8,128]{1,0:T(8,128)S(1)}) custom-call(s32[64]{0:T(128)S(1)} %reshape.23.table, bf16[4,16,128,128]{3,2,1,0:T(8,128)(2,1)S(1)} %get-tuple-element.24.left, bf16[4,16,128,128]{3,2,1,0:T(8,128)(2,1)S(1)} %get-tuple-element.25.right, ...), custom_call_target="tpu_custom_call" | custom-call | tf_op jit(solution)/shard_map/third/pallas_call | solution.py:373
  116.0 18.4 %all_to_all.47 = f32[256,1,128]{2,1,0:T(1,128)S(1)} all-to-all(f32[256,1,128]{2,1,0:T(1,128)S(1)} %bitcast.21), channel_id=1, replica_groups=mesh['y_far'=2,'y_near'=2,'z'=8,'c'=2,'wf'=4] {'y_far','y_near','z','c',..., dimensions={0} | all-to-all | bytes 262144 | tf_op jit(solution)/shard_map/all_to_all | solution.py:401
  134.4 1.1 last.1
  (18 shorter events, 2.9 us)
Async XLA Ops:
  2.5 8.1 %collective-permute-start.1 = (f32[40,128]{1,0:T(8,128)}, f32[40,128]{1,0:T(8,128)S(1)}, u32[]{:S(2)}, u32[]{:S(2)}) collective-permute-start(f32[40,128]{1,0:T(8,128)} %get-tuple-element.27.own), channel_id=1, source_target_pairs={{0,2},{1,3},{2,0},{3,1},{4,6},{5,7},{6,4},{7,5},{8,10},{9,11},{10,... | collective-permute-start | bytes 61448 | tf_op jit(solution)/shard_map/ppermute | solution.py:414
  6.1 5.1 %collective-permute-start = (f32[296,128]{1,0:T(8,128)}, f32[296,128]{1,0:T(8,128)S(1)}, u32[]{:S(2)}, u32[]{:S(2)}) collective-permute-start(f32[296,128]{1,0:T(8,128)} %get-tuple-element.28), channel_id=1, source_target_pairs={{0,1},{1,0},{2,3},{3,2},{4,5},{5,4},{6,7},{7,6},{8,9},{9,8},{10,11... | collective-permute-start | bytes 454664 | tf_op jit(solution)/shard_map/ppermute | solution.py:414
  6.4 6.0 %collective-permute-start.2 = (f32[296,128]{1,0:T(8,128)}, f32[296,128]{1,0:T(8,128)S(1)}, u32[]{:S(2)}, u32[]{:S(2)}) collective-permute-start(f32[296,128]{1,0:T(8,128)} %get-tuple-element.29), channel_id=1, source_target_pairs={{0,3},{1,2},{2,1},{3,0},{4,7},{5,6},{6,5},{7,4},{8,11},{9,10},{10,... | collective-permute-start | bytes 454664 | tf_op jit(solution)/shard_map/ppermute | solution.py:414
  8.4 4.1 %copy-start = (f32[4,128,128]{2,1,0:T(8,128)S(1)}, f32[4,128,128]{2,1,0:T(8,128)}, u32[]{:S(2)}) copy-start(f32[4,128,128]{2,1,0:T(8,128)} %get-tuple-element.26.start) | copy-start | bytes 786436
  8.4 4.1 %copy-start.2 = (f32[40,128]{1,0:T(8,128)S(1)}, f32[40,128]{1,0:T(8,128)}, u32[]{:S(2)}) copy-start(f32[40,128]{1,0:T(8,128)} %get-tuple-element.27.own) | copy-start | bytes 61444
  12.4 35.4 %copy-start.1 = (f32[2,32,128]{2,1,0:T(8,128)S(1)}, f32[2,32,128]{2,1,0:T(8,128)}, u32[]{:S(2)}) copy-start(f32[2,32,128]{2,1,0:T(8,128)} %get-tuple-element.32.masks) | copy-start | bytes 98308
  17.3 3.2 %collective-permute-start.3 = (f32[16,32,128]{2,1,0:T(8,128)S(1)}, f32[16,32,128]{2,1,0:T(8,128)S(1)}, u32[]{:S(2)}, u32[]{:S(2)}) collective-permute-start(f32[16,32,128]{2,1,0:T(8,128)S(1)} %get-tuple-element.31), channel_id=1, source_target_pairs={{0,4},{4,0},{1,5},{5,1},{2,6},{6,2},{3,7},{7,3},{8,12},{12,8},{9,1... | collective-permute-start | bytes 786440 | tf_op jit(solution)/shard_map/ppermute | solution.py:417
  61.8 4.8 %collective-permute-start.4 = (f32[528,128]{1,0:T(8,128)S(1)}, f32[528,128]{1,0:T(8,128)S(1)}, u32[]{:S(2)}, u32[]{:S(2)}) collective-permute-start(f32[528,128]{1,0:T(8,128)S(1)} %bitcast.17), channel_id=1, source_target_pairs={{0,4},{4,0},{1,5},{5,1},{2,6},{6,2},{3,7},{7,3},{8,12},{12,8},{9,1... | collective-permute-start | bytes 811016 | tf_op jit(solution)/shard_map/ppermute | solution.py:417
  71.7 1.6 %collective-permute-start.5 = (f32[16,32,128]{2,1,0:T(8,128)S(1)}, f32[16,32,128]{2,1,0:T(8,128)S(1)}, u32[]{:S(2)}, u32[]{:S(2)}) collective-permute-start(f32[16,32,128]{2,1,0:T(8,128)S(1)} %get-tuple-element.37), channel_id=1, source_target_pairs={{0,4},{4,0},{1,5},{5,1},{2,6},{6,2},{3,7},{7,3},{8,12},{12,8},{9,1... | collective-permute-start | bytes 786440 | tf_op jit(solution)/shard_map/ppermute | solution.py:417
  108.2 4.8 %collective-permute-start.6 = (f32[528,128]{1,0:T(8,128)S(1)}, f32[528,128]{1,0:T(8,128)S(1)}, u32[]{:S(2)}, u32[]{:S(2)}) collective-permute-start(f32[528,128]{1,0:T(8,128)S(1)} %bitcast.14), channel_id=1, source_target_pairs={{0,4},{4,0},{1,5},{5,1},{2,6},{6,2},{3,7},{7,3},{8,12},{12,8},{9,1... | collective-permute-start | bytes 811016 | tf_op jit(solution)/shard_map/ppermute | solution.py:417

commit v8 on v7

--- a/solution.py
+++ b/solution.py
@@ -115,26 +115,36 @@
         position = (sector + (entry >> 1)) & 7
         weight = (entry & 1).astype(f32)
         value = dot(left[index, k].T, vec_half[position])
-        back[:, k * BLOCK : (k + 1) * BLOCK] = (value * weight).astype(bf16)
-    return dot(back[...], right[index].reshape(PAIRS * BLOCK, BLOCK))
-
-
-def full_step(table, left, right, vec_half, back, sums, sector, index):
-    middle = dot(left[index].reshape(PAIRS * BLOCK, BLOCK), vec_half[sector & 7])
-    for k in range(PAIRS):
-        entry = table[index * PAIRS + k]
-        position = (sector + (entry >> 1)) & 7
-        weight = (entry & 1).astype(f32)
-        term = (middle[k * BLOCK : (k + 1) * BLOCK] * weight).astype(bf16)
-        sums[position] += dot(term, right[index, k], 1, 1)
-    sums[sector & 7] += half_step(table, left, right, vec_half, back, sector, index)
+        back[index & 1, :, k * BLOCK : (k + 1) * BLOCK] = (value * weight).astype(bf16)
+    return dot(back[index & 1], right[index].reshape(PAIRS * BLOCK, BLOCK))
+
+
+def middle_pair(left, vec_half, sector, index):
+    zero = jnp.zeros((BLOCK, BLOCK), bf16)
+    rows = [
+        jnp.concatenate([vec_half[sector & 7], zero], axis=1),
+        jnp.concatenate([zero, vec_half[(sector + 1) & 7]], axis=1),
+    ]
+    blocks = [left[index + i].reshape(PAIRS * BLOCK, BLOCK) for i in range(2)]
+    return dot(jnp.concatenate(blocks, axis=1), jnp.concatenate(rows, axis=0))
 
 
 def full_sweep(table, left, right, vec_half, back, sums, keep, give):
     sums[...] = jnp.zeros_like(sums)
     first_sector = OWN * lax.axis_index("wf")
-    for i in range(OWN):
-        full_step(table, left, right, vec_half, back, sums, first_sector + i, i)
+    for pair in range(0, OWN, 2):
+        middle = middle_pair(left, vec_half, first_sector + pair, pair)
+        for i in range(2):
+            sector, index = first_sector + pair + i, pair + i
+            for k in range(PAIRS):
+                entry = table[index * PAIRS + k]
+                position = (sector + (entry >> 1)) & 7
+                weight = (entry & 1).astype(f32)
+                value = middle[k * BLOCK : (k + 1) * BLOCK, i * BLOCK : (i + 1) * BLOCK]
+                sums[position] += dot((value * weight).astype(bf16), right[index, k], 1, 1)
+        for i in range(2):
+            sector, index = first_sector + pair + i, pair + i
+            sums[sector & 7] += half_step(table, left, right, vec_half, back, sector, index)
     core = lax.axis_index("c")
     for out, first in ((keep, HALF * core), (give, HALF - HALF * core)):
         for i in range(HALF):
@@ -388,7 +398,7 @@
 def step(kernel, name, outs, operators, arrays, sums=True):
     scratch = [
         pltpu.VMEM((WINDOW, BLOCK, BLOCK), bf16),
-        pltpu.VMEM((BLOCK, PAIRS * BLOCK), bf16),
+        pltpu.VMEM((2, BLOCK, PAIRS * BLOCK), bf16),
     ]
     if sums:
         scratch.append(pltpu.VMEM((WINDOW, BLOCK, BLOCK), f32))

time: 136 us -> 136 us (level)
  no operation moved by 1% of the time
where the time goes in v8:
time: 136 us; the launch traced here: 135 us
  blocking collectives  93.6 us (69%)
  Pallas kernels  18.7 us (14%)
  starting transfers between devices  14.1 us (10%)
  waiting for transfers between devices  6.46 us (5%)
    all_to_all x7, blocking collectives, exchange(): return lax.all_to_all(value, axes, 0, 0, tiled=True)  93.6 us
    pallas_call x12, Pallas kernels, call(): pl.pallas_call(kernel, name=name, in_specs=in_specs, out_specs=out_specs...  18.7 us
    ppermute x4, starting transfers between devices, swapped(): return lax.ppermute(value, 'c', [(0, 1), (1, 0)])  9.7 us
    ppermute x4, waiting for transfers between devices, swapped(): return lax.ppermute(value, 'c', [(0, 1), (1, 0)])  4.67 us
    ppermute x3, starting transfers between devices, partner(): return lax.ppermute(value, 'wf', [(i, i ^ distance) for i in range(4)])  4.44 us
  transfers between devices with their start and end apart: 7, of which 6 were waited for; matrix products, arithmetic and copies ran while one was open for 1% of the time, Pallas kernels for 2%

profile of v8, /device:TPU:1, one launch (start us, length us, event | category | flops | bytes accessed | tf_op | source)
XLA Modules:
  0.0 135.2 jit_solution(13249110439254979604)
XLA Ops:
  0.6 1.9 %norm.1 = (f32[4,128,128]{2,1,0:T(8,128)}, f32[2,32,128]{2,1,0:T(8,128)}, f32[296,128]{1,0:T(8,128)}, f32[40,128]{1,0:T(8,128)}, f32[296,128]{1,0:T(8,128)}) custom-call(s32[16]{0:T(128)} %left_dims.1, s32[16]{0:T(128)} %right_dims.1, f32[4,128,128]{2,1,0:T(8,128)} %guess.1), custom_call_target="tpu_custom_call" | custom-call | tf_op jit(solution)/shard_map/norm/pallas_call | solution.py:383
  2.5 3.6 %collective-permute-start.1 = (f32[40,128]{1,0:T(8,128)}, f32[40,128]{1,0:T(8,128)S(1)}, u32[]{:S(2)}, u32[]{:S(2)}) collective-permute-start(f32[40,128]{1,0:T(8,128)} %get-tuple-element.27.own), channel_id=1, source_target_pairs={{0,2},{1,3},{2,0},{3,1},{4,6},{5,7},{6,4},{7,5},{8,10},{9,11},{10,... | collective-permute-start | bytes 61448 | tf_op jit(solution)/shard_map/ppermute | solution.py:424
  6.9 0.7 broadcast_multiply_fusion
  7.6 0.7 add_bitcast_fusion
  8.4 2.3 %load.1 = (bf16[4,16,128,128]{3,2,1,0:T(8,128)(2,1)S(1)}, bf16[4,16,128,128]{3,2,1,0:T(8,128)(2,1)S(1)}) custom-call(bf16[16,4,128,128]{3,2,1,0:T(8,128)(2,1)} %left_hbm.1, bf16[16,4,128,128]{3,2,1,0:T(8,128)(2,1)} %right_hbm.1), custom_call_target="tpu_custom_call" | custom-call | tf_op jit(solution)/shard_map/load/pallas_call | solution.py:383
  11.2 1.3 collective-permute-done.2.three
  12.5 4.6 %first.1 = (f32[16,32,128]{2,1,0:T(8,128)S(1)}, f32[16,32,128]{2,1,0:T(8,128)S(1)}, f32[8,128,128]{2,1,0:T(8,128)S(1)}, f32[2,32,128]{2,1,0:T(8,128)S(1)}) custom-call(s32[64]{0:T(128)S(1)} %reshape.23.table, bf16[4,16,128,128]{3,2,1,0:T(8,128)(2,1)S(1)} %get-tuple-element.24.left, bf16[4,16,128,128]{3,2,1,0:T(8,128)(2,1)S(1)} %get-tuple-element.25.right, ...), custom_call_target="tpu_custom_call" | custom-call | tf_op jit(solution)/shard_map/first/pallas_call | solution.py:383
  17.0 2.0 %collective-permute-start.3 = (f32[16,32,128]{2,1,0:T(8,128)S(1)}, f32[16,32,128]{2,1,0:T(8,128)S(1)}, u32[]{:S(2)}, u32[]{:S(2)}) collective-permute-start(f32[16,32,128]{2,1,0:T(8,128)S(1)} %get-tuple-element.31), channel_id=1, source_target_pairs={{0,4},{4,0},{1,5},{5,1},{2,6},{6,2},{3,7},{7,3},{8,12},{12,8},{9,1... | collective-permute-start | bytes 786440 | tf_op jit(solution)/shard_map/ppermute | solution.py:427
  19.1 1.2 collective-permute-done.3.second
  20.3 19.5 %all_to_all.41.parts = bf16[16,32,128]{2,1,0:T(8,128)(2,1)S(1)} all-to-all(bf16[16,32,128]{2,1,0:T(8,128)(2,1)S(1)} %join.2), channel_id=1, replica_groups=mesh['y_far'=2,'y_near'=2,'z'=8,'c'=2,'wf'=4] {'y_far','z'}, dimensions={0} | all-to-all | bytes 262144 | tf_op jit(solution)/shard_map/all_to_all | solution.py:411
  39.8 7.8 %all_to_all.42.parts = f32[8,32,128]{2,1,0:T(8,128)S(1)} all-to-all(f32[8,32,128]{2,1,0:T(8,128)S(1)} %spread.2), channel_id=1, replica_groups=mesh['y_far'=2,'y_near'=2,'z'=8,'c'=2,'wf'=4] {'y_near','wf'}, dimensions={0} | all-to-all | bytes 262144 | tf_op jit(solution)/shard_map/all_to_all | solution.py:411
  48.0 13.6 %all_to_all.43 = f32[528,1,128]{2,1,0:T(1,128)S(1)} all-to-all(f32[528,1,128]{2,1,0:T(1,128)S(1)} %bitcast.20), channel_id=1, replica_groups=mesh['y_far'=2,'y_near'=2,'z'=8,'c'=2,'wf'=4] {'y_far','z'}, dimensions={0} | all-to-all | bytes 540672 | tf_op jit(solution)/shard_map/all_to_all | solution.py:411
  61.5 3.6 %collective-permute-start.4 = (f32[528,128]{1,0:T(8,128)S(1)}, f32[528,128]{1,0:T(8,128)S(1)}, u32[]{:S(2)}, u32[]{:S(2)}) collective-permute-start(f32[528,128]{1,0:T(8,128)S(1)} %bitcast.17), channel_id=1, source_target_pairs={{0,4},{4,0},{1,5},{5,1},{2,6},{6,2},{3,7},{7,3},{8,12},{12,8},{9,1... | collective-permute-start | bytes 811016 | tf_op jit(solution)/shard_map/ppermute | solution.py:427
  65.1 1.2 collective-permute-done.4.other
  66.3 5.0 %second.1 = (f32[16,32,128]{2,1,0:T(8,128)S(1)}, f32[16,32,128]{2,1,0:T(8,128)S(1)}, f32[8,128,128]{2,1,0:T(8,128)S(1)}, f32[8,128,128]{2,1,0:T(8,128)S(1)}, f32[8,128]{1,0:T(8,128)S(1)}) custom-call(s32[64]{0:T(128)S(1)} %reshape.23.table, bf16[4,16,128,128]{3,2,1,0:T(8,128)(2,1)S(1)} %get-tuple-element.24.left, ...), custom_call_target="tpu_custom_call" | custom-call | tf_op jit(solution)/shard_map/second/pallas_call | solution.py:383
  71.7 1.2 collective-permute-done.5.second
  72.9 12.8 %all_to_all.44.parts = bf16[16,32,128]{2,1,0:T(8,128)(2,1)S(1)} all-to-all(bf16[16,32,128]{2,1,0:T(8,128)(2,1)S(1)} %join.3), channel_id=1, replica_groups=mesh['y_far'=2,'y_near'=2,'z'=8,'c'=2,'wf'=4] {'y_far','z'}, dimensions={0} | all-to-all | bytes 262144 | tf_op jit(solution)/shard_map/all_to_all | solution.py:411
  85.7 8.0 %all_to_all.45.parts = f32[8,32,128]{2,1,0:T(8,128)S(1)} all-to-all(f32[8,32,128]{2,1,0:T(8,128)S(1)} %spread.3), channel_id=1, replica_groups=mesh['y_far'=2,'y_near'=2,'z'=8,'c'=2,'wf'=4] {'y_near','wf'}, dimensions={0} | all-to-all | bytes 262144 | tf_op jit(solution)/shard_map/all_to_all | solution.py:411
  94.3 13.5 %all_to_all.46 = f32[528,1,128]{2,1,0:T(1,128)S(1)} all-to-all(f32[528,1,128]{2,1,0:T(1,128)S(1)} %bitcast.16), channel_id=1, replica_groups=mesh['y_far'=2,'y_near'=2,'z'=8,'c'=2,'wf'=4] {'y_far','z'}, dimensions={0} | all-to-all | bytes 540672 | tf_op jit(solution)/shard_map/all_to_all | solution.py:411
  107.7 3.6 %collective-permute-start.6 = (f32[528,128]{1,0:T(8,128)S(1)}, f32[528,128]{1,0:T(8,128)S(1)}, u32[]{:S(2)}, u32[]{:S(2)}) collective-permute-start(f32[528,128]{1,0:T(8,128)S(1)} %bitcast.14), channel_id=1, source_target_pairs={{0,4},{4,0},{1,5},{5,1},{2,6},{6,2},{3,7},{7,3},{8,12},{12,8},{9,1... | collective-permute-start | bytes 811016 | tf_op jit(solution)/shard_map/ppermute | solution.py:427
  111.3 1.2 collective-permute-done.6.swapped
  112.5 3.0 %third.1 = (f32[256,128]{1,0:T(8,128)S(1)}, f32[4,128,128]{2,1,0:T(8,128)S(1)}, f32[4,128,128]{2,1,0:T(8,128)S(1)}, f32[8,128]{1,0:T(8,128)S(1)}) custom-call(s32[64]{0:T(128)S(1)} %reshape.23.table, bf16[4,16,128,128]{3,2,1,0:T(8,128)(2,1)S(1)} %get-tuple-element.24.left, bf16[4,16,128,128]{3,2,1,0:T(8,128)(2,1)S(1)} %get-tuple-element.25.right, ...), custom_call_target="tpu_custom_call" | custom-call | tf_op jit(solution)/shard_map/third/pallas_call | solution.py:383
  115.5 18.4 %all_to_all.47 = f32[256,1,128]{2,1,0:T(1,128)S(1)} all-to-all(f32[256,1,128]{2,1,0:T(1,128)S(1)} %bitcast.21), channel_id=1, replica_groups=mesh['y_far'=2,'y_near'=2,'z'=8,'c'=2,'wf'=4] {'y_far','y_near','z','c',..., dimensions={0} | all-to-all | bytes 262144 | tf_op jit(solution)/shard_map/all_to_all | solution.py:411
  134.0 1.1 last.1
  (18 shorter events, 2.9 us)
Async XLA Ops:
  2.5 8.1 %collective-permute-start.1 = (f32[40,128]{1,0:T(8,128)}, f32[40,128]{1,0:T(8,128)S(1)}, u32[]{:S(2)}, u32[]{:S(2)}) collective-permute-start(f32[40,128]{1,0:T(8,128)} %get-tuple-element.27.own), channel_id=1, source_target_pairs={{0,2},{1,3},{2,0},{3,1},{4,6},{5,7},{6,4},{7,5},{8,10},{9,11},{10,... | collective-permute-start | bytes 61448 | tf_op jit(solution)/shard_map/ppermute | solution.py:424
  6.1 5.1 %collective-permute-start = (f32[296,128]{1,0:T(8,128)}, f32[296,128]{1,0:T(8,128)S(1)}, u32[]{:S(2)}, u32[]{:S(2)}) collective-permute-start(f32[296,128]{1,0:T(8,128)} %get-tuple-element.28), channel_id=1, source_target_pairs={{0,1},{1,0},{2,3},{3,2},{4,5},{5,4},{6,7},{7,6},{8,9},{9,8},{10,11... | collective-permute-start | bytes 454664 | tf_op jit(solution)/shard_map/ppermute | solution.py:424
  6.4 6.0 %collective-permute-start.2 = (f32[296,128]{1,0:T(8,128)}, f32[296,128]{1,0:T(8,128)S(1)}, u32[]{:S(2)}, u32[]{:S(2)}) collective-permute-start(f32[296,128]{1,0:T(8,128)} %get-tuple-element.29), channel_id=1, source_target_pairs={{0,3},{1,2},{2,1},{3,0},{4,7},{5,6},{6,5},{7,4},{8,11},{9,10},{10,... | collective-permute-start | bytes 454664 | tf_op jit(solution)/shard_map/ppermute | solution.py:424
  8.4 4.1 %copy-start = (f32[4,128,128]{2,1,0:T(8,128)S(1)}, f32[4,128,128]{2,1,0:T(8,128)}, u32[]{:S(2)}) copy-start(f32[4,128,128]{2,1,0:T(8,128)} %get-tuple-element.26.start) | copy-start | bytes 786436
  8.4 4.1 %copy-start.2 = (f32[40,128]{1,0:T(8,128)S(1)}, f32[40,128]{1,0:T(8,128)}, u32[]{:S(2)}) copy-start(f32[40,128]{1,0:T(8,128)} %get-tuple-element.27.own) | copy-start | bytes 61444
  12.4 35.2 %copy-start.1 = (f32[2,32,128]{2,1,0:T(8,128)S(1)}, f32[2,32,128]{2,1,0:T(8,128)}, u32[]{:S(2)}) copy-start(f32[2,32,128]{2,1,0:T(8,128)} %get-tuple-element.32.masks) | copy-start | bytes 98308
  17.0 3.2 %collective-permute-start.3 = (f32[16,32,128]{2,1,0:T(8,128)S(1)}, f32[16,32,128]{2,1,0:T(8,128)S(1)}, u32[]{:S(2)}, u32[]{:S(2)}) collective-permute-start(f32[16,32,128]{2,1,0:T(8,128)S(1)} %get-tuple-element.31), channel_id=1, source_target_pairs={{0,4},{4,0},{1,5},{5,1},{2,6},{6,2},{3,7},{7,3},{8,12},{12,8},{9,1... | collective-permute-start | bytes 786440 | tf_op jit(solution)/shard_map/ppermute | solution.py:427
  61.5 4.8 %collective-permute-start.4 = (f32[528,128]{1,0:T(8,128)S(1)}, f32[528,128]{1,0:T(8,128)S(1)}, u32[]{:S(2)}, u32[]{:S(2)}) collective-permute-start(f32[528,128]{1,0:T(8,128)S(1)} %bitcast.17), channel_id=1, source_target_pairs={{0,4},{4,0},{1,5},{5,1},{2,6},{6,2},{3,7},{7,3},{8,12},{12,8},{9,1... | collective-permute-start | bytes 811016 | tf_op jit(solution)/shard_map/ppermute | solution.py:427
  71.3 1.6 %collective-permute-start.5 = (f32[16,32,128]{2,1,0:T(8,128)S(1)}, f32[16,32,128]{2,1,0:T(8,128)S(1)}, u32[]{:S(2)}, u32[]{:S(2)}) collective-permute-start(f32[16,32,128]{2,1,0:T(8,128)S(1)} %get-tuple-element.37), channel_id=1, source_target_pairs={{0,4},{4,0},{1,5},{5,1},{2,6},{6,2},{3,7},{7,3},{8,12},{12,8},{9,1... | collective-permute-start | bytes 786440 | tf_op jit(solution)/shard_map/ppermute | solution.py:427
  107.7 4.8 %collective-permute-start.6 = (f32[528,128]{1,0:T(8,128)S(1)}, f32[528,128]{1,0:T(8,128)S(1)}, u32[]{:S(2)}, u32[]{:S(2)}) collective-permute-start(f32[528,128]{1,0:T(8,128)S(1)} %bitcast.14), channel_id=1, source_target_pairs={{0,4},{4,0},{1,5},{5,1},{2,6},{6,2},{3,7},{7,3},{8,12},{12,8},{9,1... | collective-permute-start | bytes 811016 | tf_op jit(solution)/shard_map/ppermute | solution.py:427

commit v9 on v8

--- a/solution.py
+++ b/solution.py
@@ -20,8 +20,9 @@
 SIDE = 2 * BLOCK
 EXTRA = 8
 ENTRIES = float(SECTORS * BLOCK * BLOCK)
-LINE_AXES = ("y_far", "z")
-CROSS_AXES = ("y_near", "wf")
+LINE_AXES = ("y_near", "z")
+CROSS_AXES = ("y_far", "y_near", "wf")
+CROSS_ROWS = ((0, 3), (1, 2))
 OP_AXES = ("y_far", "y_near", "z", "c")
 
 f32 = jnp.float32
@@ -42,8 +43,12 @@
     return jnp.where(bottom > 0, top / jnp.where(bottom > 0, bottom, 1.0), 0.0)
 
 
+def half_of_line():
+    return lax.axis_index("y_near") ^ lax.axis_index("y_far")
+
+
 def place_here():
-    chunk = lax.axis_index("y_far") * lax.axis_size("z") + lax.axis_index("z")
+    chunk = half_of_line() * lax.axis_size("z") + lax.axis_index("z")
     first_row = pl.multiple_of(chunk * ROWS, ROWS)
     return lax.axis_index("wf"), HALF * lax.axis_index("c"), first_row
 
@@ -148,7 +153,11 @@
     core = lax.axis_index("c")
     for out, first in ((keep, HALF * core), (give, HALF - HALF * core)):
         for i in range(HALF):
-            out[:, i * ROWS : (i + 1) * ROWS] = sums[first + i].reshape(LINE, ROWS, BLOCK)
+            for near in range(2):
+                half = pl.multiple_of((near ^ lax.axis_index("y_far")) * (BLOCK // 2), BLOCK // 2)
+                rows = sums[first + i, pl.ds(half, BLOCK // 2)].reshape(LINE // 2, ROWS, BLOCK)
+                peers = slice(near * LINE // 2, (near + 1) * LINE // 2)
+                out[peers, i * ROWS : (i + 1) * ROWS] = rows
 
 
 def first_kernel(
@@ -242,10 +251,16 @@
     send(image, [vec_image, vec_vec, part, inner(rest, rest)], out)
 
 
+def line_rows(held, first, rows):
+    places = range(first, LINE * PACKET, PACKET)
+    parts = [held[place : place + rows] for place in places]
+    near, far = (jnp.concatenate(parts[i : i + LINE // 2], axis=0) for i in (0, LINE // 2))
+    swap = lax.axis_index("y_far") == 1
+    return jnp.concatenate([jnp.where(swap, far, near), jnp.where(swap, near, far)], axis=0)
+
+
 def both(cores, count):
-    ends = range(CHUNK, LINE * PACKET, PACKET)
-    rows = [jnp.concatenate([held[end : end + 1] for end in ends], axis=0) for held in cores]
-    return zip(*[lanes(held, count) for held in rows])
+    return zip(*[lanes(line_rows(held, CHUNK, 1), count) for held in cores])
 
 
 def add(values):
@@ -253,10 +268,7 @@
 
 
 def held_block(cores, position):
-    firsts = range(ROWS * (position % HALF), LINE * PACKET, PACKET)
-    own, other = (
-        jnp.concatenate([held[first : first + ROWS] for first in firsts], axis=0) for held in cores
-    )
+    own, other = (line_rows(held, ROWS * (position % HALF), ROWS) for held in cores)
     return jnp.where(lax.axis_index("c") == position // HALF, own, other)
 
 
@@ -407,8 +419,8 @@
     return call(kernel, name, outs, in_specs, args, scratch=scratch, limit=16)
 
 
-def exchange(value, axes):
-    return lax.all_to_all(value, axes, 0, 0, tiled=True)
+def exchange(value, axes, groups=None):
+    return lax.all_to_all(value, axes, 0, 0, axis_index_groups=groups, tiled=True)
 
 
 def shards(guess, left_ops, right_ops, op_shift, op_mask, left_dims, right_dims):
@@ -446,7 +458,8 @@
         (summed,) = small(join_kernel, "join", [sent], keep, swapped(give))
         parts = exchange(summed, LINE_AXES)
         (tiled,) = small(spread_kernel, "spread", [struct(CROSS, CHUNK, BLOCK)], parts)
-        return exchange(tiled, CROSS_AXES)
+        groups = [[4 * row + wf for row in rows for wf in range(4)] for rows in CROSS_ROWS]
+        return exchange(tiled, CROSS_AXES, groups)
 
     def gathered(packets):
         packets = exchange(packets.reshape(-1, 1, BLOCK), LINE_AXES).reshape(-1, BLOCK)

time: 136 us -> 132 us (0.971)
  blocking collectives: 93.6 us -> 89 us
    all_to_all x7, blocking collectives: 93.6 us -> 89 us  [exchange(): lax.all_to_all(value, axes, 0, 0, axis_index_groups=groups, tiled=True)]
where the time goes in v9:
time: 132 us; the launch traced here: 131 us
  blocking collectives  89 us (67%)
  Pallas kernels  18.7 us (14%)
  starting transfers between devices  14.8 us (11%)
  waiting for transfers between devices  6.46 us (5%)
  other arithmetic  1.34 us (1%)
    all_to_all x7, blocking collectives, exchange(): lax.all_to_all(value, axes, 0, 0, axis_index_groups=groups, tiled=True)  89 us
    pallas_call x12, Pallas kernels, call(): pl.pallas_call(kernel, name=name, in_specs=in_specs, out_specs=out_specs...  18.7 us
    ppermute x4, starting transfers between devices, swapped(): return lax.ppermute(value, 'c', [(0, 1), (1, 0)])  10.4 us
    ppermute x4, waiting for transfers between devices, swapped(): return lax.ppermute(value, 'c', [(0, 1), (1, 0)])  4.67 us
    ppermute x3, starting transfers between devices, partner(): return lax.ppermute(value, 'wf', [(i, i ^ distance) for i in range(4)])  4.44 us
  transfers between devices with their start and end apart: 7, of which 6 were waited for; matrix products, arithmetic and copies ran while one was open for 1% of the time, Pallas kernels for 2%

profile of v9, /device:TPU:1, one launch (start us, length us, event | category | flops | bytes accessed | tf_op | source)
XLA Modules:
  0.0 131.3 jit_solution(5310893640343953720)
XLA Ops:
  0.6 1.9 %norm.1 = (f32[4,128,128]{2,1,0:T(8,128)}, f32[2,32,128]{2,1,0:T(8,128)}, f32[296,128]{1,0:T(8,128)}, f32[40,128]{1,0:T(8,128)}, f32[296,128]{1,0:T(8,128)}) custom-call(s32[16]{0:T(128)} %left_dims.1, s32[16]{0:T(128)} %right_dims.1, f32[4,128,128]{2,1,0:T(8,128)} %guess.1), custom_call_target="tpu_custom_call" | custom-call | tf_op jit(solution)/shard_map/norm/pallas_call | solution.py:395
  2.5 3.6 %collective-permute-start.1 = (f32[40,128]{1,0:T(8,128)}, f32[40,128]{1,0:T(8,128)S(1)}, u32[]{:S(2)}, u32[]{:S(2)}) collective-permute-start(f32[40,128]{1,0:T(8,128)} %get-tuple-element.27.own), channel_id=1, source_target_pairs={{0,2},{1,3},{2,0},{3,1},{4,6},{5,7},{6,4},{7,5},{8,10},{9,11},{10,... | collective-permute-start | bytes 61448 | tf_op jit(solution)/shard_map/ppermute | solution.py:436
  6.9 0.7 broadcast_multiply_fusion
  7.6 0.7 add_bitcast_fusion
  8.4 2.3 %load.1 = (bf16[4,16,128,128]{3,2,1,0:T(8,128)(2,1)S(1)}, bf16[4,16,128,128]{3,2,1,0:T(8,128)(2,1)S(1)}) custom-call(bf16[16,4,128,128]{3,2,1,0:T(8,128)(2,1)} %left_hbm.1, bf16[16,4,128,128]{3,2,1,0:T(8,128)(2,1)} %right_hbm.1), custom_call_target="tpu_custom_call" | custom-call | tf_op jit(solution)/shard_map/load/pallas_call | solution.py:395
  11.2 1.3 collective-permute-done.2.three
  12.5 4.5 %first.1 = (f32[16,32,128]{2,1,0:T(8,128)S(1)}, f32[16,32,128]{2,1,0:T(8,128)S(1)}, f32[8,128,128]{2,1,0:T(8,128)S(1)}, f32[2,32,128]{2,1,0:T(8,128)S(1)}) custom-call(s32[64]{0:T(128)S(1)} %reshape.23.table, bf16[4,16,128,128]{3,2,1,0:T(8,128)(2,1)S(1)} %get-tuple-element.24.left, bf16[4,16,128,128]{3,2,1,0:T(8,128)(2,1)S(1)} %get-tuple-element.25.right, ...), custom_call_target="tpu_custom_call" | custom-call | tf_op jit(solution)/shard_map/first/pallas_call | solution.py:395
  17.0 2.0 %collective-permute-start.3 = (f32[16,32,128]{2,1,0:T(8,128)S(1)}, f32[16,32,128]{2,1,0:T(8,128)S(1)}, u32[]{:S(2)}, u32[]{:S(2)}) collective-permute-start(f32[16,32,128]{2,1,0:T(8,128)S(1)} %get-tuple-element.31), channel_id=1, source_target_pairs={{0,4},{4,0},{1,5},{5,1},{2,6},{6,2},{3,7},{7,3},{8,12},{12,8},{9,1... | collective-permute-start | bytes 786440 | tf_op jit(solution)/shard_map/ppermute | solution.py:439
  19.0 1.2 collective-permute-done.3.second
  20.2 16.4 %all_to_all.41.parts = bf16[16,32,128]{2,1,0:T(8,128)(2,1)S(1)} all-to-all(bf16[16,32,128]{2,1,0:T(8,128)(2,1)S(1)} %join.2), channel_id=1, replica_groups=mesh['y_far'=2,'y_near'=2,'z'=8,'c'=2,'wf'=4] {'y_near','z'}, dimensions={0} | all-to-all | bytes 262144 | tf_op jit(solution)/shard_map/all_to_all | solution.py:423
  36.6 10.2 %all_to_all.42.parts = f32[8,32,128]{2,1,0:T(8,128)S(1)} all-to-all(f32[8,32,128]{2,1,0:T(8,128)S(1)} %spread.2), channel_id=1, replica_groups={{0,1,2,3,192,193,194,195},{64,65,66,67,128,129,130,131},{4,5,6,7,196,19..., dimensions={0} | all-to-all | bytes 262144 | tf_op jit(solution)/shard_map/all_to_all | solution.py:423
  47.2 11.4 %all_to_all.43 = f32[528,1,128]{2,1,0:T(1,128)S(1)} all-to-all(f32[528,1,128]{2,1,0:T(1,128)S(1)} %bitcast.20), channel_id=1, replica_groups=mesh['y_far'=2,'y_near'=2,'z'=8,'c'=2,'wf'=4] {'y_near','z'}, dimensions={0} | all-to-all | bytes 540672 | tf_op jit(solution)/shard_map/all_to_all | solution.py:423
  58.6 4.1 %collective-permute-start.4 = (f32[528,128]{1,0:T(8,128)S(1)}, f32[528,128]{1,0:T(8,128)S(1)}, u32[]{:S(2)}, u32[]{:S(2)}) collective-permute-start(f32[528,128]{1,0:T(8,128)S(1)} %bitcast.17), channel_id=1, source_target_pairs={{0,4},{4,0},{1,5},{5,1},{2,6},{6,2},{3,7},{7,3},{8,12},{12,8},{9,1... | collective-permute-start | bytes 811016 | tf_op jit(solution)/shard_map/ppermute | solution.py:439
  62.7 1.2 collective-permute-done.4.other
  63.8 4.9 %second.1 = (f32[16,32,128]{2,1,0:T(8,128)S(1)}, f32[16,32,128]{2,1,0:T(8,128)S(1)}, f32[8,128,128]{2,1,0:T(8,128)S(1)}, f32[8,128,128]{2,1,0:T(8,128)S(1)}, f32[8,128]{1,0:T(8,128)S(1)}) custom-call(s32[64]{0:T(128)S(1)} %reshape.23.table, bf16[4,16,128,128]{3,2,1,0:T(8,128)(2,1)S(1)} %get-tuple-element.24.left, ...), custom_call_target="tpu_custom_call" | custom-call | tf_op jit(solution)/shard_map/second/pallas_call | solution.py:395
  69.2 1.2 collective-permute-done.5.second
  70.4 11.0 %all_to_all.44.parts = bf16[16,32,128]{2,1,0:T(8,128)(2,1)S(1)} all-to-all(bf16[16,32,128]{2,1,0:T(8,128)(2,1)S(1)} %join.3), channel_id=1, replica_groups=mesh['y_far'=2,'y_near'=2,'z'=8,'c'=2,'wf'=4] {'y_near','z'}, dimensions={0} | all-to-all | bytes 262144 | tf_op jit(solution)/shard_map/all_to_all | solution.py:423
  81.4 9.2 %all_to_all.45.parts = f32[8,32,128]{2,1,0:T(8,128)S(1)} all-to-all(f32[8,32,128]{2,1,0:T(8,128)S(1)} %spread.3), channel_id=1, replica_groups={{0,1,2,3,192,193,194,195},{64,65,66,67,128,129,130,131},{4,5,6,7,196,19..., dimensions={0} | all-to-all | bytes 262144 | tf_op jit(solution)/shard_map/all_to_all | solution.py:423
  91.2 11.6 %all_to_all.46 = f32[528,1,128]{2,1,0:T(1,128)S(1)} all-to-all(f32[528,1,128]{2,1,0:T(1,128)S(1)} %bitcast.16), channel_id=1, replica_groups=mesh['y_far'=2,'y_near'=2,'z'=8,'c'=2,'wf'=4] {'y_near','z'}, dimensions={0} | all-to-all | bytes 540672 | tf_op jit(solution)/shard_map/all_to_all | solution.py:423
  102.8 3.8 %collective-permute-start.6 = (f32[528,128]{1,0:T(8,128)S(1)}, f32[528,128]{1,0:T(8,128)S(1)}, u32[]{:S(2)}, u32[]{:S(2)}) collective-permute-start(f32[528,128]{1,0:T(8,128)S(1)} %bitcast.14), channel_id=1, source_target_pairs={{0,4},{4,0},{1,5},{5,1},{2,6},{6,2},{3,7},{7,3},{8,12},{12,8},{9,1... | collective-permute-start | bytes 811016 | tf_op jit(solution)/shard_map/ppermute | solution.py:439
  106.7 1.2 collective-permute-done.6.swapped
  107.8 3.1 %third.1 = (f32[256,128]{1,0:T(8,128)S(1)}, f32[4,128,128]{2,1,0:T(8,128)S(1)}, f32[4,128,128]{2,1,0:T(8,128)S(1)}, f32[8,128]{1,0:T(8,128)S(1)}) custom-call(s32[64]{0:T(128)S(1)} %reshape.23.table, bf16[4,16,128,128]{3,2,1,0:T(8,128)(2,1)S(1)} %get-tuple-element.24.left, bf16[4,16,128,128]{3,2,1,0:T(8,128)(2,1)S(1)} %get-tuple-element.25.right, ...), custom_call_target="tpu_custom_call" | custom-call | tf_op jit(solution)/shard_map/third/pallas_call | solution.py:395
  110.9 19.1 %all_to_all.47 = f32[256,1,128]{2,1,0:T(1,128)S(1)} all-to-all(f32[256,1,128]{2,1,0:T(1,128)S(1)} %bitcast.21), channel_id=1, replica_groups=mesh['y_far'=2,'y_near'=2,'z'=8,'c'=2,'wf'=4] {'y_far','y_near','z','c',..., dimensions={0} | all-to-all | bytes 262144 | tf_op jit(solution)/shard_map/all_to_all | solution.py:423
  130.0 1.1 last.1
  (18 shorter events, 2.9 us)
Async XLA Ops:
  2.5 8.1 %collective-permute-start.1 = (f32[40,128]{1,0:T(8,128)}, f32[40,128]{1,0:T(8,128)S(1)}, u32[]{:S(2)}, u32[]{:S(2)}) collective-permute-start(f32[40,128]{1,0:T(8,128)} %get-tuple-element.27.own), channel_id=1, source_target_pairs={{0,2},{1,3},{2,0},{3,1},{4,6},{5,7},{6,4},{7,5},{8,10},{9,11},{10,... | collective-permute-start | bytes 61448 | tf_op jit(solution)/shard_map/ppermute | solution.py:436
  6.1 5.1 %collective-permute-start = (f32[296,128]{1,0:T(8,128)}, f32[296,128]{1,0:T(8,128)S(1)}, u32[]{:S(2)}, u32[]{:S(2)}) collective-permute-start(f32[296,128]{1,0:T(8,128)} %get-tuple-element.28), channel_id=1, source_target_pairs={{0,1},{1,0},{2,3},{3,2},{4,5},{5,4},{6,7},{7,6},{8,9},{9,8},{10,11... | collective-permute-start | bytes 454664 | tf_op jit(solution)/shard_map/ppermute | solution.py:436
  6.4 6.0 %collective-permute-start.2 = (f32[296,128]{1,0:T(8,128)}, f32[296,128]{1,0:T(8,128)S(1)}, u32[]{:S(2)}, u32[]{:S(2)}) collective-permute-start(f32[296,128]{1,0:T(8,128)} %get-tuple-element.29), channel_id=1, source_target_pairs={{0,3},{1,2},{2,1},{3,0},{4,7},{5,6},{6,5},{7,4},{8,11},{9,10},{10,... | collective-permute-start | bytes 454664 | tf_op jit(solution)/shard_map/ppermute | solution.py:436
  8.4 4.1 %copy-start = (f32[4,128,128]{2,1,0:T(8,128)S(1)}, f32[4,128,128]{2,1,0:T(8,128)}, u32[]{:S(2)}) copy-start(f32[4,128,128]{2,1,0:T(8,128)} %get-tuple-element.26.start) | copy-start | bytes 786436
  8.4 4.1 %copy-start.2 = (f32[40,128]{1,0:T(8,128)S(1)}, f32[40,128]{1,0:T(8,128)}, u32[]{:S(2)}) copy-start(f32[40,128]{1,0:T(8,128)} %get-tuple-element.27.own) | copy-start | bytes 61444
  12.4 34.4 %copy-start.1 = (f32[2,32,128]{2,1,0:T(8,128)S(1)}, f32[2,32,128]{2,1,0:T(8,128)}, u32[]{:S(2)}) copy-start(f32[2,32,128]{2,1,0:T(8,128)} %get-tuple-element.32.masks) | copy-start | bytes 98308
  17.0 3.2 %collective-permute-start.3 = (f32[16,32,128]{2,1,0:T(8,128)S(1)}, f32[16,32,128]{2,1,0:T(8,128)S(1)}, u32[]{:S(2)}, u32[]{:S(2)}) collective-permute-start(f32[16,32,128]{2,1,0:T(8,128)S(1)} %get-tuple-element.31), channel_id=1, source_target_pairs={{0,4},{4,0},{1,5},{5,1},{2,6},{6,2},{3,7},{7,3},{8,12},{12,8},{9,1... | collective-permute-start | bytes 786440 | tf_op jit(solution)/shard_map/ppermute | solution.py:439
  58.6 5.3 %collective-permute-start.4 = (f32[528,128]{1,0:T(8,128)S(1)}, f32[528,128]{1,0:T(8,128)S(1)}, u32[]{:S(2)}, u32[]{:S(2)}) collective-permute-start(f32[528,128]{1,0:T(8,128)S(1)} %bitcast.17), channel_id=1, source_target_pairs={{0,4},{4,0},{1,5},{5,1},{2,6},{6,2},{3,7},{7,3},{8,12},{12,8},{9,1... | collective-permute-start | bytes 811016 | tf_op jit(solution)/shard_map/ppermute | solution.py:439
  68.7 1.6 %collective-permute-start.5 = (f32[16,32,128]{2,1,0:T(8,128)S(1)}, f32[16,32,128]{2,1,0:T(8,128)S(1)}, u32[]{:S(2)}, u32[]{:S(2)}) collective-permute-start(f32[16,32,128]{2,1,0:T(8,128)S(1)} %get-tuple-element.37), channel_id=1, source_target_pairs={{0,4},{4,0},{1,5},{5,1},{2,6},{6,2},{3,7},{7,3},{8,12},{12,8},{9,1... | collective-permute-start | bytes 786440 | tf_op jit(solution)/shard_map/ppermute | solution.py:439
  102.8 5.0 %collective-permute-start.6 = (f32[528,128]{1,0:T(8,128)S(1)}, f32[528,128]{1,0:T(8,128)S(1)}, u32[]{:S(2)}, u32[]{:S(2)}) collective-permute-start(f32[528,128]{1,0:T(8,128)S(1)} %bitcast.14), channel_id=1, source_target_pairs={{0,4},{4,0},{1,5},{5,1},{2,6},{6,2},{3,7},{7,3},{8,12},{12,8},{9,1... | collective-permute-start | bytes 811016 | tf_op jit(solution)/shard_map/ppermute | solution.py:439

commit v10 on v9

--- a/solution.py
+++ b/solution.py
@@ -20,10 +20,10 @@
 SIDE = 2 * BLOCK
 EXTRA = 8
 ENTRIES = float(SECTORS * BLOCK * BLOCK)
-LINE_AXES = ("y_near", "z")
-CROSS_AXES = ("y_far", "y_near", "wf")
+ALL_AXES = ("y", "z", "c", "wf")
+LINE_ROWS = ((0, 1), (3, 2))
 CROSS_ROWS = ((0, 3), (1, 2))
-OP_AXES = ("y_far", "y_near", "z", "c")
+OP_AXES = ("y", "z", "c")
 
 f32 = jnp.float32
 bf16 = jnp.bfloat16
@@ -43,14 +43,16 @@
     return jnp.where(bottom > 0, top / jnp.where(bottom > 0, bottom, 1.0), 0.0)
 
 
-def half_of_line():
-    return lax.axis_index("y_near") ^ lax.axis_index("y_far")
+def line_order(core):
+    return [(half, z) for half in range(2) for z in range(8)]
 
 
 def place_here():
-    chunk = half_of_line() * lax.axis_size("z") + lax.axis_index("z")
+    y, z, core = (lax.axis_index(axis) for axis in OP_AXES)
+    half = (y ^ (y // 2)) & 1
+    chunk = half * 8 + z
     first_row = pl.multiple_of(chunk * ROWS, ROWS)
-    return lax.axis_index("wf"), HALF * lax.axis_index("c"), first_row
+    return lax.axis_index("wf"), HALF * core, first_row
 
 
 def sector_at(wf, position):
@@ -114,11 +116,10 @@
             masks[i, k * ROWS : (k + 1) * ROWS] = jnp.where(mask, 1.0, 0.0)
 
 
-def half_step(table, left, right, vec_half, back, sector, index):
+def half_step(shift, mask, left, right, vec_half, back, sector, index):
     for k in range(PAIRS):
-        entry = table[index * PAIRS + k]
-        position = (sector + (entry >> 1)) & 7
-        weight = (entry & 1).astype(f32)
+        position = (sector + shift[k]) & 7
+        weight = mask[index, k].astype(f32)
         value = dot(left[index, k].T, vec_half[position])
         back[index & 1, :, k * BLOCK : (k + 1) * BLOCK] = (value * weight).astype(bf16)
     return dot(back[index & 1], right[index].reshape(PAIRS * BLOCK, BLOCK))
@@ -134,7 +135,7 @@
     return dot(jnp.concatenate(blocks, axis=1), jnp.concatenate(rows, axis=0))
 
 
-def full_sweep(table, left, right, vec_half, back, sums, keep, give):
+def full_sweep(shift, mask, left, right, vec_half, back, sums, keep, give):
     sums[...] = jnp.zeros_like(sums)
     first_sector = OWN * lax.axis_index("wf")
     for pair in range(0, OWN, 2):
@@ -142,26 +143,22 @@
         for i in range(2):
             sector, index = first_sector + pair + i, pair + i
             for k in range(PAIRS):
-                entry = table[index * PAIRS + k]
-                position = (sector + (entry >> 1)) & 7
-                weight = (entry & 1).astype(f32)
+                position = (sector + shift[k]) & 7
+                weight = mask[index, k].astype(f32)
                 value = middle[k * BLOCK : (k + 1) * BLOCK, i * BLOCK : (i + 1) * BLOCK]
                 sums[position] += dot((value * weight).astype(bf16), right[index, k], 1, 1)
         for i in range(2):
             sector, index = first_sector + pair + i, pair + i
-            sums[sector & 7] += half_step(table, left, right, vec_half, back, sector, index)
+            sums[sector & 7] += half_step(shift, mask, left, right, vec_half, back, sector, index)
     core = lax.axis_index("c")
     for out, first in ((keep, HALF * core), (give, HALF - HALF * core)):
         for i in range(HALF):
-            for near in range(2):
-                half = pl.multiple_of((near ^ lax.axis_index("y_far")) * (BLOCK // 2), BLOCK // 2)
-                rows = sums[first + i, pl.ds(half, BLOCK // 2)].reshape(LINE // 2, ROWS, BLOCK)
-                peers = slice(near * LINE // 2, (near + 1) * LINE // 2)
-                out[peers, i * ROWS : (i + 1) * ROWS] = rows
+            rows = sums[first + i].reshape(LINE, ROWS, BLOCK)
+            out[:, i * ROWS : (i + 1) * ROWS] = rows
 
 
 def first_kernel(
-    table, left, right, start, own, one, two, three, keep, give, vector, pieces,
+    shift, mask, left, right, start, own, one, two, three, keep, give, vector, pieces,
     vec_half, back, sums,
 ):
     wf = lax.axis_index("wf")
@@ -191,7 +188,7 @@
         for other in range(1, 4):
             value = jnp.where(source == other, held[other], value)
         pieces[place] = value * scale
-    full_sweep(table, left, right, vec_half, back, sums, keep, give)
+    full_sweep(shift, mask, left, right, vec_half, back, sums, keep, give)
 
 
 def join_kernel(first, second, out):
@@ -253,10 +250,7 @@
 
 def line_rows(held, first, rows):
     places = range(first, LINE * PACKET, PACKET)
-    parts = [held[place : place + rows] for place in places]
-    near, far = (jnp.concatenate(parts[i : i + LINE // 2], axis=0) for i in (0, LINE // 2))
-    swap = lax.axis_index("y_far") == 1
-    return jnp.concatenate([jnp.where(swap, far, near), jnp.where(swap, near, far)], axis=0)
+    return jnp.concatenate([held[place : place + rows] for place in places], axis=0)
 
 
 def both(cores, count):
@@ -273,7 +267,7 @@
 
 
 def second_kernel(
-    table, left, right, own, other, vector, keep, give, direction, image, scalars,
+    shift, mask, left, right, own, other, vector, keep, give, direction, image, scalars,
     vec_half, back, sums,
 ):
     cores = (own, other)
@@ -289,7 +283,7 @@
         image[position] = held
         direction[position] = value
         vec_half[position] = value.astype(bf16)
-    full_sweep(table, left, right, vec_half, back, sums, keep, give)
+    full_sweep(shift, mask, left, right, vec_half, back, sums, keep, give)
 
 
 def turned_kernel(parts, masks, pieces, image_pieces, scalars, out):
@@ -328,7 +322,7 @@
 
 
 def third_kernel(
-    table, left, right, gathered, swapped, vector, direction, image, scalars,
+    shift, mask, left, right, gathered, swapped, vector, direction, image, scalars,
     out, new_vector, new_direction, new_scalars, vec_half, back,
 ):
     cores = (gathered, swapped)
@@ -366,7 +360,7 @@
 
     value = jnp.zeros((1, 1), f32)
     for i in range(OWN):
-        half = half_step(table, left, right, vec_half, back, OWN * wf + i, i)
+        half = half_step(shift, mask, left, right, vec_half, back, OWN * wf + i, i)
         value = value + total(half * new_direction[i])
     out[...] = jnp.broadcast_to(2.0 * value, out.shape)
 
@@ -415,12 +409,30 @@
     if sums:
         scratch.append(pltpu.VMEM((WINDOW, BLOCK, BLOCK), f32))
     args = (*operators, *arrays)
-    in_specs = [SMEM] + [VMEM] * (len(args) - 1)
+    in_specs = [SMEM] * 2 + [VMEM] * (len(args) - 2)
     return call(kernel, name, outs, in_specs, args, scratch=scratch, limit=16)
 
 
-def exchange(value, axes, groups=None):
-    return lax.all_to_all(value, axes, 0, 0, axis_index_groups=groups, tiled=True)
+def device(y, z, core, wf):
+    return ((y * 8 + z) * 2 + core) * 4 + wf
+
+
+LINE_GROUPS = [
+    [device(rows[half], z, core, wf) for half, z in line_order(core)]
+    for rows in LINE_ROWS
+    for core in range(2)
+    for wf in range(4)
+]
+CROSS_GROUPS = [
+    [device(y, z, core, wf) for y in rows for wf in range(4)]
+    for rows in CROSS_ROWS
+    for z in range(8)
+    for core in range(2)
+]
+
+
+def exchange(value, groups=None):
+    return lax.all_to_all(value, ALL_AXES, 0, 0, axis_index_groups=groups, tiled=True)
 
 
 def shards(guess, left_ops, right_ops, op_shift, op_mask, left_dims, right_dims):
@@ -438,7 +450,6 @@
     def swapped(value):
         return lax.ppermute(value, "c", [(0, 1), (1, 0)])
 
-    table = (2 * op_shift[None, :] + op_mask.T).reshape(-1)
     tail = EXTRA + CHUNK
     start, masks, one, own, three = call(
         norm_kernel, "norm",
@@ -446,23 +457,22 @@
          struct(SIDE + tail, BLOCK)],
         [SMEM, SMEM, VMEM], (left_dims, right_dims, guess), limit=60,
     )
-    one, two, three = partner(one, 1), partner(own, 2), partner(three, 3)
+    three, one, two = partner(three, 3), partner(one, 1), partner(own, 2)
     held = struct(OWN, PAIRS, BLOCK, BLOCK, dtype=bf16)
     left, right = call(
         load_kernel, "load", [held, held], [HBM, HBM], (left_ops, right_ops),
         scratch=[pltpu.SemaphoreType.DMA((2 * OWN,))], limit=49,
     )
-    operators = (table, left, right)
+    operators = (op_shift, op_mask.T, left, right)
 
     def reduced(keep, give):
         (summed,) = small(join_kernel, "join", [sent], keep, swapped(give))
-        parts = exchange(summed, LINE_AXES)
+        parts = exchange(summed, LINE_GROUPS)
         (tiled,) = small(spread_kernel, "spread", [struct(CROSS, CHUNK, BLOCK)], parts)
-        groups = [[4 * row + wf for row in rows for wf in range(4)] for rows in CROSS_ROWS]
-        return exchange(tiled, CROSS_AXES, groups)
+        return exchange(tiled, CROSS_GROUPS)
 
     def gathered(packets):
-        packets = exchange(packets.reshape(-1, 1, BLOCK), LINE_AXES).reshape(-1, BLOCK)
+        packets = exchange(packets.reshape(-1, 1, BLOCK), LINE_GROUPS).reshape(-1, BLOCK)
         return packets, swapped(packets)
 
     keep, give, vector, pieces = step(
@@ -483,7 +493,7 @@
         third_kernel, "third", [struct(256, BLOCK), own_blocks, own_blocks, scalar_row], operators,
         (*gathered(packets), vector, direction, image, scalars), sums=False,
     )
-    sums = exchange(sums, (*OP_AXES, "wf"))
+    sums = exchange(sums)
     result, energies = small(
         last_kernel, "last", [own_blocks, struct(2)], sums, vector, direction, scalars,
         out_specs=[VMEM, SMEM],
@@ -492,7 +502,7 @@
 
 
 def solution(mesh):
-    split = Mesh(mesh.devices.reshape(2, 2, 8, 2, 4), (*OP_AXES, "wf"))
+    split = Mesh(mesh.devices.reshape(4, 8, 2, 4), (*OP_AXES, "wf"))
     in_specs = (
         P("wf", None, None),
         P(OP_AXES, "wf", None, None),

time: 132 us -> 131 us (level)
  other arithmetic: 1.34 us -> 0 us
  transfers between devices with their start and end apart: 7 -> 7, of which waited for: 6 -> 5; matrix products, arithmetic and copies ran while one was open for 1% -> 0% of each run, Pallas kernels for 2% -> 2%
where the time goes in v10:
time: 131 us; the launch traced here: 130 us
  blocking collectives  88.8 us (68%)
  Pallas kernels  18.8 us (14%)
  starting transfers between devices  15.5 us (12%)
  waiting for transfers between devices  6.4 us (5%)
    all_to_all x7, blocking collectives, exchange(): lax.all_to_all(value, ALL_AXES, 0, 0, axis_index_groups=groups, tiled=True)  88.8 us
    pallas_call x12, Pallas kernels, call(): pl.pallas_call(kernel, name=name, in_specs=in_specs, out_specs=out_specs...  18.8 us
    ppermute x4, starting transfers between devices, swapped(): return lax.ppermute(value, 'c', [(0, 1), (1, 0)])  10.9 us
    ppermute x4, waiting for transfers between devices, swapped(): return lax.ppermute(value, 'c', [(0, 1), (1, 0)])  4.67 us
    ppermute x3, starting transfers between devices, partner(): return lax.ppermute(value, 'wf', [(i, i ^ distance) for i in range(4)])  4.59 us
  transfers between devices with their start and end apart: 7, of which 5 were waited for; matrix products, arithmetic and copies ran while one was open for 0% of the time, Pallas kernels for 2%

profile of v10, /device:TPU:1, one launch (start us, length us, event | category | flops | bytes accessed | tf_op | source)
XLA Modules:
  0.0 130.3 jit_solution(1792011187094040165)
XLA Ops:
  0.6 1.9 %norm.1 = (f32[4,128,128]{2,1,0:T(8,128)}, f32[2,32,128]{2,1,0:T(8,128)}, f32[296,128]{1,0:T(8,128)}, f32[40,128]{1,0:T(8,128)}, f32[296,128]{1,0:T(8,128)}) custom-call(s32[16]{0:T(128)} %left_dims.1, s32[16]{0:T(128)} %right_dims.1, f32[4,128,128]{2,1,0:T(8,128)} %guess.1), custom_call_target="tpu_custom_call" | custom-call | tf_op jit(solution)/shard_map/norm/pallas_call | solution.py:389
  2.5 2.0 %collective-permute-start = (f32[296,128]{1,0:T(8,128)}, f32[296,128]{1,0:T(8,128)S(1)}, u32[]{:S(2)}, u32[]{:S(2)}) collective-permute-start(f32[296,128]{1,0:T(8,128)} %get-tuple-element.28), channel_id=1, source_target_pairs={{0,1},{1,0},{2,3},{3,2},{4,5},{5,4},{6,7},{7,6},{8,9},{9,8},{10,11... | collective-permute-start | bytes 454664 | tf_op jit(solution)/shard_map/ppermute | solution.py:448
  4.6 1.8 %collective-permute-start.2 = (f32[296,128]{1,0:T(8,128)}, f32[296,128]{1,0:T(8,128)S(1)}, u32[]{:S(2)}, u32[]{:S(2)}) collective-permute-start(f32[296,128]{1,0:T(8,128)} %get-tuple-element.29), channel_id=1, source_target_pairs={{0,3},{1,2},{2,1},{3,0},{4,7},{5,6},{6,5},{7,4},{8,11},{9,10},{10,... | collective-permute-start | bytes 454664 | tf_op jit(solution)/shard_map/ppermute | solution.py:448
  6.4 0.7 collective-permute-start.1
  7.1 2.2 %load.1 = (bf16[4,16,128,128]{3,2,1,0:T(8,128)(2,1)S(1)}, bf16[4,16,128,128]{3,2,1,0:T(8,128)(2,1)S(1)}) custom-call(bf16[16,4,128,128]{3,2,1,0:T(8,128)(2,1)} %left_hbm.1, bf16[16,4,128,128]{3,2,1,0:T(8,128)(2,1)} %right_hbm.1), custom_call_target="tpu_custom_call" | custom-call | tf_op jit(solution)/shard_map/load/pallas_call | solution.py:389
  9.4 1.7 %collective-permute-done.1.two = f32[40,128]{1,0:T(8,128)S(1)} collective-permute-done((f32[40,128]{1,0:T(8,128)}, f32[40,128]{1,0:T(8,128)S(1)}, u32[]{:S(2)}, u32[]{:S(2)}) %collective-permute-start.1) | collective-permute-done | bytes 20512 | tf_op jit(solution)/shard_map/ppermute | solution.py:448
  11.1 4.6 %first.1 = (f32[16,32,128]{2,1,0:T(8,128)S(1)}, f32[16,32,128]{2,1,0:T(8,128)S(1)}, f32[8,128,128]{2,1,0:T(8,128)S(1)}, f32[2,32,128]{2,1,0:T(8,128)S(1)}) custom-call(s32[16]{0:T(128)S(1)} %copy-done.4, s32[4,16]{1,0:T(4,128)S(1)} %bitcast.21, bf16[4,16,128,128]{3,2,1,0:T(8,128)(2,1)S(1)} %get-tuple-element.24.left, ...), custom_call_target="tpu_custom_call" | custom-call | tf_op jit(solution)/shard_map/first/pallas_call | solution.py:389
  15.8 2.2 %collective-permute-start.3 = (f32[16,32,128]{2,1,0:T(8,128)S(1)}, f32[16,32,128]{2,1,0:T(8,128)S(1)}, u32[]{:S(2)}, u32[]{:S(2)}) collective-permute-start(f32[16,32,128]{2,1,0:T(8,128)S(1)} %get-tuple-element.31), channel_id=1, source_target_pairs={{0,4},{4,0},{1,5},{5,1},{2,6},{6,2},{3,7},{7,3},{8,12},{12,8},{9,1... | collective-permute-start | bytes 786440 | tf_op jit(solution)/shard_map/ppermute | solution.py:451
  18.0 1.2 collective-permute-done.3.second
  19.2 16.5 %all_to_all.41.parts = bf16[16,32,128]{2,1,0:T(8,128)(2,1)S(1)} all-to-all(bf16[16,32,128]{2,1,0:T(8,128)(2,1)S(1)} %join.2), channel_id=1, replica_groups={{0,8,16,24,32,40,48,56,64,72,80,88,96,104,112,120},{1,9,17,25,33,41,49,..., dimensions={0} | all-to-all | bytes 262144 | tf_op jit(solution)/shard_map/all_to_all | solution.py:435
  35.8 10.7 %all_to_all.42.parts = f32[8,32,128]{2,1,0:T(8,128)S(1)} all-to-all(f32[8,32,128]{2,1,0:T(8,128)S(1)} %spread.2), channel_id=1, replica_groups={{0,1,2,3,192,193,194,195},{4,5,6,7,196,197,198,199},{8,9,10,11,200,201,..., dimensions={0} | all-to-all | bytes 262144 | tf_op jit(solution)/shard_map/all_to_all | solution.py:435
  46.8 11.5 %all_to_all.43 = f32[528,1,128]{2,1,0:T(1,128)S(1)} all-to-all(f32[528,1,128]{2,1,0:T(1,128)S(1)} %bitcast.19), channel_id=1, replica_groups={{0,8,16,24,32,40,48,56,64,72,80,88,96,104,112,120},{1,9,17,25,33,41,49,..., dimensions={0} | all-to-all | bytes 540672 | tf_op jit(solution)/shard_map/all_to_all | solution.py:435
  58.2 4.2 %collective-permute-start.4 = (f32[528,128]{1,0:T(8,128)S(1)}, f32[528,128]{1,0:T(8,128)S(1)}, u32[]{:S(2)}, u32[]{:S(2)}) collective-permute-start(f32[528,128]{1,0:T(8,128)S(1)} %bitcast.13), channel_id=1, source_target_pairs={{0,4},{4,0},{1,5},{5,1},{2,6},{6,2},{3,7},{7,3},{8,12},{12,8},{9,1... | collective-permute-start | bytes 811016 | tf_op jit(solution)/shard_map/ppermute | solution.py:451
  62.4 1.2 collective-permute-done.4.other
  63.6 4.9 %second.1 = (f32[16,32,128]{2,1,0:T(8,128)S(1)}, f32[16,32,128]{2,1,0:T(8,128)S(1)}, f32[8,128,128]{2,1,0:T(8,128)S(1)}, f32[8,128,128]{2,1,0:T(8,128)S(1)}, f32[8,128]{1,0:T(8,128)S(1)}) custom-call(s32[16]{0:T(128)S(1)} %copy-done.4, s32[4,16]{1,0:T(4,128)S(1)} %bitcast.22, bf16[4,16,128,128]{3,2,1,0:T(8,128)(2,1)S(1)} %get-tuple-element.24.left, ...), custom_call_target="tpu_custom_call" | custom-call | tf_op jit(solution)/shard_map/second/pallas_call | solution.py:389
  69.0 1.2 collective-permute-done.5.second
  70.2 11.1 %all_to_all.44.parts = bf16[16,32,128]{2,1,0:T(8,128)(2,1)S(1)} all-to-all(bf16[16,32,128]{2,1,0:T(8,128)(2,1)S(1)} %join.3), channel_id=1, replica_groups={{0,8,16,24,32,40,48,56,64,72,80,88,96,104,112,120},{1,9,17,25,33,41,49,..., dimensions={0} | all-to-all | bytes 262144 | tf_op jit(solution)/shard_map/all_to_all | solution.py:435
  81.3 9.1 %all_to_all.45.parts = f32[8,32,128]{2,1,0:T(8,128)S(1)} all-to-all(f32[8,32,128]{2,1,0:T(8,128)S(1)} %spread.3), channel_id=1, replica_groups={{0,1,2,3,192,193,194,195},{4,5,6,7,196,197,198,199},{8,9,10,11,200,201,..., dimensions={0} | all-to-all | bytes 262144 | tf_op jit(solution)/shard_map/all_to_all | solution.py:435
  91.0 11.5 %all_to_all.46 = f32[528,1,128]{2,1,0:T(1,128)S(1)} all-to-all(f32[528,1,128]{2,1,0:T(1,128)S(1)} %bitcast.15), channel_id=1, replica_groups={{0,8,16,24,32,40,48,56,64,72,80,88,96,104,112,120},{1,9,17,25,33,41,49,..., dimensions={0} | all-to-all | bytes 540672 | tf_op jit(solution)/shard_map/all_to_all | solution.py:435
  102.6 4.0 %collective-permute-start.6 = (f32[528,128]{1,0:T(8,128)S(1)}, f32[528,128]{1,0:T(8,128)S(1)}, u32[]{:S(2)}, u32[]{:S(2)}) collective-permute-start(f32[528,128]{1,0:T(8,128)S(1)} %bitcast.16), channel_id=1, source_target_pairs={{0,4},{4,0},{1,5},{5,1},{2,6},{6,2},{3,7},{7,3},{8,12},{12,8},{9,1... | collective-permute-start | bytes 811016 | tf_op jit(solution)/shard_map/ppermute | solution.py:451
  106.6 1.2 collective-permute-done.6.swapped
  107.8 3.0 %third.1 = (f32[256,128]{1,0:T(8,128)S(1)}, f32[4,128,128]{2,1,0:T(8,128)S(1)}, f32[4,128,128]{2,1,0:T(8,128)S(1)}, f32[8,128]{1,0:T(8,128)S(1)}) custom-call(s32[16]{0:T(128)S(1)} %copy-done.4, s32[4,16]{1,0:T(4,128)S(1)} %bitcast.23, bf16[4,16,128,128]{3,2,1,0:T(8,128)(2,1)S(1)} %get-tuple-element.24.left, ...), custom_call_target="tpu_custom_call" | custom-call | tf_op jit(solution)/shard_map/third/pallas_call | solution.py:389
  110.8 18.3 %all_to_all.47 = f32[256,1,128]{2,1,0:T(1,128)S(1)} all-to-all(f32[256,1,128]{2,1,0:T(1,128)S(1)} %bitcast.20), channel_id=1, replica_groups=mesh['y'=4,'z'=8,'c'=2,'wf'=4] {'y','z','c','wf'}, dimensions={0} | all-to-all | bytes 262144 | tf_op jit(solution)/shard_map/all_to_all | solution.py:435
  129.1 1.1 last.1
  (19 shorter events, 1.4 us)
Async XLA Ops:
  2.5 8.6 %collective-permute-start = (f32[296,128]{1,0:T(8,128)}, f32[296,128]{1,0:T(8,128)S(1)}, u32[]{:S(2)}, u32[]{:S(2)}) collective-permute-start(f32[296,128]{1,0:T(8,128)} %get-tuple-element.28), channel_id=1, source_target_pairs={{0,1},{1,0},{2,3},{3,2},{4,5},{5,4},{6,7},{7,6},{8,9},{9,8},{10,11... | collective-permute-start | bytes 454664 | tf_op jit(solution)/shard_map/ppermute | solution.py:448
  4.6 6.5 %collective-permute-start.2 = (f32[296,128]{1,0:T(8,128)}, f32[296,128]{1,0:T(8,128)S(1)}, u32[]{:S(2)}, u32[]{:S(2)}) collective-permute-start(f32[296,128]{1,0:T(8,128)} %get-tuple-element.29), channel_id=1, source_target_pairs={{0,3},{1,2},{2,1},{3,0},{4,7},{5,6},{6,5},{7,4},{8,11},{9,10},{10,... | collective-permute-start | bytes 454664 | tf_op jit(solution)/shard_map/ppermute | solution.py:448
  6.4 4.7 %copy-start = (f32[4,128,128]{2,1,0:T(8,128)S(1)}, f32[4,128,128]{2,1,0:T(8,128)}, u32[]{:S(2)}) copy-start(f32[4,128,128]{2,1,0:T(8,128)} %get-tuple-element.26.start) | copy-start | bytes 786436
  6.4 4.7 %copy-start.2 = (f32[40,128]{1,0:T(8,128)S(1)}, f32[40,128]{1,0:T(8,128)}, u32[]{:S(2)}) copy-start(f32[40,128]{1,0:T(8,128)} %get-tuple-element.27.own) | copy-start | bytes 61444
  6.4 4.7 %copy-start.3 = (s32[16,4]{0,1:T(4,128)S(1)}, s32[16,4]{0,1:T(4,128)}, u32[]{:S(2)}) copy-start(s32[16,4]{0,1:T(4,128)} %param.11) | copy-start | bytes 772
  6.4 4.7 %copy-start.4 = (s32[16]{0:T(128)S(1)}, s32[16]{0:T(128)}, u32[]{:S(2)}) copy-start(s32[16]{0:T(128)} %shift.5) | copy-start | bytes 196
  6.4 4.7 %collective-permute-start.1 = (f32[40,128]{1,0:T(8,128)}, f32[40,128]{1,0:T(8,128)S(1)}, u32[]{:S(2)}, u32[]{:S(2)}) collective-permute-start(f32[40,128]{1,0:T(8,128)} %get-tuple-element.27.own), channel_id=1, source_target_pairs={{0,2},{1,3},{2,0},{3,1},{4,6},{5,7},{6,4},{7,5},{8,10},{9,11},{10,... | collective-permute-start | bytes 61448 | tf_op jit(solution)/shard_map/ppermute | solution.py:448
  11.1 35.3 %copy-start.1 = (f32[2,32,128]{2,1,0:T(8,128)S(1)}, f32[2,32,128]{2,1,0:T(8,128)}, u32[]{:S(2)}) copy-start(f32[2,32,128]{2,1,0:T(8,128)} %get-tuple-element.32.masks) | copy-start | bytes 98308
  15.8 3.4 %collective-permute-start.3 = (f32[16,32,128]{2,1,0:T(8,128)S(1)}, f32[16,32,128]{2,1,0:T(8,128)S(1)}, u32[]{:S(2)}, u32[]{:S(2)}) collective-permute-start(f32[16,32,128]{2,1,0:T(8,128)S(1)} %get-tuple-element.31), channel_id=1, source_target_pairs={{0,4},{4,0},{1,5},{5,1},{2,6},{6,2},{3,7},{7,3},{8,12},{12,8},{9,1... | collective-permute-start | bytes 786440 | tf_op jit(solution)/shard_map/ppermute | solution.py:451
  58.2 5.4 %collective-permute-start.4 = (f32[528,128]{1,0:T(8,128)S(1)}, f32[528,128]{1,0:T(8,128)S(1)}, u32[]{:S(2)}, u32[]{:S(2)}) collective-permute-start(f32[528,128]{1,0:T(8,128)S(1)} %bitcast.13), channel_id=1, source_target_pairs={{0,4},{4,0},{1,5},{5,1},{2,6},{6,2},{3,7},{7,3},{8,12},{12,8},{9,1... | collective-permute-start | bytes 811016 | tf_op jit(solution)/shard_map/ppermute | solution.py:451
  68.6 1.6 %collective-permute-start.5 = (f32[16,32,128]{2,1,0:T(8,128)S(1)}, f32[16,32,128]{2,1,0:T(8,128)S(1)}, u32[]{:S(2)}, u32[]{:S(2)}) collective-permute-start(f32[16,32,128]{2,1,0:T(8,128)S(1)} %get-tuple-element.37), channel_id=1, source_target_pairs={{0,4},{4,0},{1,5},{5,1},{2,6},{6,2},{3,7},{7,3},{8,12},{12,8},{9,1... | collective-permute-start | bytes 786440 | tf_op jit(solution)/shard_map/ppermute | solution.py:451
  102.6 5.2 %collective-permute-start.6 = (f32[528,128]{1,0:T(8,128)S(1)}, f32[528,128]{1,0:T(8,128)S(1)}, u32[]{:S(2)}, u32[]{:S(2)}) collective-permute-start(f32[528,128]{1,0:T(8,128)S(1)} %bitcast.16), channel_id=1, source_target_pairs={{0,4},{4,0},{1,5},{5,1},{2,6},{6,2},{3,7},{7,3},{8,12},{12,8},{9,1... | collective-permute-start | bytes 811016 | tf_op jit(solution)/shard_map/ppermute | solution.py:451

commit v11 on v10

--- a/solution.py
+++ b/solution.py
@@ -95,7 +95,7 @@
         copy.wait()
 
 
-def norm_kernel(left_dims, right_dims, guess, start, masks, one, two, three):
+def norm_kernel(left_dims, right_dims, guess, masks, one, two, three, start):
     wf, base, first_row = place_here()
     sums = jnp.zeros((1, 1), f32)
     for i in range(OWN):
@@ -158,11 +158,12 @@
 
 
 def first_kernel(
-    shift, mask, left, right, start, own, one, two, three, keep, give, vector, pieces,
+    shift, mask, left, right, sent_one, sent_three, one, two, three,
+    keep, give, vector, pieces,
     vec_half, back, sums,
 ):
     wf = lax.axis_index("wf")
-    squares = (own[0:1, 0:1] + one[SIDE : SIDE + 1, 0:1]) + (
+    squares = (sent_one[SIDE : SIDE + 1, 0:1] + one[SIDE : SIDE + 1, 0:1]) + (
         two[0:1, 0:1] + three[SIDE : SIDE + 1, 0:1]
     )
     scale = 1.0 / jnp.sqrt(squares / ENTRIES + EPS)
@@ -175,13 +176,13 @@
         vec_half[position] = value.astype(bf16)
 
     odd = wf & 1
-    for i in range(OWN):
-        put(4 * odd + i, start[i])
     for i in range(2):
         rows = slice(i * BLOCK, (i + 1) * BLOCK)
+        put(6 * odd + i, sent_three[rows])
+        put(2 + 2 * odd + i, sent_one[rows])
         put(4 - 2 * odd + i, one[rows])
         put(6 - 6 * odd + i, three[rows])
-    held = [own[EXTRA:], one[SIDE + EXTRA :], two[EXTRA:], three[SIDE + EXTRA :]]
+    held = [sent_one[SIDE + EXTRA :], one[SIDE + EXTRA :], two[EXTRA:], three[SIDE + EXTRA :]]
     for place in range(2):
         source = (lax.axis_index("c") + 2 * place) ^ wf
         value = held[0]
@@ -451,13 +452,13 @@
         return lax.ppermute(value, "c", [(0, 1), (1, 0)])
 
     tail = EXTRA + CHUNK
-    start, masks, one, own, three = call(
+    masks, sent_one, sent_two, sent_three = call(
         norm_kernel, "norm",
-        [own_blocks, pair, struct(SIDE + tail, BLOCK), struct(tail, BLOCK),
-         struct(SIDE + tail, BLOCK)],
-        [SMEM, SMEM, VMEM], (left_dims, right_dims, guess), limit=60,
-    )
-    three, one, two = partner(three, 3), partner(one, 1), partner(own, 2)
+        [pair, struct(SIDE + tail, BLOCK), struct(tail, BLOCK), struct(SIDE + tail, BLOCK)],
+        [SMEM, SMEM, VMEM], (left_dims, right_dims, guess),
+        scratch=[pltpu.VMEM((OWN, BLOCK, BLOCK), f32)], limit=60,
+    )
+    three, one, two = partner(sent_three, 3), partner(sent_one, 1), partner(sent_two, 2)
     held = struct(OWN, PAIRS, BLOCK, BLOCK, dtype=bf16)
     left, right = call(
         load_kernel, "load", [held, held], [HBM, HBM], (left_ops, right_ops),
@@ -477,7 +478,7 @@
 
     keep, give, vector, pieces = step(
         first_kernel, "first", [half, half, blocks, pair], operators,
-        (start, own, one, two, three),
+        (sent_one, sent_three, one, two, three),
     )
     packets, image_pieces = small(
         image_kernel, "image", [packet, pair], reduced(keep, give), masks, pieces

time: 131 us -> 131 us (level)
  no operation moved by 1% of the time
where the time goes in v11:
time: 131 us; the launch traced here: 130 us
  blocking collectives  88.8 us (68%)
  Pallas kernels  18.8 us (14%)
  starting transfers between devices  15.5 us (12%)
  waiting for transfers between devices  6.4 us (5%)
    all_to_all x7, blocking collectives, exchange(): lax.all_to_all(value, ALL_AXES, 0, 0, axis_index_groups=groups, tiled=True)  88.8 us
    pallas_call x12, Pallas kernels, call(): pl.pallas_call(kernel, name=name, in_specs=in_specs, out_specs=out_specs...  18.8 us
    ppermute x4, starting transfers between devices, swapped(): return lax.ppermute(value, 'c', [(0, 1), (1, 0)])  10.9 us
    ppermute x4, waiting for transfers between devices, swapped(): return lax.ppermute(value, 'c', [(0, 1), (1, 0)])  4.67 us
    ppermute x3, starting transfers between devices, partner(): return lax.ppermute(value, 'wf', [(i, i ^ distance) for i in range(4)])  4.59 us
  transfers between devices with their start and end apart: 7, of which 5 were waited for; matrix products, arithmetic and copies ran while one was open for 0% of the time, Pallas kernels for 2%

profile of v11, /device:TPU:1, one launch (start us, length us, event | category | flops | bytes accessed | tf_op | source)
XLA Modules:
  0.0 130.3 jit_solution(4450933467170883228)
XLA Ops:
  0.6 1.9 %norm.1 = (f32[2,32,128]{2,1,0:T(8,128)}, f32[296,128]{1,0:T(8,128)}, f32[40,128]{1,0:T(8,128)}, f32[296,128]{1,0:T(8,128)}) custom-call(s32[16]{0:T(128)} %left_dims.1, s32[16]{0:T(128)} %right_dims.1, f32[4,128,128]{2,1,0:T(8,128)} %guess.1), custom_call_target="tpu_custom_call" | custom-call | tf_op jit(solution)/shard_map/norm/pallas_call | solution.py:390
  2.5 2.0 %collective-permute-start = (f32[296,128]{1,0:T(8,128)}, f32[296,128]{1,0:T(8,128)S(1)}, u32[]{:S(2)}, u32[]{:S(2)}) collective-permute-start(f32[296,128]{1,0:T(8,128)} %get-tuple-element.25.sent_one), channel_id=1, source_target_pairs={{0,1},{1,0},{2,3},{3,2},{4,5},{5,4},{6,7},{7,6},{8,9},{9,8},{10,11... | collective-permute-start | bytes 454664 | tf_op jit(solution)/shard_map/ppermute | solution.py:449
  4.6 1.8 %collective-permute-start.2 = (f32[296,128]{1,0:T(8,128)}, f32[296,128]{1,0:T(8,128)S(1)}, u32[]{:S(2)}, u32[]{:S(2)}) collective-permute-start(f32[296,128]{1,0:T(8,128)} %get-tuple-element.26.sent_three), channel_id=1, source_target_pairs={{0,3},{1,2},{2,1},{3,0},{4,7},{5,6},{6,5},{7,4},{8,11},{9,10},{10,... | collective-permute-start | bytes 454664 | tf_op jit(solution)/shard_map/ppermute | solution.py:449
  6.4 0.7 collective-permute-start.1
  7.1 2.2 %load.1 = (bf16[4,16,128,128]{3,2,1,0:T(8,128)(2,1)S(1)}, bf16[4,16,128,128]{3,2,1,0:T(8,128)(2,1)S(1)}) custom-call(bf16[16,4,128,128]{3,2,1,0:T(8,128)(2,1)} %left_hbm.1, bf16[16,4,128,128]{3,2,1,0:T(8,128)(2,1)} %right_hbm.1), custom_call_target="tpu_custom_call" | custom-call | tf_op jit(solution)/shard_map/load/pallas_call | solution.py:390
  9.4 1.7 %collective-permute-done.1.two = f32[40,128]{1,0:T(8,128)S(1)} collective-permute-done((f32[40,128]{1,0:T(8,128)}, f32[40,128]{1,0:T(8,128)S(1)}, u32[]{:S(2)}, u32[]{:S(2)}) %collective-permute-start.1) | collective-permute-done | bytes 20512 | tf_op jit(solution)/shard_map/ppermute | solution.py:449
  11.1 4.6 %first.1 = (f32[16,32,128]{2,1,0:T(8,128)S(1)}, f32[16,32,128]{2,1,0:T(8,128)S(1)}, f32[8,128,128]{2,1,0:T(8,128)S(1)}, f32[2,32,128]{2,1,0:T(8,128)S(1)}) custom-call(s32[16]{0:T(128)S(1)} %copy-done.4, s32[4,16]{1,0:T(4,128)S(1)} %bitcast.21, bf16[4,16,128,128]{3,2,1,0:T(8,128)(2,1)S(1)} %get-tuple-element.23.left, ...), custom_call_target="tpu_custom_call" | custom-call | tf_op jit(solution)/shard_map/first/pallas_call | solution.py:390
  15.8 2.2 %collective-permute-start.3 = (f32[16,32,128]{2,1,0:T(8,128)S(1)}, f32[16,32,128]{2,1,0:T(8,128)S(1)}, u32[]{:S(2)}, u32[]{:S(2)}) collective-permute-start(f32[16,32,128]{2,1,0:T(8,128)S(1)} %get-tuple-element.29), channel_id=1, source_target_pairs={{0,4},{4,0},{1,5},{5,1},{2,6},{6,2},{3,7},{7,3},{8,12},{12,8},{9,1... | collective-permute-start | bytes 786440 | tf_op jit(solution)/shard_map/ppermute | solution.py:452
  18.0 1.2 collective-permute-done.3.second
  19.2 16.5 %all_to_all.41.parts = bf16[16,32,128]{2,1,0:T(8,128)(2,1)S(1)} all-to-all(bf16[16,32,128]{2,1,0:T(8,128)(2,1)S(1)} %join.2), channel_id=1, replica_groups={{0,8,16,24,32,40,48,56,64,72,80,88,96,104,112,120},{1,9,17,25,33,41,49,..., dimensions={0} | all-to-all | bytes 262144 | tf_op jit(solution)/shard_map/all_to_all | solution.py:436
  35.8 10.7 %all_to_all.42.parts = f32[8,32,128]{2,1,0:T(8,128)S(1)} all-to-all(f32[8,32,128]{2,1,0:T(8,128)S(1)} %spread.2), channel_id=1, replica_groups={{0,1,2,3,192,193,194,195},{4,5,6,7,196,197,198,199},{8,9,10,11,200,201,..., dimensions={0} | all-to-all | bytes 262144 | tf_op jit(solution)/shard_map/all_to_all | solution.py:436
  46.8 11.5 %all_to_all.43 = f32[528,1,128]{2,1,0:T(1,128)S(1)} all-to-all(f32[528,1,128]{2,1,0:T(1,128)S(1)} %bitcast.19), channel_id=1, replica_groups={{0,8,16,24,32,40,48,56,64,72,80,88,96,104,112,120},{1,9,17,25,33,41,49,..., dimensions={0} | all-to-all | bytes 540672 | tf_op jit(solution)/shard_map/all_to_all | solution.py:436
  58.2 4.2 %collective-permute-start.4 = (f32[528,128]{1,0:T(8,128)S(1)}, f32[528,128]{1,0:T(8,128)S(1)}, u32[]{:S(2)}, u32[]{:S(2)}) collective-permute-start(f32[528,128]{1,0:T(8,128)S(1)} %bitcast.13), channel_id=1, source_target_pairs={{0,4},{4,0},{1,5},{5,1},{2,6},{6,2},{3,7},{7,3},{8,12},{12,8},{9,1... | collective-permute-start | bytes 811016 | tf_op jit(solution)/shard_map/ppermute | solution.py:452
  62.4 1.2 collective-permute-done.4.other
  63.6 4.9 %second.1 = (f32[16,32,128]{2,1,0:T(8,128)S(1)}, f32[16,32,128]{2,1,0:T(8,128)S(1)}, f32[8,128,128]{2,1,0:T(8,128)S(1)}, f32[8,128,128]{2,1,0:T(8,128)S(1)}, f32[8,128]{1,0:T(8,128)S(1)}) custom-call(s32[16]{0:T(128)S(1)} %copy-done.4, s32[4,16]{1,0:T(4,128)S(1)} %bitcast.22, bf16[4,16,128,128]{3,2,1,0:T(8,128)(2,1)S(1)} %get-tuple-element.23.left, ...), custom_call_target="tpu_custom_call" | custom-call | tf_op jit(solution)/shard_map/second/pallas_call | solution.py:390
  69.0 1.2 collective-permute-done.5.second
  70.2 11.1 %all_to_all.44.parts = bf16[16,32,128]{2,1,0:T(8,128)(2,1)S(1)} all-to-all(bf16[16,32,128]{2,1,0:T(8,128)(2,1)S(1)} %join.3), channel_id=1, replica_groups={{0,8,16,24,32,40,48,56,64,72,80,88,96,104,112,120},{1,9,17,25,33,41,49,..., dimensions={0} | all-to-all | bytes 262144 | tf_op jit(solution)/shard_map/all_to_all | solution.py:436
  81.3 9.1 %all_to_all.45.parts = f32[8,32,128]{2,1,0:T(8,128)S(1)} all-to-all(f32[8,32,128]{2,1,0:T(8,128)S(1)} %spread.3), channel_id=1, replica_groups={{0,1,2,3,192,193,194,195},{4,5,6,7,196,197,198,199},{8,9,10,11,200,201,..., dimensions={0} | all-to-all | bytes 262144 | tf_op jit(solution)/shard_map/all_to_all | solution.py:436
  91.0 11.5 %all_to_all.46 = f32[528,1,128]{2,1,0:T(1,128)S(1)} all-to-all(f32[528,1,128]{2,1,0:T(1,128)S(1)} %bitcast.15), channel_id=1, replica_groups={{0,8,16,24,32,40,48,56,64,72,80,88,96,104,112,120},{1,9,17,25,33,41,49,..., dimensions={0} | all-to-all | bytes 540672 | tf_op jit(solution)/shard_map/all_to_all | solution.py:436
  102.5 4.0 %collective-permute-start.6 = (f32[528,128]{1,0:T(8,128)S(1)}, f32[528,128]{1,0:T(8,128)S(1)}, u32[]{:S(2)}, u32[]{:S(2)}) collective-permute-start(f32[528,128]{1,0:T(8,128)S(1)} %bitcast.16), channel_id=1, source_target_pairs={{0,4},{4,0},{1,5},{5,1},{2,6},{6,2},{3,7},{7,3},{8,12},{12,8},{9,1... | collective-permute-start | bytes 811016 | tf_op jit(solution)/shard_map/ppermute | solution.py:452
  106.6 1.2 collective-permute-done.6.swapped
  107.7 3.0 %third.1 = (f32[256,128]{1,0:T(8,128)S(1)}, f32[4,128,128]{2,1,0:T(8,128)S(1)}, f32[4,128,128]{2,1,0:T(8,128)S(1)}, f32[8,128]{1,0:T(8,128)S(1)}) custom-call(s32[16]{0:T(128)S(1)} %copy-done.4, s32[4,16]{1,0:T(4,128)S(1)} %bitcast.23, bf16[4,16,128,128]{3,2,1,0:T(8,128)(2,1)S(1)} %get-tuple-element.23.left, ...), custom_call_target="tpu_custom_call" | custom-call | tf_op jit(solution)/shard_map/third/pallas_call | solution.py:390
  110.8 18.3 %all_to_all.47 = f32[256,1,128]{2,1,0:T(1,128)S(1)} all-to-all(f32[256,1,128]{2,1,0:T(1,128)S(1)} %bitcast.20), channel_id=1, replica_groups=mesh['y'=4,'z'=8,'c'=2,'wf'=4] {'y','z','c','wf'}, dimensions={0} | all-to-all | bytes 262144 | tf_op jit(solution)/shard_map/all_to_all | solution.py:436
  129.1 1.1 last.1
  (19 shorter events, 1.4 us)
Async XLA Ops:
  2.5 8.6 %collective-permute-start = (f32[296,128]{1,0:T(8,128)}, f32[296,128]{1,0:T(8,128)S(1)}, u32[]{:S(2)}, u32[]{:S(2)}) collective-permute-start(f32[296,128]{1,0:T(8,128)} %get-tuple-element.25.sent_one), channel_id=1, source_target_pairs={{0,1},{1,0},{2,3},{3,2},{4,5},{5,4},{6,7},{7,6},{8,9},{9,8},{10,11... | collective-permute-start | bytes 454664 | tf_op jit(solution)/shard_map/ppermute | solution.py:449
  4.6 6.5 %collective-permute-start.2 = (f32[296,128]{1,0:T(8,128)}, f32[296,128]{1,0:T(8,128)S(1)}, u32[]{:S(2)}, u32[]{:S(2)}) collective-permute-start(f32[296,128]{1,0:T(8,128)} %get-tuple-element.26.sent_three), channel_id=1, source_target_pairs={{0,3},{1,2},{2,1},{3,0},{4,7},{5,6},{6,5},{7,4},{8,11},{9,10},{10,... | collective-permute-start | bytes 454664 | tf_op jit(solution)/shard_map/ppermute | solution.py:449
  6.4 4.7 %copy-start = (f32[296,128]{1,0:T(8,128)S(1)}, f32[296,128]{1,0:T(8,128)}, u32[]{:S(2)}) copy-start(f32[296,128]{1,0:T(8,128)} %get-tuple-element.25.sent_one) | copy-start | bytes 454660
  6.4 4.7 %copy-start.1 = (f32[296,128]{1,0:T(8,128)S(1)}, f32[296,128]{1,0:T(8,128)}, u32[]{:S(2)}) copy-start(f32[296,128]{1,0:T(8,128)} %get-tuple-element.26.sent_three) | copy-start | bytes 454660
  6.4 4.7 %copy-start.3 = (s32[16,4]{0,1:T(4,128)S(1)}, s32[16,4]{0,1:T(4,128)}, u32[]{:S(2)}) copy-start(s32[16,4]{0,1:T(4,128)} %param.11) | copy-start | bytes 772
  6.4 4.7 %copy-start.4 = (s32[16]{0:T(128)S(1)}, s32[16]{0:T(128)}, u32[]{:S(2)}) copy-start(s32[16]{0:T(128)} %shift.5) | copy-start | bytes 196
  6.4 4.7 %collective-permute-start.1 = (f32[40,128]{1,0:T(8,128)}, f32[40,128]{1,0:T(8,128)S(1)}, u32[]{:S(2)}, u32[]{:S(2)}) collective-permute-start(f32[40,128]{1,0:T(8,128)} %get-tuple-element.27), channel_id=1, source_target_pairs={{0,2},{1,3},{2,0},{3,1},{4,6},{5,7},{6,4},{7,5},{8,10},{9,11},{10,... | collective-permute-start | bytes 61448 | tf_op jit(solution)/shard_map/ppermute | solution.py:449
  11.1 35.3 %copy-start.2 = (f32[2,32,128]{2,1,0:T(8,128)S(1)}, f32[2,32,128]{2,1,0:T(8,128)}, u32[]{:S(2)}) copy-start(f32[2,32,128]{2,1,0:T(8,128)} %get-tuple-element.30.masks) | copy-start | bytes 98308
  15.8 3.4 %collective-permute-start.3 = (f32[16,32,128]{2,1,0:T(8,128)S(1)}, f32[16,32,128]{2,1,0:T(8,128)S(1)}, u32[]{:S(2)}, u32[]{:S(2)}) collective-permute-start(f32[16,32,128]{2,1,0:T(8,128)S(1)} %get-tuple-element.29), channel_id=1, source_target_pairs={{0,4},{4,0},{1,5},{5,1},{2,6},{6,2},{3,7},{7,3},{8,12},{12,8},{9,1... | collective-permute-start | bytes 786440 | tf_op jit(solution)/shard_map/ppermute | solution.py:452
  58.2 5.4 %collective-permute-start.4 = (f32[528,128]{1,0:T(8,128)S(1)}, f32[528,128]{1,0:T(8,128)S(1)}, u32[]{:S(2)}, u32[]{:S(2)}) collective-permute-start(f32[528,128]{1,0:T(8,128)S(1)} %bitcast.13), channel_id=1, source_target_pairs={{0,4},{4,0},{1,5},{5,1},{2,6},{6,2},{3,7},{7,3},{8,12},{12,8},{9,1... | collective-permute-start | bytes 811016 | tf_op jit(solution)/shard_map/ppermute | solution.py:452
  68.6 1.6 %collective-permute-start.5 = (f32[16,32,128]{2,1,0:T(8,128)S(1)}, f32[16,32,128]{2,1,0:T(8,128)S(1)}, u32[]{:S(2)}, u32[]{:S(2)}) collective-permute-start(f32[16,32,128]{2,1,0:T(8,128)S(1)} %get-tuple-element.35), channel_id=1, source_target_pairs={{0,4},{4,0},{1,5},{5,1},{2,6},{6,2},{3,7},{7,3},{8,12},{12,8},{9,1... | collective-permute-start | bytes 786440 | tf_op jit(solution)/shard_map/ppermute | solution.py:452
  102.5 5.2 %collective-permute-start.6 = (f32[528,128]{1,0:T(8,128)S(1)}, f32[528,128]{1,0:T(8,128)S(1)}, u32[]{:S(2)}, u32[]{:S(2)}) collective-permute-start(f32[528,128]{1,0:T(8,128)S(1)} %bitcast.16), channel_id=1, source_target_pairs={{0,4},{4,0},{1,5},{5,1},{2,6},{6,2},{3,7},{7,3},{8,12},{12,8},{9,1... | collective-permute-start | bytes 811016 | tf_op jit(solution)/shard_map/ppermute | solution.py:452

commit v12 on v11

--- a/solution.py
+++ b/solution.py
@@ -44,13 +44,13 @@
 
 
 def line_order(core):
-    return [(half, z) for half in range(2) for z in range(8)]
+    return [(half, (1 + 2 * core) * z % 8) for half in range(2) for z in range(8)]
 
 
 def place_here():
     y, z, core = (lax.axis_index(axis) for axis in OP_AXES)
     half = (y ^ (y // 2)) & 1
-    chunk = half * 8 + z
+    chunk = half * 8 + ((z + 2 * z * core) & 7)
     first_row = pl.multiple_of(chunk * ROWS, ROWS)
     return lax.axis_index("wf"), HALF * core, first_row
 

time: 131 us -> 131 us (level)
  no operation moved by 1% of the time
where the time goes in v12:
time: 131 us; the launch traced here: 130 us
  blocking collectives  88.4 us (67%)
  Pallas kernels  18.8 us (14%)
  starting transfers between devices  15.9 us (12%)
  waiting for transfers between devices  6.4 us (5%)
    all_to_all x7, blocking collectives, exchange(): lax.all_to_all(value, ALL_AXES, 0, 0, axis_index_groups=groups, tiled=True)  88.4 us
    pallas_call x12, Pallas kernels, call(): pl.pallas_call(kernel, name=name, in_specs=in_specs, out_specs=out_specs...  18.8 us
    ppermute x4, starting transfers between devices, swapped(): return lax.ppermute(value, 'c', [(0, 1), (1, 0)])  11.3 us
    ppermute x4, waiting for transfers between devices, swapped(): return lax.ppermute(value, 'c', [(0, 1), (1, 0)])  4.67 us
    ppermute x3, starting transfers between devices, partner(): return lax.ppermute(value, 'wf', [(i, i ^ distance) for i in range(4)])  4.59 us
  transfers between devices with their start and end apart: 7, of which 5 were waited for; matrix products, arithmetic and copies ran while one was open for 0% of the time, Pallas kernels for 2%

profile of v12, /device:TPU:1, one launch (start us, length us, event | category | flops | bytes accessed | tf_op | source)
XLA Modules:
  0.0 130.4 jit_solution(11768757362030382930)
XLA Ops:
  0.6 1.9 %norm.1 = (f32[2,32,128]{2,1,0:T(8,128)}, f32[296,128]{1,0:T(8,128)}, f32[40,128]{1,0:T(8,128)}, f32[296,128]{1,0:T(8,128)}) custom-call(s32[16]{0:T(128)} %left_dims.1, s32[16]{0:T(128)} %right_dims.1, f32[4,128,128]{2,1,0:T(8,128)} %guess.1), custom_call_target="tpu_custom_call" | custom-call | tf_op jit(solution)/shard_map/norm/pallas_call | solution.py:390
  2.5 2.0 %collective-permute-start = (f32[296,128]{1,0:T(8,128)}, f32[296,128]{1,0:T(8,128)S(1)}, u32[]{:S(2)}, u32[]{:S(2)}) collective-permute-start(f32[296,128]{1,0:T(8,128)} %get-tuple-element.25.sent_one), channel_id=1, source_target_pairs={{0,1},{1,0},{2,3},{3,2},{4,5},{5,4},{6,7},{7,6},{8,9},{9,8},{10,11... | collective-permute-start | bytes 454664 | tf_op jit(solution)/shard_map/ppermute | solution.py:449
  4.6 1.8 %collective-permute-start.2 = (f32[296,128]{1,0:T(8,128)}, f32[296,128]{1,0:T(8,128)S(1)}, u32[]{:S(2)}, u32[]{:S(2)}) collective-permute-start(f32[296,128]{1,0:T(8,128)} %get-tuple-element.26.sent_three), channel_id=1, source_target_pairs={{0,3},{1,2},{2,1},{3,0},{4,7},{5,6},{6,5},{7,4},{8,11},{9,10},{10,... | collective-permute-start | bytes 454664 | tf_op jit(solution)/shard_map/ppermute | solution.py:449
  6.4 0.7 collective-permute-start.1
  7.1 2.2 %load.1 = (bf16[4,16,128,128]{3,2,1,0:T(8,128)(2,1)S(1)}, bf16[4,16,128,128]{3,2,1,0:T(8,128)(2,1)S(1)}) custom-call(bf16[16,4,128,128]{3,2,1,0:T(8,128)(2,1)} %left_hbm.1, bf16[16,4,128,128]{3,2,1,0:T(8,128)(2,1)} %right_hbm.1), custom_call_target="tpu_custom_call" | custom-call | tf_op jit(solution)/shard_map/load/pallas_call | solution.py:390
  9.4 1.7 %collective-permute-done.1.two = f32[40,128]{1,0:T(8,128)S(1)} collective-permute-done((f32[40,128]{1,0:T(8,128)}, f32[40,128]{1,0:T(8,128)S(1)}, u32[]{:S(2)}, u32[]{:S(2)}) %collective-permute-start.1) | collective-permute-done | bytes 20512 | tf_op jit(solution)/shard_map/ppermute | solution.py:449
  11.1 4.6 %first.1 = (f32[16,32,128]{2,1,0:T(8,128)S(1)}, f32[16,32,128]{2,1,0:T(8,128)S(1)}, f32[8,128,128]{2,1,0:T(8,128)S(1)}, f32[2,32,128]{2,1,0:T(8,128)S(1)}) custom-call(s32[16]{0:T(128)S(1)} %copy-done.4, s32[4,16]{1,0:T(4,128)S(1)} %bitcast.21, bf16[4,16,128,128]{3,2,1,0:T(8,128)(2,1)S(1)} %get-tuple-element.23.left, ...), custom_call_target="tpu_custom_call" | custom-call | tf_op jit(solution)/shard_map/first/pallas_call | solution.py:390
  15.8 2.2 %collective-permute-start.3 = (f32[16,32,128]{2,1,0:T(8,128)S(1)}, f32[16,32,128]{2,1,0:T(8,128)S(1)}, u32[]{:S(2)}, u32[]{:S(2)}) collective-permute-start(f32[16,32,128]{2,1,0:T(8,128)S(1)} %get-tuple-element.29), channel_id=1, source_target_pairs={{0,4},{4,0},{1,5},{5,1},{2,6},{6,2},{3,7},{7,3},{8,12},{12,8},{9,1... | collective-permute-start | bytes 786440 | tf_op jit(solution)/shard_map/ppermute | solution.py:452
  18.0 1.2 collective-permute-done.3.second
  19.2 16.6 %all_to_all.41.parts = bf16[16,32,128]{2,1,0:T(8,128)(2,1)S(1)} all-to-all(bf16[16,32,128]{2,1,0:T(8,128)(2,1)S(1)} %join.2), channel_id=1, replica_groups={{0,8,16,24,32,40,48,56,64,72,80,88,96,104,112,120},{1,9,17,25,33,41,49,..., dimensions={0} | all-to-all | bytes 262144 | tf_op jit(solution)/shard_map/all_to_all | solution.py:436
  35.8 10.7 %all_to_all.42.parts = f32[8,32,128]{2,1,0:T(8,128)S(1)} all-to-all(f32[8,32,128]{2,1,0:T(8,128)S(1)} %spread.2), channel_id=1, replica_groups={{0,1,2,3,192,193,194,195},{4,5,6,7,196,197,198,199},{8,9,10,11,200,201,..., dimensions={0} | all-to-all | bytes 262144 | tf_op jit(solution)/shard_map/all_to_all | solution.py:436
  46.9 11.2 %all_to_all.43 = f32[528,1,128]{2,1,0:T(1,128)S(1)} all-to-all(f32[528,1,128]{2,1,0:T(1,128)S(1)} %bitcast.19), channel_id=1, replica_groups={{0,8,16,24,32,40,48,56,64,72,80,88,96,104,112,120},{1,9,17,25,33,41,49,..., dimensions={0} | all-to-all | bytes 540672 | tf_op jit(solution)/shard_map/all_to_all | solution.py:436
  58.0 4.4 %collective-permute-start.4 = (f32[528,128]{1,0:T(8,128)S(1)}, f32[528,128]{1,0:T(8,128)S(1)}, u32[]{:S(2)}, u32[]{:S(2)}) collective-permute-start(f32[528,128]{1,0:T(8,128)S(1)} %bitcast.13), channel_id=1, source_target_pairs={{0,4},{4,0},{1,5},{5,1},{2,6},{6,2},{3,7},{7,3},{8,12},{12,8},{9,1... | collective-permute-start | bytes 811016 | tf_op jit(solution)/shard_map/ppermute | solution.py:452
  62.5 1.2 collective-permute-done.4.other
  63.6 5.0 %second.1 = (f32[16,32,128]{2,1,0:T(8,128)S(1)}, f32[16,32,128]{2,1,0:T(8,128)S(1)}, f32[8,128,128]{2,1,0:T(8,128)S(1)}, f32[8,128,128]{2,1,0:T(8,128)S(1)}, f32[8,128]{1,0:T(8,128)S(1)}) custom-call(s32[16]{0:T(128)S(1)} %copy-done.4, s32[4,16]{1,0:T(4,128)S(1)} %bitcast.22, bf16[4,16,128,128]{3,2,1,0:T(8,128)(2,1)S(1)} %get-tuple-element.23.left, ...), custom_call_target="tpu_custom_call" | custom-call | tf_op jit(solution)/shard_map/second/pallas_call | solution.py:390
  69.0 1.2 collective-permute-done.5.second
  70.2 11.2 %all_to_all.44.parts = bf16[16,32,128]{2,1,0:T(8,128)(2,1)S(1)} all-to-all(bf16[16,32,128]{2,1,0:T(8,128)(2,1)S(1)} %join.3), channel_id=1, replica_groups={{0,8,16,24,32,40,48,56,64,72,80,88,96,104,112,120},{1,9,17,25,33,41,49,..., dimensions={0} | all-to-all | bytes 262144 | tf_op jit(solution)/shard_map/all_to_all | solution.py:436
  81.4 9.1 %all_to_all.45.parts = f32[8,32,128]{2,1,0:T(8,128)S(1)} all-to-all(f32[8,32,128]{2,1,0:T(8,128)S(1)} %spread.3), channel_id=1, replica_groups={{0,1,2,3,192,193,194,195},{4,5,6,7,196,197,198,199},{8,9,10,11,200,201,..., dimensions={0} | all-to-all | bytes 262144 | tf_op jit(solution)/shard_map/all_to_all | solution.py:436
  91.0 11.1 %all_to_all.46 = f32[528,1,128]{2,1,0:T(1,128)S(1)} all-to-all(f32[528,1,128]{2,1,0:T(1,128)S(1)} %bitcast.15), channel_id=1, replica_groups={{0,8,16,24,32,40,48,56,64,72,80,88,96,104,112,120},{1,9,17,25,33,41,49,..., dimensions={0} | all-to-all | bytes 540672 | tf_op jit(solution)/shard_map/all_to_all | solution.py:436
  102.2 4.2 %collective-permute-start.6 = (f32[528,128]{1,0:T(8,128)S(1)}, f32[528,128]{1,0:T(8,128)S(1)}, u32[]{:S(2)}, u32[]{:S(2)}) collective-permute-start(f32[528,128]{1,0:T(8,128)S(1)} %bitcast.16), channel_id=1, source_target_pairs={{0,4},{4,0},{1,5},{5,1},{2,6},{6,2},{3,7},{7,3},{8,12},{12,8},{9,1... | collective-permute-start | bytes 811016 | tf_op jit(solution)/shard_map/ppermute | solution.py:452
  106.4 1.2 collective-permute-done.6.swapped
  107.5 3.0 %third.1 = (f32[256,128]{1,0:T(8,128)S(1)}, f32[4,128,128]{2,1,0:T(8,128)S(1)}, f32[4,128,128]{2,1,0:T(8,128)S(1)}, f32[8,128]{1,0:T(8,128)S(1)}) custom-call(s32[16]{0:T(128)S(1)} %copy-done.4, s32[4,16]{1,0:T(4,128)S(1)} %bitcast.23, bf16[4,16,128,128]{3,2,1,0:T(8,128)(2,1)S(1)} %get-tuple-element.23.left, ...), custom_call_target="tpu_custom_call" | custom-call | tf_op jit(solution)/shard_map/third/pallas_call | solution.py:390
  110.6 18.5 %all_to_all.47 = f32[256,1,128]{2,1,0:T(1,128)S(1)} all-to-all(f32[256,1,128]{2,1,0:T(1,128)S(1)} %bitcast.20), channel_id=1, replica_groups=mesh['y'=4,'z'=8,'c'=2,'wf'=4] {'y','z','c','wf'}, dimensions={0} | all-to-all | bytes 262144 | tf_op jit(solution)/shard_map/all_to_all | solution.py:436
  129.1 1.1 last.1
  (19 shorter events, 1.4 us)
Async XLA Ops:
  2.5 8.6 %collective-permute-start = (f32[296,128]{1,0:T(8,128)}, f32[296,128]{1,0:T(8,128)S(1)}, u32[]{:S(2)}, u32[]{:S(2)}) collective-permute-start(f32[296,128]{1,0:T(8,128)} %get-tuple-element.25.sent_one), channel_id=1, source_target_pairs={{0,1},{1,0},{2,3},{3,2},{4,5},{5,4},{6,7},{7,6},{8,9},{9,8},{10,11... | collective-permute-start | bytes 454664 | tf_op jit(solution)/shard_map/ppermute | solution.py:449
  4.6 6.5 %collective-permute-start.2 = (f32[296,128]{1,0:T(8,128)}, f32[296,128]{1,0:T(8,128)S(1)}, u32[]{:S(2)}, u32[]{:S(2)}) collective-permute-start(f32[296,128]{1,0:T(8,128)} %get-tuple-element.26.sent_three), channel_id=1, source_target_pairs={{0,3},{1,2},{2,1},{3,0},{4,7},{5,6},{6,5},{7,4},{8,11},{9,10},{10,... | collective-permute-start | bytes 454664 | tf_op jit(solution)/shard_map/ppermute | solution.py:449
  6.4 4.7 %copy-start = (f32[296,128]{1,0:T(8,128)S(1)}, f32[296,128]{1,0:T(8,128)}, u32[]{:S(2)}) copy-start(f32[296,128]{1,0:T(8,128)} %get-tuple-element.25.sent_one) | copy-start | bytes 454660
  6.4 4.7 %copy-start.1 = (f32[296,128]{1,0:T(8,128)S(1)}, f32[296,128]{1,0:T(8,128)}, u32[]{:S(2)}) copy-start(f32[296,128]{1,0:T(8,128)} %get-tuple-element.26.sent_three) | copy-start | bytes 454660
  6.4 4.7 %copy-start.3 = (s32[16,4]{0,1:T(4,128)S(1)}, s32[16,4]{0,1:T(4,128)}, u32[]{:S(2)}) copy-start(s32[16,4]{0,1:T(4,128)} %param.11) | copy-start | bytes 772
  6.4 4.7 %copy-start.4 = (s32[16]{0:T(128)S(1)}, s32[16]{0:T(128)}, u32[]{:S(2)}) copy-start(s32[16]{0:T(128)} %shift.5) | copy-start | bytes 196
  6.4 4.7 %collective-permute-start.1 = (f32[40,128]{1,0:T(8,128)}, f32[40,128]{1,0:T(8,128)S(1)}, u32[]{:S(2)}, u32[]{:S(2)}) collective-permute-start(f32[40,128]{1,0:T(8,128)} %get-tuple-element.27), channel_id=1, source_target_pairs={{0,2},{1,3},{2,0},{3,1},{4,6},{5,7},{6,4},{7,5},{8,10},{9,11},{10,... | collective-permute-start | bytes 61448 | tf_op jit(solution)/shard_map/ppermute | solution.py:449
  11.1 35.4 %copy-start.2 = (f32[2,32,128]{2,1,0:T(8,128)S(1)}, f32[2,32,128]{2,1,0:T(8,128)}, u32[]{:S(2)}) copy-start(f32[2,32,128]{2,1,0:T(8,128)} %get-tuple-element.30.masks) | copy-start | bytes 98308
  15.8 3.4 %collective-permute-start.3 = (f32[16,32,128]{2,1,0:T(8,128)S(1)}, f32[16,32,128]{2,1,0:T(8,128)S(1)}, u32[]{:S(2)}, u32[]{:S(2)}) collective-permute-start(f32[16,32,128]{2,1,0:T(8,128)S(1)} %get-tuple-element.29), channel_id=1, source_target_pairs={{0,4},{4,0},{1,5},{5,1},{2,6},{6,2},{3,7},{7,3},{8,12},{12,8},{9,1... | collective-permute-start | bytes 786440 | tf_op jit(solution)/shard_map/ppermute | solution.py:452
  58.0 5.6 %collective-permute-start.4 = (f32[528,128]{1,0:T(8,128)S(1)}, f32[528,128]{1,0:T(8,128)S(1)}, u32[]{:S(2)}, u32[]{:S(2)}) collective-permute-start(f32[528,128]{1,0:T(8,128)S(1)} %bitcast.13), channel_id=1, source_target_pairs={{0,4},{4,0},{1,5},{5,1},{2,6},{6,2},{3,7},{7,3},{8,12},{12,8},{9,1... | collective-permute-start | bytes 811016 | tf_op jit(solution)/shard_map/ppermute | solution.py:452
  68.6 1.6 %collective-permute-start.5 = (f32[16,32,128]{2,1,0:T(8,128)S(1)}, f32[16,32,128]{2,1,0:T(8,128)S(1)}, u32[]{:S(2)}, u32[]{:S(2)}) collective-permute-start(f32[16,32,128]{2,1,0:T(8,128)S(1)} %get-tuple-element.35), channel_id=1, source_target_pairs={{0,4},{4,0},{1,5},{5,1},{2,6},{6,2},{3,7},{7,3},{8,12},{12,8},{9,1... | collective-permute-start | bytes 786440 | tf_op jit(solution)/shard_map/ppermute | solution.py:452
  102.2 5.4 %collective-permute-start.6 = (f32[528,128]{1,0:T(8,128)S(1)}, f32[528,128]{1,0:T(8,128)S(1)}, u32[]{:S(2)}, u32[]{:S(2)}) collective-permute-start(f32[528,128]{1,0:T(8,128)S(1)} %bitcast.16), channel_id=1, source_target_pairs={{0,4},{4,0},{1,5},{5,1},{2,6},{6,2},{3,7},{7,3},{8,12},{12,8},{9,1... | collective-permute-start | bytes 811016 | tf_op jit(solution)/shard_map/ppermute | solution.py:452
